TPU v7x, 128 devices: a whole 4x4x4 slice. The times are simulated.
128 devices in a mesh: rows: 32 (over z, y, core), cent: 4 (over x).
Axes of the slice: x: 4, y: 4, z: 4, core: 2. Of those that a mesh axis runs over, the one named last changes fastest.
Arguments:
- embeddings: float32 [262144, 256], P(('rows', 'cent')), may hold values from -6 to 6
- centroids: float32 [8192, 256], P('cent'), may hold values from -6 to 6
- owners: int32 [2048], P(('rows', 'cent')), may hold values from 0 to 31, as said below
- live_blocks: int32 [128], P(('rows', 'cent')), may hold values from 9 to 16
Outputs:
- moved: bfloat16 [524288, 256], P(('rows', 'cent'))
- moved_score: bfloat16 [524288], P(('rows', 'cent'))
- balance: float32 [8192], replicated
Inputs may be any that keep to these rules, and one draw needn't show every extreme that they name: `owners`: within one device the blocks name each owner at most 1 times; in each cent group one owner is named exactly 1 times by the live blocks of every device.
All inputs are finite; a program needn't handle non-finite values.
Results may differ from a plain program's by a relative error of at most 0.0041.
Values may be sent and summed in bfloat16 or wider, within the bound.
No kernel may reach another device: no remote copies, remote signals or barrier semaphores. Data moves between devices by JAX's collectives and lax.ppermute only.
A program may use at most 64 MiB of HBM per device.

v0:
```python
import math

import jax
import jax.numpy as jnp
from jax import lax
from jax.sharding import PartitionSpec as P

BLOCK_ROWS = 128
ITERS = 1


SCALE = 50.0
EPSILON = 1e-06
HIGHEST = lax.Precision.HIGHEST


def unit_of(values):
    squares = jnp.sum(values * values, axis=-1, keepdims=True)
    return (values * lax.rsqrt(squares + EPSILON)).astype(jnp.bfloat16)


def logits_of(rows_tile, centres):
    product = lax.dot_general(
        rows_tile, centres, (((1,), (1,)), ((), ())), preferred_element_type=jnp.float32
    )
    return product * SCALE


def tiles_of(rows_here, col_count):
    row_count = rows_here.shape[0]
    tile_rows = math.gcd(row_count, max(8, 2**21 // col_count))
    return rows_here.reshape(row_count // tile_rows, tile_rows, rows_here.shape[1])


def joined_sweep(row_tiles, centres, scaling, with_score):

    def one_tile(running, rows_tile):
        logits = logits_of(rows_tile, centres)
        weights = jnp.exp(logits)
        if scaling is None:
            inverse = jnp.ones((rows_tile.shape[0],), jnp.float32)
        else:
            inverse = 1.0 / jnp.dot(weights, scaling, precision=HIGHEST)
        running = running + jnp.dot(inverse, weights, precision=HIGHEST)
        if with_score:
            expected = inverse * jnp.dot(weights * logits, scaling, precision=HIGHEST)
        else:
            expected = inverse
        return (running, expected)

    initial = jnp.zeros((centres.shape[0],), jnp.float32)
    column, per_row = lax.scan(one_tile, initial, row_tiles)
    return (column, per_row.reshape(-1))


def local(embeddings, centroids, owners, live_blocks):
    unit_rows = unit_of(embeddings)
    unit_own = unit_of(centroids)
    own_rows = unit_rows.shape[0]
    centres = lax.all_gather(unit_own, "cent", axis=0, tiled=True)
    row_tiles = tiles_of(unit_rows, centres.shape[0])
    share_ratio = float(own_rows * lax.axis_size(("rows", "cent"))) / centres.shape[0]
    column, expected = joined_sweep(row_tiles, centres, None, False)
    scaling = None
    for rounds in range(ITERS + 1):
        column_total = lax.psum(column, ("rows", "cent"))
        if rounds < ITERS:
            scaling = share_ratio / column_total
            column, expected = joined_sweep(row_tiles, centres, scaling, rounds == ITERS - 1)
    balance = scaling * column_total / share_ratio
    score_low = expected.astype(jnp.bfloat16)
    blocks = owners.shape[0]
    peer_count = lax.axis_size("rows")
    slot_count = -(-blocks // peer_count)
    positions = jnp.arange(blocks, dtype=jnp.int32)
    live_mask = positions < live_blocks[0]
    earlier = (
        (owners[None, :] == owners[:, None])
        & live_mask[None, :]
        & (positions[None, :] < positions[:, None])
    )
    target = owners * slot_count + jnp.sum(earlier.astype(jnp.int32), axis=1)
    slot_ids = jnp.arange(peer_count * slot_count, dtype=jnp.int32)
    select = ((target[None, :] == slot_ids[:, None]) & live_mask[None, :]).astype(jnp.bfloat16)
    row_blocks = unit_rows.reshape(blocks, BLOCK_ROWS, unit_rows.shape[1])
    outgoing = jnp.einsum(
        "sb,brd->srd", select, row_blocks, preferred_element_type=jnp.float32
    ).astype(jnp.bfloat16)
    outgoing_score = jnp.einsum(
        "sb,br->sr",
        select,
        score_low.reshape(blocks, BLOCK_ROWS),
        preferred_element_type=jnp.float32,
    ).astype(jnp.bfloat16)
    arrived, arrived_score = (
        lax.all_to_all(outgoing, "rows", split_axis=0, concat_axis=0, tiled=True),
        lax.all_to_all(outgoing_score, "rows", split_axis=0, concat_axis=0, tiled=True),
    )
    moved = arrived.reshape(peer_count * slot_count * BLOCK_ROWS, unit_rows.shape[1])
    moved_score = arrived_score.reshape(peer_count * slot_count * BLOCK_ROWS)
    return (moved, moved_score, balance)


def solution(mesh):
    placed = (P(("rows", "cent"), None), P("cent", None), P(("rows", "cent")), P(("rows", "cent")))
    return jax.shard_map(
        local,
        mesh=mesh,
        in_specs=placed,
        out_specs=(P(("rows", "cent"), None), P(("rows", "cent")), P()),
        check_vma=False,
    )
```

profile of v0, /device:TPU:1, one launch (start us, length us, event | category | flops | bytes accessed | tf_op | source)
XLA Modules:
  0.0 448.0 jit_solution(11984325566736732387)
XLA Ops:
  20.2 9.6 %all-to-all-start = ((bf16[32,128,256]{2,1,0:T(8,128)(2,1)}), bf16[32,128,256]{2,1,0:T(8,128)(2,1)S(1)}, u32[]{:S(2)}, u32[]{:S(2)}) async-start(bf16[32,128,256]{2,1,0:T(8,128)(2,1)} %copy.17), calls=%async_computation | async-start | bytes 4194304 | tf_op jit(solution)/shard_map/all_to_all | solution.py:96
  29.8 27.8 %all-to-all-done = bf16[32,128,256]{2,1,0:T(8,128)(2,1)S(1)} async-done(((bf16[32,128,256]{2,1,0:T(8,128)(2,1)}), bf16[32,128,256]{2,1,0:T(8,128)(2,1)S(1)}, u32[]{:S(2)}, u32[]{:S(2)}) %all-to-all-start) | async-done | bytes 2097184 | tf_op jit(solution)/shard_map/all_to_all | solution.py:96
  57.7 6.2 %all-gather.2.cloned.1.call-done = bf16[8192,256]{1,0:T(8,128)(2,1)} async-done(((bf16[2048,256]{1,0:T(8,128)(2,1)}), bf16[8192,256]{1,0:T(8,128)(2,1)}) %all-gather.2.cloned.1.call-update) | async-done | bytes 4194320 | tf_op jit(solution)/shard_map/all_gather | solution.py:60
  63.8 61.3 %while.24 = (s32[]{:T(128)}, f32[8192]{0:T(1024)S(1)}, bf16[8,256,256]{2,1,0:T(8,128)(2,1)S(1)}, bf16[8192,256]{1,0:T(8,128)(2,1)}, s32[]{:T(128)}, /*index=5*/s32[]{:T(128)}) while((s32[]{:T(128)}, f32[8192]{0:T(1024)S(1)}, bf16[8,256,256]{2,1,0:T(8,128)(2,1)S(1)}, bf16[8192,256]{1,0:T(8,128)(2,1)}, s32[]{:T(128)}, ...), condition=%wide.region_4.5_spmd.clone, body=%wide.region_3.4_spmd.clone.sunk | while | flops 1101021184 | bytes 21233744 | solution.py:52
  125.1 65.1 %psum.14 = f32[8192]{0:T(1024)S(1)} all-reduce(f32[8192]{0:T(1024)S(1)} %get-tuple-element.58), channel_id=1, replica_groups=mesh['rows'=32,'cent'=4] {'rows','cent'}, use_global_device_ids=true, to_apply=%region_5.6 | all-reduce | flops 8192 | bytes 65536 | tf_op jit(solution)/shard_map/psum | solution.py:66
  190.3 177.0 %while.25 = (s32[]{:T(128)}, f32[8192]{0:T(1024)S(1)}, bf16[8,256]{1,0:T(8,128)(2,1)S(1)}, bf16[8,256,256]{2,1,0:T(8,128)(2,1)S(1)}, bf16[8192,256]{1,0:T(8,128)...) while((s32[]{:T(128)}, f32[8192]{0:T(1024)S(1)}, bf16[8,256]{1,0:T(8,128)(2,1)S(1)}, ...), condition=%wide.region_7.8_spmd.clone, body=%wide.region_6.7_spmd.clone.sunk | while | flops 1153450496 | bytes 38085732 | solution.py:52
  194.0 7.1 %fusion.64 = f32[1,256]{1,0:T(1,128)S(1)} fusion(f32[8192,1]{0,1:T(1,128)S(1)} %bitcast.65, f32[256,8192]{1,0:T(8,128)S(1)} %convolution_multiply_fusion.3), kind=kOutput, calls=%fused_computation.15.clone.1 | convolution fusion | flops 27262976 | bytes 8422400 | tf_op jit(solution)/shard_map/while/body/eval_jaxpr/dot_general | solution.py:46
  201.1 6.9 %fusion.65 = f32[1,256]{1,0:T(1,128)S(1)} fusion(f32[8192,1]{0,1:T(1,128)S(1)} %bitcast.66, f32[256,8192]{1,0:T(8,128)S(1)} %convolution_multiply_fusion.3), kind=kOutput, calls=%fused_computation.12.clone.1 | convolution fusion | flops 25165824 | bytes 8422400 | tf_op jit(solution)/shard_map/while/body/eval_jaxpr/dot_general | solution.py:43
  216.1 7.1 %fusion.64 = f32[1,256]{1,0:T(1,128)S(1)} fusion(f32[8192,1]{0,1:T(1,128)S(1)} %bitcast.65, f32[256,8192]{1,0:T(8,128)S(1)} %convolution_multiply_fusion.3), kind=kOutput, calls=%fused_computation.15.clone.1 | convolution fusion | flops 27262976 | bytes 8422400 | tf_op jit(solution)/shard_map/while/body/eval_jaxpr/dot_general | solution.py:46
  223.2 6.9 %fusion.65 = f32[1,256]{1,0:T(1,128)S(1)} fusion(f32[8192,1]{0,1:T(1,128)S(1)} %bitcast.66, f32[256,8192]{1,0:T(8,128)S(1)} %convolution_multiply_fusion.3), kind=kOutput, calls=%fused_computation.12.clone.1 | convolution fusion | flops 25165824 | bytes 8422400 | tf_op jit(solution)/shard_map/while/body/eval_jaxpr/dot_general | solution.py:43
  238.2 7.1 %fusion.64 = f32[1,256]{1,0:T(1,128)S(1)} fusion(f32[8192,1]{0,1:T(1,128)S(1)} %bitcast.65, f32[256,8192]{1,0:T(8,128)S(1)} %convolution_multiply_fusion.3), kind=kOutput, calls=%fused_computation.15.clone.1 | convolution fusion | flops 27262976 | bytes 8422400 | tf_op jit(solution)/shard_map/while/body/eval_jaxpr/dot_general | solution.py:46
  245.3 6.9 %fusion.65 = f32[1,256]{1,0:T(1,128)S(1)} fusion(f32[8192,1]{0,1:T(1,128)S(1)} %bitcast.66, f32[256,8192]{1,0:T(8,128)S(1)} %convolution_multiply_fusion.3), kind=kOutput, calls=%fused_computation.12.clone.1 | convolution fusion | flops 25165824 | bytes 8422400 | tf_op jit(solution)/shard_map/while/body/eval_jaxpr/dot_general | solution.py:43
  260.3 7.1 %fusion.64 = f32[1,256]{1,0:T(1,128)S(1)} fusion(f32[8192,1]{0,1:T(1,128)S(1)} %bitcast.65, f32[256,8192]{1,0:T(8,128)S(1)} %convolution_multiply_fusion.3), kind=kOutput, calls=%fused_computation.15.clone.1 | convolution fusion | flops 27262976 | bytes 8422400 | tf_op jit(solution)/shard_map/while/body/eval_jaxpr/dot_general | solution.py:46
  267.4 6.9 %fusion.65 = f32[1,256]{1,0:T(1,128)S(1)} fusion(f32[8192,1]{0,1:T(1,128)S(1)} %bitcast.66, f32[256,8192]{1,0:T(8,128)S(1)} %convolution_multiply_fusion.3), kind=kOutput, calls=%fused_computation.12.clone.1 | convolution fusion | flops 25165824 | bytes 8422400 | tf_op jit(solution)/shard_map/while/body/eval_jaxpr/dot_general | solution.py:43
  282.4 7.1 %fusion.64 = f32[1,256]{1,0:T(1,128)S(1)} fusion(f32[8192,1]{0,1:T(1,128)S(1)} %bitcast.65, f32[256,8192]{1,0:T(8,128)S(1)} %convolution_multiply_fusion.3), kind=kOutput, calls=%fused_computation.15.clone.1 | convolution fusion | flops 27262976 | bytes 8422400 | tf_op jit(solution)/shard_map/while/body/eval_jaxpr/dot_general | solution.py:46
  289.5 6.9 %fusion.65 = f32[1,256]{1,0:T(1,128)S(1)} fusion(f32[8192,1]{0,1:T(1,128)S(1)} %bitcast.66, f32[256,8192]{1,0:T(8,128)S(1)} %convolution_multiply_fusion.3), kind=kOutput, calls=%fused_computation.12.clone.1 | convolution fusion | flops 25165824 | bytes 8422400 | tf_op jit(solution)/shard_map/while/body/eval_jaxpr/dot_general | solution.py:43
  304.5 7.1 %fusion.64 = f32[1,256]{1,0:T(1,128)S(1)} fusion(f32[8192,1]{0,1:T(1,128)S(1)} %bitcast.65, f32[256,8192]{1,0:T(8,128)S(1)} %convolution_multiply_fusion.3), kind=kOutput, calls=%fused_computation.15.clone.1 | convolution fusion | flops 27262976 | bytes 8422400 | tf_op jit(solution)/shard_map/while/body/eval_jaxpr/dot_general | solution.py:46
  311.6 6.9 %fusion.65 = f32[1,256]{1,0:T(1,128)S(1)} fusion(f32[8192,1]{0,1:T(1,128)S(1)} %bitcast.66, f32[256,8192]{1,0:T(8,128)S(1)} %convolution_multiply_fusion.3), kind=kOutput, calls=%fused_computation.12.clone.1 | convolution fusion | flops 25165824 | bytes 8422400 | tf_op jit(solution)/shard_map/while/body/eval_jaxpr/dot_general | solution.py:43
  326.5 7.1 %fusion.64 = f32[1,256]{1,0:T(1,128)S(1)} fusion(f32[8192,1]{0,1:T(1,128)S(1)} %bitcast.65, f32[256,8192]{1,0:T(8,128)S(1)} %convolution_multiply_fusion.3), kind=kOutput, calls=%fused_computation.15.clone.1 | convolution fusion | flops 27262976 | bytes 8422400 | tf_op jit(solution)/shard_map/while/body/eval_jaxpr/dot_general | solution.py:46
  333.7 6.9 %fusion.65 = f32[1,256]{1,0:T(1,128)S(1)} fusion(f32[8192,1]{0,1:T(1,128)S(1)} %bitcast.66, f32[256,8192]{1,0:T(8,128)S(1)} %convolution_multiply_fusion.3), kind=kOutput, calls=%fused_computation.12.clone.1 | convolution fusion | flops 25165824 | bytes 8422400 | tf_op jit(solution)/shard_map/while/body/eval_jaxpr/dot_general | solution.py:43
  348.6 7.1 %fusion.64 = f32[1,256]{1,0:T(1,128)S(1)} fusion(f32[8192,1]{0,1:T(1,128)S(1)} %bitcast.65, f32[256,8192]{1,0:T(8,128)S(1)} %convolution_multiply_fusion.3), kind=kOutput, calls=%fused_computation.15.clone.1 | convolution fusion | flops 27262976 | bytes 8422400 | tf_op jit(solution)/shard_map/while/body/eval_jaxpr/dot_general | solution.py:46
  355.8 6.9 %fusion.65 = f32[1,256]{1,0:T(1,128)S(1)} fusion(f32[8192,1]{0,1:T(1,128)S(1)} %bitcast.66, f32[256,8192]{1,0:T(8,128)S(1)} %convolution_multiply_fusion.3), kind=kOutput, calls=%fused_computation.12.clone.1 | convolution fusion | flops 25165824 | bytes 8422400 | tf_op jit(solution)/shard_map/while/body/eval_jaxpr/dot_general | solution.py:43
  368.1 5.3 %all-to-all-start.1 = ((bf16[32,1,128]{2,1,0:T(2,128)(2,1)}), bf16[32,1,128]{2,1,0:T(2,128)(2,1)S(1)}, u32[]{:S(2)}, u32[]{:S(2)}) async-start(bf16[32,1,128]{2,1,0:T(2,128)(2,1)} %copy.18), calls=%async_computation.1 | async-start | bytes 32768 | tf_op jit(solution)/shard_map/all_to_all | solution.py:97
  373.4 65.1 %psum.15 = f32[8192]{0:T(1024)S(1)} all-reduce(f32[8192]{0:T(1024)S(1)} %get-tuple-element.60), channel_id=1, replica_groups=mesh['rows'=32,'cent'=4] {'rows','cent'}, use_global_device_ids=true, to_apply=%region_8.9 | all-reduce | flops 8192 | bytes 65536 | tf_op jit(solution)/shard_map/psum | solution.py:66
  (90 shorter events, 141.0 us)
Async XLA Ops:
  7.2 9.3 %copy-start = (f32[2048,256]{1,0:T(8,128)S(1)}, f32[2048,256]{1,0:T(8,128)}, u32[]{:S(2)}) copy-start(f32[2048,256]{1,0:T(8,128)} %param.8) | copy-start | bytes 6291460
  7.2 56.7 %all-gather.2.cloned.1.call-start = ((), (), s32[]{:S(2)}) async-start(), calls=%async_computation.2 | async-start | bytes 5242880 | tf_op jit(solution)/shard_map/all_gather | solution.py:60
  20.2 37.5 %all-to-all-start = ((bf16[32,128,256]{2,1,0:T(8,128)(2,1)}), bf16[32,128,256]{2,1,0:T(8,128)(2,1)S(1)}, u32[]{:S(2)}, u32[]{:S(2)}) async-start(bf16[32,128,256]{2,1,0:T(8,128)(2,1)} %copy.17), calls=%async_computation | async-start | bytes 4194304 | tf_op jit(solution)/shard_map/all_to_all | solution.py:96
  368.1 71.1 %all-to-all-start.1 = ((bf16[32,1,128]{2,1,0:T(2,128)(2,1)}), bf16[32,1,128]{2,1,0:T(2,128)(2,1)S(1)}, u32[]{:S(2)}, u32[]{:S(2)}) async-start(bf16[32,1,128]{2,1,0:T(2,128)(2,1)} %copy.18), calls=%async_computation.1 | async-start | bytes 32768 | tf_op jit(solution)/shard_map/all_to_all | solution.py:97
Sparse Core Ops, SparseCore 0:
  12.4 51.4 all-gather.1
where the time goes:
time: 449 us; the launch traced here: 448 us
  matrix products  238 us (53%)
  blocking collectives  130 us (29%)
  waiting for transfers between devices  34 us (8%)
  starting transfers between devices  14.9 us (3%)
  between operations  14.8 us (3%)
  other arithmetic  10.3 us (2%)
  local copies, waits for them, and re-layouts  4.74 us (1%)
    psum x2, blocking collectives, local(): column_total = lax.psum(column, ('rows', 'cent'))  130 us
    dot_general x16, matrix products, one_tile(): running = running + jnp.dot(inverse, weights, precision=HIGHEST)  68 us
    dot_general x8, matrix products, one_tile(): expected = inverse * jnp.dot(weights * logits, scaling, precision=HIGHEST)  56.9 us
    dot_general x16, matrix products, logits_of(): lax.dot_general(rows_tile, centres, (((1,), (1,)), ((), ())), preferred_e...  56.6 us
    dot_general x8, matrix products, one_tile(): inverse = 1.0 / jnp.dot(weights, scaling, precision=HIGHEST)  55.4 us
    all_to_all x1, waiting for transfers between devices, local(): lax.all_to_all(outgoing, 'rows', split_axis=0, concat_axis=0, tiled=True)  27.8 us
    all_to_all x1, starting transfers between devices, local(): lax.all_to_all(outgoing, 'rows', split_axis=0, concat_axis=0, tiled=True)  9.6 us
  transfers between devices with their start and end apart: 3, of which 2 were waited for; matrix products, arithmetic and copies ran while one was open for 2% of the time, Pallas kernels for 0%

commit v1 on v0

v1 whole, which is shorter than its diff:
```python
import functools
import math

import jax
import jax.numpy as jnp
from jax import lax
from jax.experimental import pallas as pl
from jax.experimental.pallas import tpu as pltpu
from jax.sharding import PartitionSpec as P

BLOCK_ROWS = 128
SCALE = 50.0
EPSILON = 1e-06
LOG2E = math.log2(math.e)
NT = (((1,), (1,)), ((), ()))
NN = (((1,), (0,)), ((), ()))
F32, BF16 = jnp.float32, jnp.bfloat16
NX, NY, NZ, NK = 4, 4, 4, 2
TILE = 512
MIB = 2**20


def params(mib):
    return pltpu.CompilerParams(vmem_limit_bytes=mib * MIB)


def x_perm(shift):
    return [(i, (i + shift) % NX) for i in range(NX)]


def rows_perm(dz, dy, dk):
    out = []
    for z in range(NZ):
        for y in range(NY):
            for k in range(NK):
                target = ((z + dz) % NZ * NY + (y + dy) % NY) * NK + (k + dk) % NK
                out.append(((z * NY + y) * NK + k, target))
    return out


def unit_f32(values):
    squares = jnp.sum(values * values, axis=-1, keepdims=True)
    return values * lax.rsqrt(squares + EPSILON)


def cents_kernel(place_ref, c_ref, all_ref, half_ref):
    step = pl.program_id(0)
    unit = unit_f32(c_ref[...]).astype(BF16)
    all_ref[...] = unit

    @pl.when(step == place_ref[0])
    def _():
        half_ref[...] = unit


def unit_cents(place, centroids):
    n, d = centroids.shape
    half = n // NK
    return pl.pallas_call(
        cents_kernel,
        grid_spec=pltpu.PrefetchScalarGridSpec(
            num_scalar_prefetch=1,
            grid=(NK,),
            in_specs=[pl.BlockSpec((half, d), lambda i, p: (i, 0))],
            out_specs=[
                pl.BlockSpec((half, d), lambda i, p: (i, 0)),
                pl.BlockSpec((half, d), lambda i, p: (0, 0)),
            ],
        ),
        out_shape=[jax.ShapeDtypeStruct((n, d), BF16), jax.ShapeDtypeStruct((half, d), BF16)],
        compiler_params=params(16),
        name="unit_cents",
    )(place, centroids)


def rows_kernel(owner_ref, live_ref, e_ref, out_ref, scaled_ref):
    step = pl.program_id(0)

    @pl.when(step == 0)
    def _():
        out_ref[...] = jnp.zeros_like(out_ref)

    unit = unit_f32(e_ref[...])
    scaled_ref[...] = (unit * (SCALE * LOG2E)).astype(BF16)
    low = unit.astype(BF16)
    count = e_ref.shape[0] // BLOCK_ROWS
    for b in range(count):
        block = step * count + b

        @pl.when(block < live_ref[0])
        def _():
            out_ref[owner_ref[block]] = low[b * BLOCK_ROWS : (b + 1) * BLOCK_ROWS]


def unit_rows(owners, live, embeddings, peers):
    n, d = embeddings.shape
    steps = 4
    return pl.pallas_call(
        rows_kernel,
        grid_spec=pltpu.PrefetchScalarGridSpec(
            num_scalar_prefetch=2,
            grid=(steps,),
            in_specs=[pl.BlockSpec((n // steps, d), lambda i, o, l: (i, 0))],
            out_specs=[
                pl.BlockSpec((peers, BLOCK_ROWS, d), lambda i, o, l: (0, 0, 0)),
                pl.BlockSpec((n // steps, d), lambda i, o, l: (i, 0)),
            ],
        ),
        out_shape=[
            jax.ShapeDtypeStruct((peers, BLOCK_ROWS, d), BF16),
            jax.ShapeDtypeStruct((n, d), BF16),
        ],
        compiler_params=params(24),
        name="unit_rows",
    )(owners, live, embeddings)


def column_sums(r_ref, c_ref, tr):
    n = c_ref.shape[0]
    tc = min(TILE, n)
    out = []
    for c in range(0, n, tc):
        cents = c_ref[c : c + tc, :]
        total = jnp.zeros((8, tc), F32)
        for i in range(0, r_ref.shape[0], tr):
            p = lax.dot_general(r_ref[i : i + tr, :], cents, NT, preferred_element_type=F32)
            total = total + jnp.exp2(p).reshape(tr // 8, 8, tc).sum(0)
        out.append(jnp.sum(total, axis=0, keepdims=True))
    return out


def first_kernel(r_ref, *refs):
    count = len(refs) // 2
    for c_ref, o_ref in zip(refs[:count], refs[count:]):
        tc = min(TILE, c_ref.shape[0])
        for j, part in enumerate(column_sums(r_ref, c_ref, 256)):
            o_ref[:, j * tc : (j + 1) * tc] = part


def first_sweep(scaled, pieces):
    return pl.pallas_call(
        first_kernel,
        out_shape=[jax.ShapeDtypeStruct((1, p.shape[0]), F32) for p in pieces],
        compiler_params=params(24),
        name="first_sweep",
    )(scaled, *pieces)


def last_kernel(off_ref, r_ref, *refs, n_new):
    pieces, ready, o_ref = refs[:n_new], refs[n_new:-1], refs[-1]
    tile = 0
    for ref in ready:
        for j in range(0, ref.shape[1], TILE):
            o_ref[:, pl.ds(pl.multiple_of(off_ref[tile], TILE), TILE)] = ref[:, j : j + TILE]
            tile += 1
    for c_ref in pieces:
        for part in column_sums(r_ref, c_ref, 256):
            o_ref[:, pl.ds(pl.multiple_of(off_ref[tile], TILE), TILE)] = part
            tile += 1


def last_sweep(offsets, scaled, pieces, ready):
    total = sum(p.shape[0] for p in pieces) + sum(p.shape[1] for p in ready)
    vmem = pl.BlockSpec(memory_space=pltpu.VMEM)
    return pl.pallas_call(
        functools.partial(last_kernel, n_new=len(pieces)),
        in_specs=[pl.BlockSpec(memory_space=pltpu.SMEM)] + [vmem] * (1 + len(pieces) + len(ready)),
        out_specs=vmem,
        out_shape=jax.ShapeDtypeStruct((1, total), F32),
        compiler_params=params(24),
        name="last_sweep",
    )(offsets, scaled, *pieces, *ready)


def lane_sum(x):
    parts = [x[:, j : j + 128] for j in range(0, x.shape[1], 128)]
    while len(parts) > 1:
        parts = [parts[i] + parts[i + 1] for i in range(0, len(parts), 2)]
    return parts[0]


def second_kernel(off_ref, r_ref, b_ref, *refs, n_pieces, tr, rg):
    pieces = refs[:n_pieces]
    col_ref, score_ref, e_scr, s_scr, u_scr, i_scr = refs[n_pieces:]
    rows = r_ref.shape[0]
    tiles = [(ref, j) for ref in pieces for j in range(0, ref.shape[0], TILE)]
    offsets = [pl.multiple_of(off_ref[i], TILE) for i in range(len(tiles))]
    col_ref[...] = jnp.zeros_like(col_ref)

    def body(t, carry):
        r = r_ref[pl.ds(pl.multiple_of(t * tr, tr), tr), :]
        for i, (ref, j) in enumerate(tiles):
            p = lax.dot_general(r, ref[j : j + TILE, :], NT, preferred_element_type=F32)
            bias = b_ref[:, pl.ds(offsets[i], TILE)]
            for g in range(0, tr, rg):
                part = p[g : g + rg]
                e = jnp.exp2(part + bias)
                e_scr[g : g + rg, i * TILE : (i + 1) * TILE] = e.astype(BF16)
                q = e * part
                if i == 0:
                    s_scr[g : g + rg] = lane_sum(e)
                    u_scr[g : g + rg] = lane_sum(q)
                else:
                    s_scr[g : g + rg] += lane_sum(e)
                    u_scr[g : g + rg] += lane_sum(q)
        inverse = 1.0 / jnp.sum(s_scr[...].T, axis=0, keepdims=True)
        weighted = jnp.sum(u_scr[...].T, axis=0, keepdims=True)
        score_ref[pl.ds(t, 1), :] = weighted * inverse * (1.0 / LOG2E)
        high = inverse.astype(BF16)
        low = (inverse - high.astype(F32)).astype(BF16)
        i_scr[...] = jnp.concatenate([high, low, jnp.zeros((14, tr), BF16)], axis=0)
        for i in range(len(tiles)):
            part = lax.dot_general(
                i_scr[...], e_scr[:, i * TILE : (i + 1) * TILE], NN, preferred_element_type=F32
            )
            col_ref[:, pl.ds(offsets[i], TILE)] += part[0:8]
        return carry

    lax.fori_loop(0, rows // tr, body, 0)


def second_sweep(offsets, scaled, bias, pieces):
    rows = scaled.shape[0]
    total = sum(p.shape[0] for p in pieces)
    tr = 256
    vmem = pl.BlockSpec(memory_space=pltpu.VMEM)
    return pl.pallas_call(
        functools.partial(second_kernel, n_pieces=len(pieces), tr=tr, rg=16),
        in_specs=[pl.BlockSpec(memory_space=pltpu.SMEM)] + [vmem] * (2 + len(pieces)),
        out_specs=[vmem, vmem],
        out_shape=[
            jax.ShapeDtypeStruct((8, total), F32),
            jax.ShapeDtypeStruct((rows // tr, tr), F32),
        ],
        scratch_shapes=[
            pltpu.VMEM((tr, total), BF16),
            pltpu.VMEM((tr, 128), F32),
            pltpu.VMEM((tr, 128), F32),
            pltpu.VMEM((16, tr), BF16),
        ],
        compiler_params=params(32),
        name="second_sweep",
    )(offsets, scaled, bias, *pieces)


def all_sum(values):
    for name, perms in (
        ("cent", [x_perm(s) for s in (1, 2, 3)]),
        ("rows", [rows_perm(0, s, 0) for s in (1, 2, 3)]),
        ("rows", [rows_perm(s, 0, 0) for s in (1, 2, 3)]),
        ("rows", [rows_perm(0, 0, 1)]),
    ):
        arrived = [lax.ppermute(values, name, perm) for perm in perms]
        for part in arrived:
            values = values + part
    return values


def local(embeddings, centroids, owners, live_blocks):
    x = lax.axis_index("cent")
    row_place = lax.axis_index("rows")
    k = row_place % NK
    y = row_place // NK % NY
    z = row_place // (NK * NY)
    n_cent, d = centroids.shape
    half = n_cent // NK
    rows = embeddings.shape[0]
    peers = NZ * NY * NK
    total = n_cent * NX

    own, mine = unit_cents(k.reshape(1).astype(jnp.int32), centroids)
    right = lax.ppermute(mine, "cent", x_perm(1))
    left = lax.ppermute(mine, "cent", x_perm(-1))
    outgoing, scaled = unit_rows(owners, live_blocks, embeddings, peers)
    arrived = lax.all_to_all(outgoing, "rows", split_axis=0, concat_axis=0, tiled=True)
    far_0 = lax.ppermute(right[: half // 2], "cent", x_perm(1))
    far_1 = lax.ppermute(left[half // 2 :], "cent", x_perm(-1))
    swap = rows_perm(0, 0, 1)
    right_o = lax.ppermute(right, "rows", swap)
    left_o = lax.ppermute(left, "rows", swap)
    far_0o = lax.ppermute(far_0, "rows", swap)
    far_1o = lax.ppermute(far_1, "rows", swap)

    def place(dx, kk, quarter):
        return (x + dx) % NX * n_cent + kk * half + quarter * TILE

    starts = [place(0, q // 2, q % 2) for q in range(4)]
    starts += [place(-1, k, 0), place(-1, k, 1), place(-1, 1 - k, 0), place(-1, 1 - k, 1)]
    starts += [place(1, k, 0), place(1, k, 1), place(1, 1 - k, 0), place(1, 1 - k, 1)]
    starts += [place(2, k, 0), place(2, k, 1), place(2, 1 - k, 0), place(2, 1 - k, 1)]
    offsets = jnp.stack(starts).astype(jnp.int32)

    sums_own = first_sweep(scaled, [own])
    sums_right = first_sweep(scaled, [right, right_o])
    sums_left = first_sweep(scaled, [left, left_o])
    far = [far_0, far_1, far_0o, far_1o]
    column = last_sweep(offsets, scaled, far, [*sums_own, *sums_right, *sums_left])
    column = all_sum(column)
    ratio = float(rows * NX * peers) / total
    bias = jnp.log2(ratio / column)
    pieces = [own, right, right_o, left, left_o, *far]
    column, score = second_sweep(offsets, scaled, bias, pieces)
    column = jnp.sum(column, axis=0)

    blocks = owners.shape[0]
    score = score.astype(BF16).astype(F32).reshape(blocks, BLOCK_ROWS)
    owner_z = (owners // (NK * NY) - z) % NZ
    owner_y = (owners // NK % NY - y) % NY
    owner_k = (owners % NK - k) % NK
    relative = (owner_z * NY + owner_y) * NK + owner_k
    live = jnp.arange(blocks, dtype=jnp.int32) < live_blocks[0]
    hit = (relative[None, :] == jnp.arange(peers, dtype=jnp.int32)[:, None]) & live[None, :]
    sent = jnp.sum(jnp.where(hit[:, :, None], score[None], 0.0), axis=1)
    sent = sent.reshape(NZ, NY * NK * BLOCK_ROWS)

    arrived_x = [lax.ppermute(column, "cent", x_perm(s)) for s in (1, 2, 3)]
    for part in arrived_x:
        column = column + part
    got = [sent[0]]
    new = column
    for s in (1, 2, 3):
        both = lax.ppermute(jnp.concatenate([column, sent[s]]), "rows", rows_perm(s, 0, 0))
        new = new + both[:total]
        got.append(both[total:])
    column = new
    sent = jnp.stack(got).reshape(NZ, NY, NK * BLOCK_ROWS)
    got = [sent[:, 0]]
    for s in (1, 2, 3):
        both = lax.ppermute(
            jnp.concatenate([column, sent[:, s].reshape(-1)]), "rows", rows_perm(0, s, 0)
        )
        new = new + both[:total]
        got.append(both[total:].reshape(NZ, NK * BLOCK_ROWS))
    column = new
    sent = jnp.stack(got, axis=1).reshape(NZ, NY, NK, BLOCK_ROWS)
    both = lax.ppermute(
        jnp.concatenate([column, sent[:, :, 1].reshape(-1)]), "rows", rows_perm(0, 0, 1)
    )
    column = column + both[:total]
    got = jnp.stack([sent[:, :, 0], both[total:].reshape(NZ, NY, BLOCK_ROWS)], axis=2)
    ids = jnp.arange(peers, dtype=jnp.int32)
    src = ((z - ids // (NK * NY)) % NZ * NY + (y - ids // NK % NY) % NY) * NK + (k - ids % NK) % NK
    hit = src[None, :] == ids[:, None]
    got = got.reshape(peers, BLOCK_ROWS)
    moved_score = jnp.sum(jnp.where(hit[:, :, None], got[None], 0.0), axis=1).astype(BF16)

    balance = column * (1.0 / ratio)
    return arrived.reshape(peers * BLOCK_ROWS, d), moved_score.reshape(-1), balance


def solution(mesh):
    placed = (P(("rows", "cent"), None), P("cent", None), P(("rows", "cent")), P(("rows", "cent")))
    return jax.shard_map(
        local,
        mesh=mesh,
        in_specs=placed,
        out_specs=(P(("rows", "cent"), None), P(("rows", "cent")), P()),
        check_vma=False,
    )
```

time: 449 us -> 153 us (0.34)
  matrix products: 238 us -> 0 us
  blocking collectives: 130 us -> 0 us
  Pallas kernels: 0 us -> 36.2 us
  starting transfers between devices: 14.9 us -> 51.1 us
  waiting for transfers between devices: 34 us -> 51.6 us
  between operations: 14.8 us -> 1.64 us
  other arithmetic: 10.3 us -> 3.05 us
    dot_general x50 -> x0, matrix products: 238 us -> none  [the longest x16 68 us: one_tile(): running = running + jnp.dot(inverse, weights, precision=HIGHEST)]
    psum x2 -> x0, blocking collectives: 130 us -> none  [local(): column_total = lax.psum(column, ('rows', 'cent'))]
    ppermute x0 -> x28, waiting for transfers between devices: none -> 51.6 us  [the longest x10 27.5 us: all_sum(): arrived = [lax.ppermute(values, name, perm) for perm in perms]]
    ppermute x0 -> x28, starting transfers between devices: none -> 42.2 us  [the longest x10 15.8 us: all_sum(): arrived = [lax.ppermute(values, name, perm) for perm in perms]]
    pallas_call x0 -> x7, Pallas kernels: none -> 36.2 us  [the longest x1 21.5 us: second_sweep(): pl.pallas_call(functools.partial(second_kernel, n_pieces=len(pieces), tr=...]
    all_to_all x1, waiting for transfers between devices: 27.8 us -> 0.01 us  [local(): lax.all_to_all(outgoing, 'rows', split_axis=0, concat_axis=0, tiled=True)]
    unnamed x3 -> x14, local copies, waits for them, and re-layouts: 1.32 us -> 8.25 us
    all_gather x1 -> x0, waiting for transfers between devices: 6.19 us -> none  [local(): centres = lax.all_gather(unit_own, 'cent', axis=0, tiled=True)]
  transfers between devices with their start and end apart: 3 -> 29, of which waited for: 2 -> 17; matrix products, arithmetic and copies ran while one was open for 2% -> 2% of each run, Pallas kernels for 0% -> 21%
where the time goes in v1:
time: 153 us; the launch traced here: 152 us
  waiting for transfers between devices  51.6 us (34%)
  starting transfers between devices  51.1 us (33%)
  Pallas kernels  36.2 us (24%)
  local copies, waits for them, and re-layouts  8.51 us (6%)
  other arithmetic  3.05 us (2%)
  between operations  1.64 us (1%)
    ppermute x10, waiting for transfers between devices, all_sum(): arrived = [lax.ppermute(values, name, perm) for perm in perms]  27.5 us
    pallas_call x1, Pallas kernels, second_sweep(): pl.pallas_call(functools.partial(second_kernel, n_pieces=len(pieces), tr=...  21.5 us
    ppermute x10, starting transfers between devices, all_sum(): arrived = [lax.ppermute(values, name, perm) for perm in perms]  15.8 us
    ppermute x1, waiting for transfers between devices, local(): right = lax.ppermute(mine, 'cent', x_perm(1))  11.1 us
    pallas_call x3, Pallas kernels, first_sweep(): pl.pallas_call(first_kernel, out_shape=[jax.ShapeDtypeStruct((1, p.shape[...  9.22 us
    all_to_all x1, starting transfers between devices, local(): lax.all_to_all(outgoing, 'rows', split_axis=0, concat_axis=0, tiled=True)  8.9 us
    unnamed x14, local copies, waits for them, and re-layouts  8.25 us
    ppermute x1, starting transfers between devices, local(): lax.ppermute(jnp.concatenate([column, sent[:, :, 1].reshape(-1)]), 'rows'...  5.29 us
  transfers between devices with their start and end apart: 29, of which 17 were waited for; matrix products, arithmetic and copies ran while one was open for 2% of the time, Pallas kernels for 21%

profile of v1, /device:TPU:1, one launch (start us, length us, event | category | flops | bytes accessed | tf_op | source)
XLA Modules:
  0.0 152.1 jit_solution(2051115761808172057)
XLA Ops:
  2.7 2.1 %collective-permute-start = (bf16[1024,256]{1,0:T(8,128)(2,1)S(1)}, bf16[1024,256]{1,0:T(8,128)(2,1)S(1)}, u32[]{:S(2)}, u32[]{:S(2)}) collective-permute-start(bf16[1024,256]{1,0:T(8,128)(2,1)S(1)} %get-tuple-element.15), channel_id=1, source_target_pairs={{0,1},{1,2},{2,3},{3,0},{4,5},{5,6},{6,7},{7,4},{8,9},{9,10},{10,1... | collective-permute-start | bytes 1572872 | tf_op jit(solution)/shard_map/ppermute | solution.py:272
  6.2 11.1 %collective-permute-done.refs_0_.refs_1_ = bf16[1024,256]{1,0:T(8,128)(2,1)S(1)} collective-permute-done((bf16[1024,256]{1,0:T(8,128)(2,1)S(1)}, bf16[1024,256]{1,0:T(8,128)(2,1)S(1)}, u32[]{:S(2)}, u32[]{:S(2)}) %collective-permute-start) | collective-permute-done | bytes 524320 | tf_op jit(solution)/shard_map/ppermute | solution.py:272
  19.6 2.6 %collective-permute-start.3 = (bf16[512,256]{1,0:T(8,128)(2,1)S(1)}, bf16[512,256]{1,0:T(8,128)(2,1)}, u32[]{:S(2)}, u32[]{:S(2)}) collective-permute-start(bf16[512,256]{1,0:T(8,128)(2,1)S(1)} %slice.180), channel_id=1, source_target_pairs={{0,3},{1,0},{2,1},{3,2},{4,7},{5,4},{6,5},{7,6},{8,11},{9,8},{10,9... | collective-permute-start | bytes 786440 | tf_op jit(solution)/shard_map/ppermute | solution.py:277
  22.1 2.6 %collective-permute-done.1.refs_0_.refs_5_ = bf16[512,256]{1,0:T(8,128)(2,1)S(1)} collective-permute-done((bf16[512,256]{1,0:T(8,128)(2,1)S(1)}, bf16[512,256]{1,0:T(8,128)(2,1)S(1)}, u32[]{:S(2)}, u32[]{:S(2)}) %collective-permute-start.1) | collective-permute-done | bytes 262176 | tf_op jit(solution)/shard_map/ppermute | solution.py:276
  24.8 2.6 %collective-permute-start.4 = (bf16[512,256]{1,0:T(8,128)(2,1)S(1)}, bf16[512,256]{1,0:T(8,128)(2,1)}, u32[]{:S(2)}, u32[]{:S(2)}) collective-permute-start(bf16[512,256]{1,0:T(8,128)(2,1)S(1)} %collective-permute-done.1.refs_0_.refs_5_), channel_id=1, source_target_pairs={{0,4},{4,0},{8,12},{12,8},{16,20},{20,16},{24,28},{28,24},{32,36},... | collective-permute-start | bytes 786440 | tf_op jit(solution)/shard_map/ppermute | solution.py:281
  33.8 2.4 %first_sweep.3.refs_4_ = f32[1,2048]{1,0:T(1,128)S(1)} custom-call(bf16[2048,256]{1,0:T(8,128)(2,1)S(1)} %get-tuple-element.14.r_ref, bf16[2048,256]{1,0:T(8,128)(2,1)S(1)} %get-tuple-element.16.refs_0_), custom_call_target="tpu_custom_call" | custom-call | tf_op jit(solution)/shard_map/first_sweep/pallas_call | solution.py:141
  36.3 3.4 %first_sweep.4 = (f32[1,1024]{1,0:T(1,128)S(1)}, f32[1,1024]{1,0:T(1,128)S(1)}) custom-call(bf16[2048,256]{1,0:T(8,128)(2,1)S(1)} %get-tuple-element.14.r_ref, bf16[1024,256]{1,0:T(8,128)(2,1)S(1)} %collective-permute-done.refs_0_.refs_1_, bf16[1024,256]{1,0:T(8,128)(2,1)} %collective-permute-done.6.refs_1_.refs_2_), custom_call_target="tpu_custom_call" | custom-call | tf_op jit(solution)/shard_map/first_sweep/pallas_call | solution.py:141
  39.7 3.4 %first_sweep.5 = (f32[1,1024]{1,0:T(1,128)S(1)}, f32[1,1024]{1,0:T(1,128)S(1)}) custom-call(bf16[2048,256]{1,0:T(8,128)(2,1)S(1)} %get-tuple-element.14.r_ref, bf16[1024,256]{1,0:T(8,128)(2,1)S(1)} %collective-permute-done.2.refs_0_.refs_3_, bf16[1024,256]{1,0:T(8,128)(2,1)} %collective-permute-done.7.refs_1_.refs_4_), custom_call_target="tpu_custom_call" | custom-call | tf_op jit(solution)/shard_map/first_sweep/pallas_call | solution.py:141
  43.1 3.5 %last_sweep.1 = f32[1,8192]{1,0:T(1,128)S(1)} custom-call(s32[16]{0:T(128)S(1)} %stack.81.off_ref, bf16[2048,256]{1,0:T(8,128)(2,1)S(1)} %get-tuple-element.14.r_ref, bf16[512,256]{1,0:T(8,128)(2,1)S(1)} %collective-permute-done.1.refs_0_.refs_5_, bf16[512,256]{1,0:T(8,128)(2,1)} %collective-permute-done.3.refs_1_.refs_6_, ...), custom_call_target="tpu_custom_call" | custom-call | tf_op jit(solution)/shard_map/last_sweep/pallas_call | solution.py:165
  46.7 3.6 %collective-permute-start.10 = (f32[1,8192]{1,0:T(1,128)S(1)}, f32[1,8192]{1,0:T(1,128)S(1)}, u32[]{:S(2)}, u32[]{:S(2)}) collective-permute-start(f32[1,8192]{1,0:T(1,128)S(1)} %last_sweep.1), channel_id=1, source_target_pairs={{0,3},{1,0},{2,1},{3,2},{4,7},{5,4},{6,5},{7,6},{8,11},{9,8},{10,9... | collective-permute-start | bytes 98312 | tf_op jit(solution)/shard_map/ppermute | solution.py:253
  50.9 8.9 %all-to-all-start = ((bf16[32,128,256]{2,1,0:T(8,128)(2,1)}), bf16[32,128,256]{2,1,0:T(8,128)(2,1)}, u32[]{:S(2)}, u32[]{:S(2)}) async-start(bf16[32,128,256]{2,1,0:T(8,128)(2,1)} %copy-done.2), calls=%async_computation | async-start | bytes 4194304 | tf_op jit(solution)/shard_map/all_to_all | solution.py:275
  60.0 2.9 %collective-permute-start.13 = (f32[1,8192]{1,0:T(1,128)S(1)}, f32[1,8192]{1,0:T(1,128)S(1)}, u32[]{:S(2)}, u32[]{:S(2)}) collective-permute-start(f32[1,8192]{1,0:T(1,128)S(1)} %add_add_fusion.3), channel_id=1, source_target_pairs={{0,24},{4,28},{8,0},{12,4},{16,8},{20,12},{24,16},{28,20},{32,56},... | collective-permute-start | bytes 98312 | tf_op jit(solution)/shard_map/ppermute | solution.py:253
  64.0 21.1 %collective-permute-done.13 = f32[1,8192]{1,0:T(1,128)S(1)} collective-permute-done((f32[1,8192]{1,0:T(1,128)S(1)}, f32[1,8192]{1,0:T(1,128)S(1)}, u32[]{:S(2)}, u32[]{:S(2)}) %collective-permute-start.13) | collective-permute-done | bytes 32800 | tf_op jit(solution)/shard_map/ppermute | solution.py:253
  87.0 3.4 %collective-permute-start.16 = (f32[1,8192]{1,0:T(1,128)S(1)}, f32[1,8192]{1,0:T(1,128)S(1)}, u32[]{:S(2)}, u32[]{:S(2)}) collective-permute-start(f32[1,8192]{1,0:T(1,128)S(1)} %add_add_fusion.2), channel_id=1, source_target_pairs={{0,96},{4,100},{8,104},{12,108},{16,112},{20,116},{24,120},{28,124... | collective-permute-start | bytes 98312 | tf_op jit(solution)/shard_map/ppermute | solution.py:253
  91.4 3.2 %collective-permute-done.15 = f32[1,8192]{1,0:T(1,128)S(1)} collective-permute-done((f32[1,8192]{1,0:T(1,128)S(1)}, f32[1,8192]{1,0:T(1,128)S(1)}, u32[]{:S(2)}, u32[]{:S(2)}) %collective-permute-start.15) | collective-permute-done | bytes 32800 | tf_op jit(solution)/shard_map/ppermute | solution.py:253
  95.0 3.2 %collective-permute-start.17 = (f32[1,8192]{1,0:T(1,128)S(1)}, f32[1,8192]{1,0:T(1,128)S(1)}, u32[]{:S(2)}, u32[]{:S(2)}) collective-permute-start(f32[1,8192]{1,0:T(1,128)S(1)} %add_add_fusion.1), channel_id=1, source_target_pairs={{0,4},{4,0},{8,12},{12,8},{16,20},{20,16},{24,28},{28,24},{32,36},... | collective-permute-start | bytes 98312 | tf_op jit(solution)/shard_map/ppermute | solution.py:253
  99.2 21.5 %second_sweep.1 = (f32[8,8192]{1,0:T(8,128)S(1)}, f32[8,256]{1,0:T(8,128)S(1)}) custom-call(s32[16]{0:T(128)S(1)} %stack.81.off_ref, bf16[2048,256]{1,0:T(8,128)(2,1)S(1)} %get-tuple-element.14.r_ref, f32[1,8192]{1,0:T(1,128)S(1)} %log_multiply_fusion.b_ref, bf16[2048,256]{1,0:T(8,128)(2,1)S(1)} %get-tuple-element.16.refs_0_, ...), custom_call_target="tpu_custom_call" | custom-call | tf_op jit(solution)/shard_map/second_sweep/pallas_call | solution.py:227
  122.4 2.0 %collective-permute-start.20 = (f32[8192]{0:T(1024)S(1)}, f32[8192]{0:T(1024)S(1)}, u32[]{:S(2)}, u32[]{:S(2)}) collective-permute-start(f32[8192]{0:T(1024)S(1)} %reduce_sum.28), channel_id=1, source_target_pairs={{0,3},{1,0},{2,1},{3,2},{4,7},{5,4},{6,5},{7,6},{8,11},{9,8},{10,9... | collective-permute-start | bytes 98312 | tf_op jit(solution)/shard_map/ppermute | solution.py:316
  124.4 2.0 %collective-permute-start.19 = (f32[8192]{0:T(1024)S(1)}, f32[8192]{0:T(1024)S(1)}, u32[]{:S(2)}, u32[]{:S(2)}) collective-permute-start(f32[8192]{0:T(1024)S(1)} %reduce_sum.28), channel_id=1, source_target_pairs={{0,2},{1,3},{2,0},{3,1},{4,6},{5,7},{6,4},{7,5},{8,10},{9,11},{10,... | collective-permute-start | bytes 98312 | tf_op jit(solution)/shard_map/ppermute | solution.py:316
  126.6 2.0 %collective-permute-done.19 = f32[8192]{0:T(1024)S(1)} collective-permute-done((f32[8192]{0:T(1024)S(1)}, f32[8192]{0:T(1024)S(1)}, u32[]{:S(2)}, u32[]{:S(2)}) %collective-permute-start.19) | collective-permute-done | bytes 32800 | tf_op jit(solution)/shard_map/ppermute | solution.py:316
  131.8 2.0 %collective-permute-start.23 = (f32[9216]{0:T(1024)S(1)}, f32[9216]{0:T(1024)S(1)}, u32[]{:S(2)}, u32[]{:S(2)}) collective-permute-start(f32[9216]{0:T(1024)S(1)} %get-tuple-element.26), channel_id=1, source_target_pairs={{0,96},{4,100},{8,104},{12,108},{16,112},{20,116},{24,120},{28,124... | collective-permute-start | bytes 110600 | tf_op jit(solution)/shard_map/ppermute | solution.py:322
  138.6 2.1 %collective-permute-done.25 = f32[9216]{0:T(1024)S(1)} collective-permute-done((f32[9216]{0:T(1024)S(1)}, f32[9216]{0:T(1024)S(1)}, u32[]{:S(2)}, u32[]{:S(2)}) %collective-permute-start.25) | collective-permute-done | bytes 36896 | tf_op jit(solution)/shard_map/ppermute | solution.py:329
  141.4 5.3 %collective-permute-start.27 = (f32[10240]{0:T(1024)S(1)}, f32[10240]{0:T(1024)S(1)}, u32[]{:S(2)}, u32[]{:S(2)}) collective-permute-start(f32[10240]{0:T(1024)S(1)} %pad_maximum_fusion), channel_id=1, source_target_pairs={{0,4},{4,0},{8,12},{12,8},{16,20},{20,16},{24,28},{28,24},{32,36},... | collective-permute-start | bytes 122888 | tf_op jit(solution)/shard_map/ppermute | solution.py:336
  149.0 3.0 %copy.12 = bf16[4096,256]{1,0:T(8,128)(2,1)} copy(bf16[4096,256]{1,0:T(8,128)(2,1)} %bitcast) | data formatting | bytes 4194304
  (97 shorter events, 30.4 us)
Async XLA Ops:
  2.7 14.6 %collective-permute-start = (bf16[1024,256]{1,0:T(8,128)(2,1)S(1)}, bf16[1024,256]{1,0:T(8,128)(2,1)S(1)}, u32[]{:S(2)}, u32[]{:S(2)}) collective-permute-start(bf16[1024,256]{1,0:T(8,128)(2,1)S(1)} %get-tuple-element.15), channel_id=1, source_target_pairs={{0,1},{1,2},{2,3},{3,0},{4,5},{5,6},{6,7},{7,4},{8,9},{9,10},{10,1... | collective-permute-start | bytes 1572872 | tf_op jit(solution)/shard_map/ppermute | solution.py:272
  4.9 14.7 %collective-permute-start.2 = (bf16[1024,256]{1,0:T(8,128)(2,1)S(1)}, bf16[1024,256]{1,0:T(8,128)(2,1)S(1)}, u32[]{:S(2)}, u32[]{:S(2)}) collective-permute-start(bf16[1024,256]{1,0:T(8,128)(2,1)S(1)} %get-tuple-element.15), channel_id=1, source_target_pairs={{0,3},{1,0},{2,1},{3,2},{4,7},{5,4},{6,5},{7,6},{8,11},{9,8},{10,9... | collective-permute-start | bytes 1572872 | tf_op jit(solution)/shard_map/ppermute | solution.py:273
  17.3 7.4 %collective-permute-start.1 = (bf16[512,256]{1,0:T(8,128)(2,1)S(1)}, bf16[512,256]{1,0:T(8,128)(2,1)S(1)}, u32[]{:S(2)}, u32[]{:S(2)}) collective-permute-start(bf16[512,256]{1,0:T(8,128)(2,1)S(1)} %slice.179), channel_id=1, source_target_pairs={{0,1},{1,2},{2,3},{3,0},{4,5},{5,6},{6,7},{7,4},{8,9},{9,10},{10,1... | collective-permute-start | bytes 786440 | tf_op jit(solution)/shard_map/ppermute | solution.py:276
  17.7 18.5 %collective-permute-start.6 = (bf16[1024,256]{1,0:T(8,128)(2,1)S(1)}, bf16[1024,256]{1,0:T(8,128)(2,1)}, u32[]{:S(2)}, u32[]{:S(2)}) collective-permute-start(bf16[1024,256]{1,0:T(8,128)(2,1)S(1)} %collective-permute-done.refs_0_.refs_1_), channel_id=1, source_target_pairs={{0,4},{4,0},{8,12},{12,8},{16,20},{20,16},{24,28},{28,24},{32,36},... | collective-permute-start | bytes 1572872 | tf_op jit(solution)/shard_map/ppermute | solution.py:279
  19.6 20.1 %collective-permute-start.7 = (bf16[1024,256]{1,0:T(8,128)(2,1)S(1)}, bf16[1024,256]{1,0:T(8,128)(2,1)}, u32[]{:S(2)}, u32[]{:S(2)}) collective-permute-start(bf16[1024,256]{1,0:T(8,128)(2,1)S(1)} %collective-permute-done.2.refs_0_.refs_3_), channel_id=1, source_target_pairs={{0,4},{4,0},{8,12},{12,8},{16,20},{20,16},{24,28},{28,24},{32,36},... | collective-permute-start | bytes 1572872 | tf_op jit(solution)/shard_map/ppermute | solution.py:280
  19.6 7.8 %collective-permute-start.3 = (bf16[512,256]{1,0:T(8,128)(2,1)S(1)}, bf16[512,256]{1,0:T(8,128)(2,1)}, u32[]{:S(2)}, u32[]{:S(2)}) collective-permute-start(bf16[512,256]{1,0:T(8,128)(2,1)S(1)} %slice.180), channel_id=1, source_target_pairs={{0,3},{1,0},{2,1},{3,2},{4,7},{5,4},{6,5},{7,6},{8,11},{9,8},{10,9... | collective-permute-start | bytes 786440 | tf_op jit(solution)/shard_map/ppermute | solution.py:277
  24.8 18.4 %collective-permute-start.4 = (bf16[512,256]{1,0:T(8,128)(2,1)S(1)}, bf16[512,256]{1,0:T(8,128)(2,1)}, u32[]{:S(2)}, u32[]{:S(2)}) collective-permute-start(bf16[512,256]{1,0:T(8,128)(2,1)S(1)} %collective-permute-done.1.refs_0_.refs_5_), channel_id=1, source_target_pairs={{0,4},{4,0},{8,12},{12,8},{16,20},{20,16},{24,28},{28,24},{32,36},... | collective-permute-start | bytes 786440 | tf_op jit(solution)/shard_map/ppermute | solution.py:281
  27.4 15.8 %collective-permute-start.5 = (bf16[512,256]{1,0:T(8,128)(2,1)}, bf16[512,256]{1,0:T(8,128)(2,1)}, u32[]{:S(2)}, u32[]{:S(2)}) collective-permute-start(bf16[512,256]{1,0:T(8,128)(2,1)} %collective-permute-done.3.refs_1_.refs_6_), channel_id=1, source_target_pairs={{0,4},{4,0},{8,12},{12,8},{16,20},{20,16},{24,28},{28,24},{32,36},... | collective-permute-start | bytes 786440 | tf_op jit(solution)/shard_map/ppermute | solution.py:282
  46.7 13.2 %collective-permute-start.10 = (f32[1,8192]{1,0:T(1,128)S(1)}, f32[1,8192]{1,0:T(1,128)S(1)}, u32[]{:S(2)}, u32[]{:S(2)}) collective-permute-start(f32[1,8192]{1,0:T(1,128)S(1)} %last_sweep.1), channel_id=1, source_target_pairs={{0,3},{1,0},{2,1},{3,2},{4,7},{5,4},{6,5},{7,6},{8,11},{9,8},{10,9... | collective-permute-start | bytes 98312 | tf_op jit(solution)/shard_map/ppermute | solution.py:253
  50.2 9.6 %collective-permute-start.9 = (f32[1,8192]{1,0:T(1,128)S(1)}, f32[1,8192]{1,0:T(1,128)S(1)}, u32[]{:S(2)}, u32[]{:S(2)}) collective-permute-start(f32[1,8192]{1,0:T(1,128)S(1)} %last_sweep.1), channel_id=1, source_target_pairs={{0,2},{1,3},{2,0},{3,1},{4,6},{5,7},{6,4},{7,5},{8,10},{9,11},{10,... | collective-permute-start | bytes 98312 | tf_op jit(solution)/shard_map/ppermute | solution.py:253
  50.3 9.6 %collective-permute-start.8 = (f32[1,8192]{1,0:T(1,128)S(1)}, f32[1,8192]{1,0:T(1,128)S(1)}, u32[]{:S(2)}, u32[]{:S(2)}) collective-permute-start(f32[1,8192]{1,0:T(1,128)S(1)} %last_sweep.1), channel_id=1, source_target_pairs={{0,1},{1,2},{2,3},{3,0},{4,5},{5,6},{6,7},{7,4},{8,9},{9,10},{10,1... | collective-permute-start | bytes 98312 | tf_op jit(solution)/shard_map/ppermute | solution.py:253
  50.9 98.1 %all-to-all-start = ((bf16[32,128,256]{2,1,0:T(8,128)(2,1)}), bf16[32,128,256]{2,1,0:T(8,128)(2,1)}, u32[]{:S(2)}, u32[]{:S(2)}) async-start(bf16[32,128,256]{2,1,0:T(8,128)(2,1)} %copy-done.2), calls=%async_computation | async-start | bytes 4194304 | tf_op jit(solution)/shard_map/all_to_all | solution.py:275
  60.0 25.2 %collective-permute-start.13 = (f32[1,8192]{1,0:T(1,128)S(1)}, f32[1,8192]{1,0:T(1,128)S(1)}, u32[]{:S(2)}, u32[]{:S(2)}) collective-permute-start(f32[1,8192]{1,0:T(1,128)S(1)} %add_add_fusion.3), channel_id=1, source_target_pairs={{0,24},{4,28},{8,0},{12,4},{16,8},{20,12},{24,16},{28,20},{32,56},... | collective-permute-start | bytes 98312 | tf_op jit(solution)/shard_map/ppermute | solution.py:253
  62.9 24.0 %collective-permute-start.12 = (f32[1,8192]{1,0:T(1,128)S(1)}, f32[1,8192]{1,0:T(1,128)S(1)}, u32[]{:S(2)}, u32[]{:S(2)}) collective-permute-start(f32[1,8192]{1,0:T(1,128)S(1)} %add_add_fusion.3), channel_id=1, source_target_pairs={{0,16},{4,20},{8,24},{12,28},{16,0},{20,4},{24,8},{28,12},{32,48},... | collective-permute-start | bytes 98312 | tf_op jit(solution)/shard_map/ppermute | solution.py:253
  63.4 23.5 %collective-permute-start.11 = (f32[1,8192]{1,0:T(1,128)S(1)}, f32[1,8192]{1,0:T(1,128)S(1)}, u32[]{:S(2)}, u32[]{:S(2)}) collective-permute-start(f32[1,8192]{1,0:T(1,128)S(1)} %add_add_fusion.3), channel_id=1, source_target_pairs={{0,8},{4,12},{8,16},{12,20},{16,24},{20,28},{24,0},{28,4},{32,40},... | collective-permute-start | bytes 98312 | tf_op jit(solution)/shard_map/ppermute | solution.py:253
  87.0 4.4 %collective-permute-start.16 = (f32[1,8192]{1,0:T(1,128)S(1)}, f32[1,8192]{1,0:T(1,128)S(1)}, u32[]{:S(2)}, u32[]{:S(2)}) collective-permute-start(f32[1,8192]{1,0:T(1,128)S(1)} %add_add_fusion.2), channel_id=1, source_target_pairs={{0,96},{4,100},{8,104},{12,108},{16,112},{20,116},{24,120},{28,124... | collective-permute-start | bytes 98312 | tf_op jit(solution)/shard_map/ppermute | solution.py:253
  90.3 4.3 %collective-permute-start.15 = (f32[1,8192]{1,0:T(1,128)S(1)}, f32[1,8192]{1,0:T(1,128)S(1)}, u32[]{:S(2)}, u32[]{:S(2)}) collective-permute-start(f32[1,8192]{1,0:T(1,128)S(1)} %add_add_fusion.2), channel_id=1, source_target_pairs={{0,64},{4,68},{8,72},{12,76},{16,80},{20,84},{24,88},{28,92},{32,9... | collective-permute-start | bytes 98312 | tf_op jit(solution)/shard_map/ppermute | solution.py:253
  95.0 4.1 %collective-permute-start.17 = (f32[1,8192]{1,0:T(1,128)S(1)}, f32[1,8192]{1,0:T(1,128)S(1)}, u32[]{:S(2)}, u32[]{:S(2)}) collective-permute-start(f32[1,8192]{1,0:T(1,128)S(1)} %add_add_fusion.1), channel_id=1, source_target_pairs={{0,4},{4,0},{8,12},{12,8},{16,20},{20,16},{24,28},{28,24},{32,36},... | collective-permute-start | bytes 98312 | tf_op jit(solution)/shard_map/ppermute | solution.py:253
  122.4 4.2 %collective-permute-start.20 = (f32[8192]{0:T(1024)S(1)}, f32[8192]{0:T(1024)S(1)}, u32[]{:S(2)}, u32[]{:S(2)}) collective-permute-start(f32[8192]{0:T(1024)S(1)} %reduce_sum.28), channel_id=1, source_target_pairs={{0,3},{1,0},{2,1},{3,2},{4,7},{5,4},{6,5},{7,6},{8,11},{9,8},{10,9... | collective-permute-start | bytes 98312 | tf_op jit(solution)/shard_map/ppermute | solution.py:316
  124.4 4.3 %collective-permute-start.19 = (f32[8192]{0:T(1024)S(1)}, f32[8192]{0:T(1024)S(1)}, u32[]{:S(2)}, u32[]{:S(2)}) collective-permute-start(f32[8192]{0:T(1024)S(1)} %reduce_sum.28), channel_id=1, source_target_pairs={{0,2},{1,3},{2,0},{3,1},{4,6},{5,7},{6,4},{7,5},{8,10},{9,11},{10,... | collective-permute-start | bytes 98312 | tf_op jit(solution)/shard_map/ppermute | solution.py:316
  130.4 4.1 %collective-permute-start.21 = (f32[9216]{0:T(1024)S(1)}, f32[9216]{0:T(1024)S(1)}, u32[]{:S(2)}, u32[]{:S(2)}) collective-permute-start(f32[9216]{0:T(1024)S(1)} %get-tuple-element.28), channel_id=1, source_target_pairs={{0,32},{4,36},{8,40},{12,44},{16,48},{20,52},{24,56},{28,60},{32,6... | collective-permute-start | bytes 110600 | tf_op jit(solution)/shard_map/ppermute | solution.py:322
  130.5 4.4 %collective-permute-start.22 = (f32[9216]{0:T(1024)S(1)}, f32[9216]{0:T(1024)S(1)}, u32[]{:S(2)}, u32[]{:S(2)}) collective-permute-start(f32[9216]{0:T(1024)S(1)} %get-tuple-element.27), channel_id=1, source_target_pairs={{0,64},{4,68},{8,72},{12,76},{16,80},{20,84},{24,88},{28,92},{32,9... | collective-permute-start | bytes 110600 | tf_op jit(solution)/shard_map/ppermute | solution.py:322
  136.4 4.3 %collective-permute-start.25 = (f32[9216]{0:T(1024)S(1)}, f32[9216]{0:T(1024)S(1)}, u32[]{:S(2)}, u32[]{:S(2)}) collective-permute-start(f32[9216]{0:T(1024)S(1)} %get-tuple-element.24), channel_id=1, source_target_pairs={{0,16},{4,20},{8,24},{12,28},{16,0},{20,4},{24,8},{28,12},{32,48},... | collective-permute-start | bytes 110600 | tf_op jit(solution)/shard_map/ppermute | solution.py:329
  141.4 6.2 %collective-permute-start.27 = (f32[10240]{0:T(1024)S(1)}, f32[10240]{0:T(1024)S(1)}, u32[]{:S(2)}, u32[]{:S(2)}) collective-permute-start(f32[10240]{0:T(1024)S(1)} %pad_maximum_fusion), channel_id=1, source_target_pairs={{0,4},{4,0},{8,12},{12,8},{16,20},{20,16},{24,28},{28,24},{32,36},... | collective-permute-start | bytes 122888 | tf_op jit(solution)/shard_map/ppermute | solution.py:336
  (10 other events, 52.7 us)

commit v2 on v1

v2 whole, which is shorter than its diff:
```python
import functools
import math

import jax
import jax.numpy as jnp
from jax import lax
from jax.experimental import pallas as pl
from jax.experimental.pallas import tpu as pltpu
from jax.sharding import PartitionSpec as P

BLOCK_ROWS = 128
SCALE = 50.0
EPSILON = 1e-06
LOG2E = math.log2(math.e)
NT = (((1,), (1,)), ((), ()))
NN = (((1,), (0,)), ((), ()))
F32, BF16 = jnp.float32, jnp.bfloat16
NX, NY, NZ, NK = 4, 4, 4, 2
TILE = 512
ROW_TILE = 512
MIB = 2**20


def params(mib):
    return pltpu.CompilerParams(vmem_limit_bytes=mib * MIB)


def in_hbm(x):
    return pltpu.with_memory_space_constraint(x, pltpu.HBM)


def in_vmem(x):
    return pltpu.with_memory_space_constraint(x, pltpu.VMEM)


def cost(rows, cents, passes):
    return pl.CostEstimate(flops=passes * rows, transcendentals=0, bytes_accessed=cents)


def x_perm(shift):
    return [(i, (i + shift) % NX) for i in range(NX)]


def rows_perm(dz, dy, dk):
    out = []
    for z in range(NZ):
        for y in range(NY):
            for k in range(NK):
                target = ((z + dz) % NZ * NY + (y + dy) % NY) * NK + (k + dk) % NK
                out.append(((z * NY + y) * NK + k, target))
    return out


def unit_f32(values):
    squares = jnp.sum(values * values, axis=-1, keepdims=True)
    return values * lax.rsqrt(squares + EPSILON)


def cents_kernel(place_ref, c_ref, all_ref, half_ref, buf, sems):
    half = buf.shape[1]
    copies = []
    for i in range(NK):
        start = pl.multiple_of((place_ref[0] ^ i) * half, half)
        copies.append(pltpu.make_async_copy(c_ref.at[pl.ds(start, half), :], buf.at[i], sems.at[i]))
    for copy in copies:
        copy.start()
    for i, copy in enumerate(copies):
        copy.wait()
        unit = unit_f32(buf[i]).astype(BF16)
        all_ref[pl.ds(pl.multiple_of((place_ref[0] ^ i) * half, half), half), :] = unit
        if i == 0:
            half_ref[...] = unit


def unit_cents(place, centroids):
    n, d = centroids.shape
    half = n // NK
    vmem = pl.BlockSpec(memory_space=pltpu.VMEM)
    return pl.pallas_call(
        cents_kernel,
        in_specs=[pl.BlockSpec(memory_space=pltpu.SMEM), pl.BlockSpec(memory_space=pltpu.HBM)],
        out_specs=[vmem, vmem],
        out_shape=[pltpu.VMEM((n, d), BF16), pltpu.VMEM((half, d), BF16)],
        scratch_shapes=[pltpu.VMEM((NK, half, d), F32), pltpu.SemaphoreType.DMA((NK,))],
        compiler_params=params(8),
        name="unit_cents",
    )(place, in_hbm(centroids))


def forward_kernel(right_ref, left_ref, first_ref, second_ref):
    n = first_ref.shape[0]
    first_ref[...] = right_ref[:n, :]
    second_ref[...] = left_ref[n:, :]


def forward_parts(right, left):
    n, d = right.shape
    vmem = pl.BlockSpec(memory_space=pltpu.VMEM)
    return pl.pallas_call(
        forward_kernel,
        in_specs=[vmem, vmem],
        out_specs=[vmem, vmem],
        out_shape=[jax.ShapeDtypeStruct((n // 2, d), BF16)] * 2,
        compiler_params=params(8),
        cost_estimate=cost(2**26, 0, 2**11),
        name="forward_parts",
    )(right, left)


def rows_kernel(owner_ref, live_ref, e_ref, out_ref, scaled_ref):
    step = pl.program_id(0)

    @pl.when(step == 0)
    def _():
        out_ref[...] = jnp.zeros_like(out_ref)

    unit = unit_f32(e_ref[...])
    scaled_ref[...] = (unit * (SCALE * LOG2E)).astype(BF16)
    low = unit.astype(BF16)
    count = e_ref.shape[0] // BLOCK_ROWS
    for b in range(count):
        block = step * count + b

        @pl.when(block < live_ref[0])
        def _():
            out_ref[owner_ref[block]] = low[b * BLOCK_ROWS : (b + 1) * BLOCK_ROWS]


def unit_rows(owners, live, embeddings, peers):
    n, d = embeddings.shape
    steps = 4
    return pl.pallas_call(
        rows_kernel,
        grid_spec=pltpu.PrefetchScalarGridSpec(
            num_scalar_prefetch=2,
            grid=(steps,),
            in_specs=[pl.BlockSpec((n // steps, d), lambda i, o, l: (i, 0))],
            out_specs=[
                pl.BlockSpec((peers, BLOCK_ROWS, d), lambda i, o, l: (0, 0, 0)),
                pl.BlockSpec((n // steps, d), lambda i, o, l: (i, 0)),
            ],
        ),
        out_shape=[pltpu.HBM((peers, BLOCK_ROWS, d), BF16), pltpu.VMEM((n, d), BF16)],
        compiler_params=params(8),
        name="unit_rows",
    )(owners, live, embeddings)


def column_sums(r_ref, c_ref, tr):
    n = c_ref.shape[0]
    tc = min(TILE, n)
    out = []
    for c in range(0, n, tc):
        cents = c_ref[c : c + tc, :]
        total = jnp.zeros((8, tc), F32)
        for i in range(0, r_ref.shape[0], tr):
            p = lax.dot_general(r_ref[i : i + tr, :], cents, NT, preferred_element_type=F32)
            total = total + jnp.exp2(p).reshape(tr // 8, 8, tc).sum(0)
        out.append(jnp.sum(total, axis=0, keepdims=True))
    return out


def first_kernel(r_ref, *refs):
    count = len(refs) // 2
    for c_ref, o_ref in zip(refs[:count], refs[count:]):
        tc = min(TILE, c_ref.shape[0])
        for j, part in enumerate(column_sums(r_ref, c_ref, 256)):
            o_ref[:, j * tc : (j + 1) * tc] = part


def first_sweep(scaled, pieces):
    return pl.pallas_call(
        first_kernel,
        out_shape=[pltpu.VMEM((1, p.shape[0]), F32) for p in pieces],
        compiler_params=params(8),
        cost_estimate=cost(scaled.shape[0], sum(p.shape[0] for p in pieces), 1),
        name="first_sweep",
    )(in_vmem(scaled), *[in_vmem(p) for p in pieces])


def last_kernel(off_ref, r_ref, *refs, n_new):
    pieces, ready, o_ref = refs[:n_new], refs[n_new:-1], refs[-1]
    parts = [ref[:, j : j + TILE] for ref in ready for j in range(0, ref.shape[1], TILE)]
    for c_ref in pieces:
        parts += column_sums(r_ref, c_ref, 256)
    for tile, part in enumerate(parts):
        for j in range(TILE // 128):
            o_ref[pl.ds(off_ref[tile] + j, 1), :] = part[:, j * 128 : (j + 1) * 128]


def last_sweep(offsets, scaled, pieces, ready):
    total = sum(p.shape[0] for p in pieces) + sum(p.shape[1] for p in ready)
    vmem = pl.BlockSpec(memory_space=pltpu.VMEM)
    return pl.pallas_call(
        functools.partial(last_kernel, n_new=len(pieces)),
        in_specs=[pl.BlockSpec(memory_space=pltpu.SMEM)] + [vmem] * (1 + len(pieces) + len(ready)),
        out_specs=vmem,
        out_shape=jax.ShapeDtypeStruct((total // 128, 128), F32),
        compiler_params=params(8),
        cost_estimate=cost(scaled.shape[0], sum(p.shape[0] for p in pieces), 1),
        name="last_sweep",
    )(offsets, *[in_vmem(p) for p in (scaled, *pieces, *ready)])


def lane_sum(x):
    parts = [x[:, j : j + 128] for j in range(0, x.shape[1], 128)]
    while len(parts) > 1:
        parts = [parts[i] + parts[i + 1] for i in range(0, len(parts), 2)]
    return parts[0]


def second_kernel(off_ref, r_ref, first_ref, in_ref, *refs, n_pieces, tr, rg, ratio):
    pieces = refs[:n_pieces]
    out_ref, score_ref, moved_ref, *scratch = refs[n_pieces:]
    b_scr, col_scr, e_scr, s_scr, u_scr, i_scr, c_scr, m_scr, sem, sems = scratch
    rows = r_ref.shape[0]
    copies = []
    at = 0
    for i, ref in enumerate(pieces):
        n = ref.shape[0]
        copies.append(pltpu.make_async_copy(ref, c_scr.at[at : at + n, :], sems.at[i]))
        copies[-1].start()
        at += n
    load = pltpu.make_async_copy(in_ref, m_scr, sem.at[0])
    load.start()
    store = pltpu.make_async_copy(m_scr, moved_ref, sem.at[1])
    tiles = range(0, c_scr.shape[0], TILE)
    n_own = pieces[0].shape[0] // TILE
    lanes = TILE // 128
    for i in range(len(tiles)):
        for j in range(lanes):
            at = (i * lanes + j) * 128
            b_scr[:, at : at + 128] = first_ref[pl.ds(off_ref[i] + j, 1), :]
    b_scr[...] = jnp.log2(ratio / b_scr[...])
    copies[0].wait()
    col_scr[...] = jnp.zeros_like(col_scr)
    width = 256

    def body(t, carry):
        r = r_ref[pl.ds(pl.multiple_of(t * tr, tr), tr), :]
        for i, j in enumerate(tiles):
            if i == n_own:

                @pl.when(t == 0)
                def _():
                    for piece in copies[1:]:
                        piece.wait()
                    load.wait()
                    store.start()

            here = slice(i * TILE, (i + 1) * TILE)
            p = lax.dot_general(r, c_scr[j : j + TILE, :], NT, preferred_element_type=F32)
            bias = b_scr[:, here]
            for g in range(0, tr, rg):
                part = p[g : g + rg]
                e = jnp.exp2(part + bias)
                e_scr[g : g + rg, here] = e.astype(BF16)
                q = e * part
                if i == 0:
                    s_scr[g : g + rg] = lane_sum(e)
                    u_scr[g : g + rg] = lane_sum(q)
                else:
                    s_scr[g : g + rg] += lane_sum(e)
                    u_scr[g : g + rg] += lane_sum(q)
        for g in range(0, tr, width):
            inverse = 1.0 / jnp.sum(s_scr[g : g + width].T, axis=0, keepdims=True)
            weighted = jnp.sum(u_scr[g : g + width].T, axis=0, keepdims=True)
            place = t * (tr // width) + g // width
            score_ref[pl.ds(place, 1), :] = weighted * inverse * (1.0 / LOG2E)
            high = inverse.astype(BF16)
            low = (inverse - high.astype(F32)).astype(BF16)
            i_scr[:, g : g + width] = jnp.concatenate(
                [high, low, jnp.zeros((14, width), BF16)], axis=0
            )
        for i in range(len(tiles)):
            here = slice(i * TILE, (i + 1) * TILE)
            part = lax.dot_general(i_scr[...], e_scr[:, here], NN, preferred_element_type=F32)
            col_scr[:, here] += part[0:8]
        return carry

    lax.fori_loop(0, rows // tr, body, 0)
    for i in range(len(tiles)):
        for j in range(lanes):
            at = (i * lanes + j) * 128
            line = jnp.sum(col_scr[:, at : at + 128], axis=0, keepdims=True)
            out_ref[pl.ds(off_ref[i] + j, 1), :] = line
    store.wait()


def second_sweep(offsets, scaled, first, arrived, pieces, ratio):
    rows = scaled.shape[0]
    total = sum(p.shape[0] for p in pieces)
    tr = ROW_TILE
    vmem = pl.BlockSpec(memory_space=pltpu.VMEM)
    any_space = pl.BlockSpec(memory_space=pl.ANY)
    return pl.pallas_call(
        functools.partial(second_kernel, n_pieces=len(pieces), tr=tr, rg=16, ratio=ratio),
        in_specs=[pl.BlockSpec(memory_space=pltpu.SMEM), vmem, vmem, any_space]
        + [any_space] * len(pieces),
        out_specs=[vmem, vmem, any_space],
        out_shape=[
            jax.ShapeDtypeStruct((total // 128, 128), F32),
            jax.ShapeDtypeStruct((rows // 256, 256), F32),
            pltpu.HBM(arrived.shape, BF16),
        ],
        scratch_shapes=[
            pltpu.VMEM((1, total), F32),
            pltpu.VMEM((8, total), F32),
            pltpu.VMEM((tr, total), BF16),
            pltpu.VMEM((tr, 128), F32),
            pltpu.VMEM((tr, 128), F32),
            pltpu.VMEM((16, tr), BF16),
            pltpu.VMEM((total, scaled.shape[1]), BF16),
            pltpu.VMEM(arrived.shape, BF16),
            pltpu.SemaphoreType.DMA((2,)),
            pltpu.SemaphoreType.DMA((len(pieces),)),
        ],
        compiler_params=params(26),
        cost_estimate=cost(rows, total, 3),
        name="second_sweep",
    )(offsets, in_vmem(scaled), first, in_hbm(arrived), *pieces)


def finish_kernel(place_ref, col_ref, last_ref, kept_ref, bal_ref, out_ref, buf, *, scale):
    lines = col_ref.shape[0]
    bal_ref[...] = (col_ref[...] + last_ref[:lines, :]) * scale
    z, y, k = place_ref[0], place_ref[1], place_ref[2]
    for dz in range(NZ):
        for dy in range(NY):
            at = dz * NY + dy
            to = (((z - dz) & (NZ - 1)) * NY + ((y - dy) & (NY - 1))) * NK
            buf[pl.ds(to + k, 1), :] = kept_ref[at : at + 1, :]
            buf[pl.ds(to + 1 - k, 1), :] = last_ref[lines + at : lines + at + 1, :]
    out_ref[...] = buf[...].astype(BF16)


def finish(place, column, last, kept, scale):
    peers = NZ * NY * NK
    vmem = pl.BlockSpec(memory_space=pltpu.VMEM)
    return pl.pallas_call(
        functools.partial(finish_kernel, scale=scale),
        in_specs=[pl.BlockSpec(memory_space=pltpu.SMEM), vmem, vmem, vmem],
        out_specs=[vmem, vmem],
        out_shape=[
            jax.ShapeDtypeStruct(column.shape, F32),
            jax.ShapeDtypeStruct((peers, 128), BF16),
        ],
        scratch_shapes=[pltpu.VMEM((peers, 128), F32)],
        compiler_params=params(8),
        name="finish",
    )(place, column, last, kept)


def all_sum(values, other):
    for name, perms in (
        ("cent", [x_perm(s) for s in (1, 3, 2)]),
        ("rows", [rows_perm(0, 0, 1)]),
        ("rows", [rows_perm(0, s, 0) for s in (1, 3, 2)]),
        ("rows", [rows_perm(s, 0, 0) for s in (1, 3, 2)]),
    ):
        arrived = [lax.ppermute(values, name, perm) for perm in perms]
        for part in arrived:
            values = values + part
    values, other = lax.optimization_barrier((values, other))
    return values, other


def local(embeddings, centroids, owners, live_blocks):
    x = lax.axis_index("cent")
    row_place = lax.axis_index("rows")
    k = row_place & (NK - 1)
    y = (row_place // NK) & (NY - 1)
    z = row_place // (NK * NY)
    n_cent, d = centroids.shape
    half = n_cent // NK
    rows = embeddings.shape[0]
    peers = NZ * NY * NK
    total = n_cent * NX

    place = jnp.stack([z, y, k]).astype(jnp.int32)
    own, mine = unit_cents(k.reshape(1).astype(jnp.int32), centroids)
    right = lax.ppermute(mine, "cent", x_perm(1))
    left = lax.ppermute(mine, "cent", x_perm(-1))
    embeddings, mine = lax.optimization_barrier((embeddings, mine))
    outgoing, scaled = unit_rows(owners, live_blocks, embeddings, peers)
    arrived = lax.all_to_all(outgoing, "rows", split_axis=0, concat_axis=0, tiled=True)
    right, left, scaled = lax.optimization_barrier((right, left, scaled))
    swap = rows_perm(0, 0, 1)
    far = [lax.ppermute(t, "cent", x_perm(s)) for t, s in zip(forward_parts(right, left), (1, -1))]
    right = [right, lax.ppermute(right, "rows", swap)]
    left = [left, lax.ppermute(left, "rows", swap)]
    sums_own = first_sweep(scaled, [own])
    sums_right = first_sweep(scaled, right)
    sums_left = first_sweep(scaled, left)
    far, sums_own, sums_right, sums_left = lax.optimization_barrier(
        (far, sums_own, sums_right, sums_left)
    )
    far += [lax.ppermute(t, "rows", swap) for t in far]

    def line(dx, kk, quarter):
        return (((x + dx) & (NX - 1)) * n_cent + kk * half + quarter * TILE) // 128

    starts = [line(0, q // 2, q % 2) for q in range(4)]
    for dx in (-1, 1, 2):
        starts += [line(dx, k, 0), line(dx, k, 1), line(dx, 1 - k, 0), line(dx, 1 - k, 1)]
    offsets = jnp.stack(starts).astype(jnp.int32)

    column = last_sweep(offsets, scaled, far, [*sums_own, *sums_right, *sums_left])
    column, arrived = all_sum(column, arrived)
    ratio = float(rows * NX * peers) / total
    pieces = [own, right[0], in_hbm(right[1]), left[0], in_hbm(left[1]), *far]
    column, score, moved = second_sweep(offsets, scaled, column, arrived, pieces, ratio)

    blocks = owners.shape[0]
    score = score.astype(BF16).astype(F32).reshape(blocks, BLOCK_ROWS)
    owner_z = (owners // (NK * NY) - z) & (NZ - 1)
    owner_y = (owners // NK - y) & (NY - 1)
    owner_k = (owners - k) & (NK - 1)
    relative = (owner_z * NY + owner_y) * NK + owner_k
    live = jnp.arange(blocks, dtype=jnp.int32) < live_blocks[0]
    hit = (relative[None, :] == jnp.arange(peers, dtype=jnp.int32)[:, None]) & live[None, :]
    sent = jnp.sum(jnp.where(hit[:, :, None], score[None], 0.0), axis=1)
    sent = sent.reshape(NZ, NY * NK, BLOCK_ROWS)
    lines = total // 128

    for part in [lax.ppermute(column, "cent", x_perm(s)) for s in (1, 3, 2)]:
        column = column + part
    both = [
        lax.ppermute(jnp.concatenate([column, sent[s]]), "rows", rows_perm(s, 0, 0))
        for s in (1, 3, 2)
    ]
    column = column + both[0][:lines] + both[1][:lines] + both[2][:lines]
    both = [both[0], both[2], both[1]]
    sent = jnp.stack([sent[0]] + [b[lines:] for b in both]).reshape(NZ, NY, NK, BLOCK_ROWS)
    both = [
        lax.ppermute(
            jnp.concatenate([column, sent[:, s].reshape(NZ * NK, BLOCK_ROWS)]),
            "rows",
            rows_perm(0, s, 0),
        )
        for s in (1, 3, 2)
    ]
    column = column + both[0][:lines] + both[1][:lines] + both[2][:lines]
    both = [both[0], both[2], both[1]]
    got = [b[lines:].reshape(NZ, NK, BLOCK_ROWS) for b in both]
    sent = jnp.stack([sent[:, 0], *got], axis=1)
    kept = sent[:, :, 0].reshape(NZ * NY, BLOCK_ROWS)
    given = sent[:, :, 1].reshape(NZ * NY, BLOCK_ROWS)
    last = lax.ppermute(jnp.concatenate([column, given]), "rows", swap)
    balance, moved_score = finish(place, column, last, kept, 1.0 / ratio)
    return moved.reshape(peers * BLOCK_ROWS, d), moved_score.reshape(-1), balance.reshape(-1)


def solution(mesh):
    placed = (P(("rows", "cent"), None), P("cent", None), P(("rows", "cent")), P(("rows", "cent")))
    return jax.shard_map(
        local,
        mesh=mesh,
        in_specs=placed,
        out_specs=(P(("rows", "cent"), None), P(("rows", "cent")), P()),
        check_vma=False,
    )
```

time: 153 us -> 114 us (0.75)
  waiting for transfers between devices: 51.6 us -> 19.8 us
  local copies, waits for them, and re-layouts: 8.51 us -> 0.21 us
  Pallas kernels: 36.2 us -> 39.8 us
  other arithmetic: 3.05 us -> 1.14 us
    ppermute x10, waiting for transfers between devices: 27.5 us -> 8.36 us  [all_sum(): arrived = [lax.ppermute(values, name, perm) for perm in perms]]
    ppermute x1, waiting for transfers between devices: 11.1 us -> 0.01 us  [local(): right = lax.ppermute(mine, 'cent', x_perm(1))]
    unnamed x14 -> x11, local copies, waits for them, and re-layouts: 8.25 us -> 0.04 us
    ppermute x13, waiting for transfers between devices: 11.3 us -> 7.3 us  [the longest x3 2.97 us: local(): lax.ppermute(column, 'cent', x_perm(s))]
    ppermute x3, waiting for transfers between devices: 1.71 us -> 4.08 us  [local(): lax.ppermute(jnp.concatenate([column, sent[s]]), 'rows', rows_perm(s, 0, 0))]
    reduce_sum x2 -> x0, other arithmetic: 1.84 us -> none  [the longest x1 1.01 us: local(): column = jnp.sum(column, axis=0)]
    pallas_call x4 -> x6, Pallas kernels: 9.71 us -> 10.9 us  [the longest x3 7.15 us: first_sweep(): pl.pallas_call(first_kernel, out_shape=[pltpu.VMEM((1, p.shape[0]), F32)...]
  transfers between devices with their start and end apart: 29 -> 29, of which waited for: 17 -> 14; matrix products, arithmetic and copies ran while one was open for 2% -> 1% of each run, Pallas kernels for 21% -> 12%
where the time goes in v2:
time: 114 us
  starting transfers between devices  51.6 us (45%)
  Pallas kernels  39.8 us (35%)
  waiting for transfers between devices  19.8 us (17%)
  between operations  1.64 us (1%)
    pallas_call x1, Pallas kernels, second_sweep(): pl.pallas_call(functools.partial(second_kernel, n_pieces=len(pieces), tr=...  22.5 us
    ppermute x10, starting transfers between devices, all_sum(): arrived = [lax.ppermute(values, name, perm) for perm in perms]  15 us
    all_to_all x1, starting transfers between devices, local(): lax.all_to_all(outgoing, 'rows', split_axis=0, concat_axis=0, tiled=True)  9.51 us
    ppermute x10, waiting for transfers between devices, all_sum(): arrived = [lax.ppermute(values, name, perm) for perm in perms]  8.36 us
    ppermute x1, starting transfers between devices, local(): last = lax.ppermute(jnp.concatenate([column, given]), 'rows', swap)  8.12 us
    pallas_call x3, Pallas kernels, first_sweep(): pl.pallas_call(first_kernel, out_shape=[pltpu.VMEM((1, p.shape[0]), F32)...  7.15 us
    ppermute x3, starting transfers between devices, local(): lax.ppermute(column, 'cent', x_perm(s))  4.32 us
    ppermute x3, waiting for transfers between devices, local(): lax.ppermute(jnp.concatenate([column, sent[s]]), 'rows', rows_perm(s, 0, 0))  4.08 us
  transfers between devices with their start and end apart: 29, of which 14 were waited for; matrix products, arithmetic and copies ran while one was open for 1% of the time, Pallas kernels for 12%

profile of v2, /device:TPU:1, one launch (start us, length us, event | category | flops | bytes accessed | tf_op | source)
XLA Modules:
  0.0 114.1 jit_solution(9918180880458598389)
XLA Ops:
  0.7 2.5 %unit_cents.1 = (bf16[2048,256]{1,0:T(8,128)(2,1)S(1)}, bf16[1024,256]{1,0:T(8,128)(2,1)}) custom-call(s32[1]{0:T(128)} %bitcast.16.place_ref, f32[2048,256]{1,0:T(8,128)} %c_ref.1), custom_call_target="tpu_custom_call" | custom-call | tf_op jit(solution)/shard_map/unit_cents/pallas_call | solution.py:79
  3.2 2.1 %collective-permute-start = (bf16[1024,256]{1,0:T(8,128)(2,1)}, bf16[1024,256]{1,0:T(8,128)(2,1)S(1)}, u32[]{:S(2)}, u32[]{:S(2)}) collective-permute-start(bf16[1024,256]{1,0:T(8,128)(2,1)} %get-tuple-element.31), channel_id=1, source_target_pairs={{0,1},{1,2},{2,3},{3,0},{4,5},{5,6},{6,7},{7,4},{8,9},{9,10},{10,1... | collective-permute-start | bytes 1572872 | tf_op jit(solution)/shard_map/ppermute | solution.py:382
  7.3 2.8 %unit_rows.1 = (bf16[32,128,256]{2,1,0:T(8,128)(2,1)}, bf16[2048,256]{1,0:T(8,128)(2,1)S(1)}) custom-call(s32[16]{0:T(128)S(1)} %copy-done.3, s32[1]{0:T(128)} %copy.34.live_ref, f32[2048,256]{1,0:T(8,128)S(1)} %copy-done), custom_call_target="tpu_custom_call" | custom-call | tf_op jit(solution)/shard_map/unit_rows/pallas_call | solution.py:132
  10.1 9.5 %all-to-all-start = ((bf16[32,128,256]{2,1,0:T(8,128)(2,1)}), bf16[32,128,256]{2,1,0:T(8,128)(2,1)}, u32[]{:S(2)}, u32[]{:S(2)}) async-start(bf16[32,128,256]{2,1,0:T(8,128)(2,1)} %get-tuple-element.51), calls=%async_computation | async-start | bytes 4194304 | tf_op jit(solution)/shard_map/all_to_all | solution.py:386
  21.2 1.9 %collective-permute-start.3 = (bf16[512,256]{1,0:T(8,128)(2,1)S(1)}, bf16[512,256]{1,0:T(8,128)(2,1)}, u32[]{:S(2)}, u32[]{:S(2)}) collective-permute-start(bf16[512,256]{1,0:T(8,128)(2,1)S(1)} %get-tuple-element.38), channel_id=1, source_target_pairs={{0,3},{1,0},{2,1},{3,2},{4,7},{5,4},{6,5},{7,6},{8,11},{9,8},{10,9... | collective-permute-start | bytes 786440 | tf_op jit(solution)/shard_map/ppermute | solution.py:389
  23.1 2.4 %first_sweep.3.refs_4_ = f32[1,2048]{1,0:T(1,128)S(1)} custom-call(bf16[2048,256]{1,0:T(8,128)(2,1)S(1)} %get-tuple-element.34.r_ref, bf16[2048,256]{1,0:T(8,128)(2,1)S(1)} %get-tuple-element.39.refs_0_), custom_call_target="tpu_custom_call" | custom-call | flops 2048 | bytes 2048 | tf_op jit(solution)/shard_map/first_sweep/pallas_call | solution.py:172
  25.5 2.4 %first_sweep.5 = (f32[1,1024]{1,0:T(1,128)S(1)}, f32[1,1024]{1,0:T(1,128)S(1)}) custom-call(bf16[2048,256]{1,0:T(8,128)(2,1)S(1)} %get-tuple-element.34.r_ref, bf16[1024,256]{1,0:T(8,128)(2,1)S(1)} %collective-permute-done.1.left_ref.refs_0_.refs_3_, bf16[1024,256]{1,0:T(8,128)(2,1)S(1)} %collective-permute-done.5.refs_1_.refs_4_), custom_call_target="tpu_custom_call" | custom-call | flops 2048 | bytes 2048 | tf_op jit(solution)/shard_map/first_sweep/pallas_call | solution.py:172
  27.9 2.4 %first_sweep.4 = (f32[1,1024]{1,0:T(1,128)S(1)}, f32[1,1024]{1,0:T(1,128)S(1)}) custom-call(bf16[2048,256]{1,0:T(8,128)(2,1)S(1)} %get-tuple-element.34.r_ref, bf16[1024,256]{1,0:T(8,128)(2,1)S(1)} %collective-permute-done.right_ref.refs_0_.refs_1_, bf16[1024,256]{1,0:T(8,128)(2,1)S(1)} %collective-permute-done.4.refs_1_.refs_2_), custom_call_target="tpu_custom_call" | custom-call | flops 2048 | bytes 2048 | tf_op jit(solution)/shard_map/first_sweep/pallas_call | solution.py:172
  33.1 3.5 %last_sweep.1 = f32[64,128]{1,0:T(8,128)S(1)} custom-call(s32[16]{0:T(128)S(1)} %stack.94.off_ref, bf16[2048,256]{1,0:T(8,128)(2,1)S(1)} %get-tuple-element.34.r_ref, bf16[512,256]{1,0:T(8,128)(2,1)S(1)} %collective-permute-done.2.refs_0_.refs_5_, bf16[512,256]{1,0:T(8,128)(2,1)} %collective-permute-done.3.refs_1_.refs_6_, ...), custom_call_target="tpu_custom_call" | custom-call | flops 2048 | bytes 2048 | tf_op jit(solution)/shard_map/last_sweep/pallas_call | solution.py:194
  39.1 1.5 %collective-permute-start.9 = (f32[64,128]{1,0:T(8,128)S(1)}, f32[64,128]{1,0:T(8,128)}, u32[]{:S(2)}, u32[]{:S(2)}) collective-permute-start(f32[64,128]{1,0:T(8,128)S(1)} %last_sweep.1), channel_id=1, source_target_pairs={{0,3},{1,0},{2,1},{3,2},{4,7},{5,4},{6,5},{7,6},{8,11},{9,8},{10,9... | collective-permute-start | bytes 98312 | tf_op jit(solution)/shard_map/ppermute | solution.py:361
  43.3 1.6 %collective-permute-start.11 = (f32[64,128]{1,0:T(8,128)S(1)}, f32[64,128]{1,0:T(8,128)S(1)}, u32[]{:S(2)}, u32[]{:S(2)}) collective-permute-start(f32[64,128]{1,0:T(8,128)S(1)} %add_add_fusion.3), channel_id=1, source_target_pairs={{0,4},{4,0},{8,12},{12,8},{16,20},{20,16},{24,28},{28,24},{32,36},... | collective-permute-start | bytes 98312 | tf_op jit(solution)/shard_map/ppermute | solution.py:361
  45.8 1.4 %collective-permute-start.12 = (f32[64,128]{1,0:T(8,128)S(1)}, f32[64,128]{1,0:T(8,128)S(1)}, u32[]{:S(2)}, u32[]{:S(2)}) collective-permute-start(f32[64,128]{1,0:T(8,128)S(1)} %add.176), channel_id=1, source_target_pairs={{0,8},{4,12},{8,16},{12,20},{16,24},{20,28},{24,0},{28,4},{32,40},... | collective-permute-start | bytes 98312 | tf_op jit(solution)/shard_map/ppermute | solution.py:361
  48.5 1.7 %collective-permute-start.14 = (f32[64,128]{1,0:T(8,128)S(1)}, f32[64,128]{1,0:T(8,128)S(1)}, u32[]{:S(2)}, u32[]{:S(2)}) collective-permute-start(f32[64,128]{1,0:T(8,128)S(1)} %add.176), channel_id=1, source_target_pairs={{0,16},{4,20},{8,24},{12,28},{16,0},{20,4},{24,8},{28,12},{32,48},... | collective-permute-start | bytes 98312 | tf_op jit(solution)/shard_map/ppermute | solution.py:361
  50.2 2.6 %collective-permute-done.14 = f32[64,128]{1,0:T(8,128)S(1)} collective-permute-done((f32[64,128]{1,0:T(8,128)S(1)}, f32[64,128]{1,0:T(8,128)S(1)}, u32[]{:S(2)}, u32[]{:S(2)}) %collective-permute-start.14) | collective-permute-done | bytes 32800 | tf_op jit(solution)/shard_map/ppermute | solution.py:361
  52.8 1.6 %collective-permute-start.15 = (f32[64,128]{1,0:T(8,128)S(1)}, f32[64,128]{1,0:T(8,128)S(1)}, u32[]{:S(2)}, u32[]{:S(2)}) collective-permute-start(f32[64,128]{1,0:T(8,128)S(1)} %add_add_fusion.2), channel_id=1, source_target_pairs={{0,32},{4,36},{8,40},{12,44},{16,48},{20,52},{24,56},{28,60},{32,6... | collective-permute-start | bytes 98312 | tf_op jit(solution)/shard_map/ppermute | solution.py:361
  54.4 2.2 %collective-permute-start.16 = (f32[64,128]{1,0:T(8,128)S(1)}, f32[64,128]{1,0:T(8,128)S(1)}, u32[]{:S(2)}, u32[]{:S(2)}) collective-permute-start(f32[64,128]{1,0:T(8,128)S(1)} %add_add_fusion.2), channel_id=1, source_target_pairs={{0,96},{4,100},{8,104},{12,108},{16,112},{20,116},{24,120},{28,124... | collective-permute-start | bytes 98312 | tf_op jit(solution)/shard_map/ppermute | solution.py:361
  57.8 3.0 %collective-permute-done.17 = f32[64,128]{1,0:T(8,128)S(1)} collective-permute-done((f32[64,128]{1,0:T(8,128)S(1)}, f32[64,128]{1,0:T(8,128)S(1)}, u32[]{:S(2)}, u32[]{:S(2)}) %collective-permute-start.17) | collective-permute-done | bytes 32800 | tf_op jit(solution)/shard_map/ppermute | solution.py:361
  60.9 22.5 %second_sweep.1 = (f32[64,128]{1,0:T(8,128)S(1)}, f32[8,256]{1,0:T(8,128)S(1)}, bf16[32,128,256]{2,1,0:T(8,128)(2,1)}) custom-call(s32[16]{0:T(128)S(1)} %stack.94.off_ref, bf16[2048,256]{1,0:T(8,128)(2,1)S(1)} %get-tuple-element.34.r_ref, f32[64,128]{1,0:T(8,128)S(1)} %add_add_fusion.1.first_ref, bf16[32,128,256]{2,1,0:T(8,128)(2,1)} %all-to-all-done.in_ref, ...), custom_call_target="tpu_custom_call" | custom-call | flops 6144 | bytes 8192 | tf_op jit(solution)/shard_map/second_sweep/pallas_call | solution.py:296
  83.7 3.0 %collective-permute-start.19 = (f32[64,128]{1,0:T(8,128)S(1)}, f32[64,128]{1,0:T(8,128)S(1)}, u32[]{:S(2)}, u32[]{:S(2)}) collective-permute-start(f32[64,128]{1,0:T(8,128)S(1)} %get-tuple-element.55), channel_id=1, source_target_pairs={{0,3},{1,0},{2,1},{3,2},{4,7},{5,4},{6,5},{7,6},{8,11},{9,8},{10,9... | collective-permute-start | bytes 98312 | tf_op jit(solution)/shard_map/ppermute | solution.py:426
  87.9 3.0 %collective-permute-done.20 = f32[64,128]{1,0:T(8,128)S(1)} collective-permute-done((f32[64,128]{1,0:T(8,128)S(1)}, f32[64,128]{1,0:T(8,128)S(1)}, u32[]{:S(2)}, u32[]{:S(2)}) %collective-permute-start.20) | collective-permute-done | bytes 32800 | tf_op jit(solution)/shard_map/ppermute | solution.py:426
  91.0 2.7 %collective-permute-start.22 = (f32[72,128]{1,0:T(8,128)S(1)}, f32[72,128]{1,0:T(8,128)S(1)}, u32[]{:S(2)}, u32[]{:S(2)}) collective-permute-start(f32[72,128]{1,0:T(8,128)S(1)} %get-tuple-element.62), channel_id=1, source_target_pairs={{0,96},{4,100},{8,104},{12,108},{16,112},{20,116},{24,120},{28,124... | collective-permute-start | bytes 110600 | tf_op jit(solution)/shard_map/ppermute | solution.py:429
  95.3 2.7 %collective-permute-done.23 = f32[72,128]{1,0:T(8,128)S(1)} collective-permute-done((f32[72,128]{1,0:T(8,128)S(1)}, f32[72,128]{1,0:T(8,128)S(1)}, u32[]{:S(2)}, u32[]{:S(2)}) %collective-permute-start.23) | collective-permute-done | bytes 36896 | tf_op jit(solution)/shard_map/ppermute | solution.py:429
  98.4 2.4 %collective-permute-start.26 = (f32[72,128]{1,0:T(8,128)S(1)}, f32[72,128]{1,0:T(8,128)S(1)}, u32[]{:S(2)}, u32[]{:S(2)}) collective-permute-start(f32[72,128]{1,0:T(8,128)S(1)} %get-tuple-element.61), channel_id=1, source_target_pairs={{0,16},{4,20},{8,24},{12,28},{16,0},{20,4},{24,8},{28,12},{32,48},... | collective-permute-start | bytes 110600 | tf_op jit(solution)/shard_map/ppermute | solution.py:436
  103.9 8.1 %collective-permute-start.27 = (f32[80,128]{1,0:T(8,128)S(1)}, f32[80,128]{1,0:T(8,128)S(1)}, u32[]{:S(2)}, u32[]{:S(2)}) collective-permute-start(f32[80,128]{1,0:T(8,128)S(1)} %pad_maximum_fusion), channel_id=1, source_target_pairs={{0,4},{4,0},{8,12},{12,8},{16,20},{20,16},{24,28},{28,24},{32,36},... | collective-permute-start | bytes 122888 | tf_op jit(solution)/shard_map/ppermute | solution.py:449
  (89 shorter events, 23.0 us)
Async XLA Ops:
  3.2 16.5 %collective-permute-start = (bf16[1024,256]{1,0:T(8,128)(2,1)}, bf16[1024,256]{1,0:T(8,128)(2,1)S(1)}, u32[]{:S(2)}, u32[]{:S(2)}) collective-permute-start(bf16[1024,256]{1,0:T(8,128)(2,1)} %get-tuple-element.31), channel_id=1, source_target_pairs={{0,1},{1,2},{2,3},{3,0},{4,5},{5,6},{6,7},{7,4},{8,9},{9,10},{10,1... | collective-permute-start | bytes 1572872 | tf_op jit(solution)/shard_map/ppermute | solution.py:382
  5.3 14.4 %collective-permute-start.1 = (bf16[1024,256]{1,0:T(8,128)(2,1)}, bf16[1024,256]{1,0:T(8,128)(2,1)S(1)}, u32[]{:S(2)}, u32[]{:S(2)}) collective-permute-start(bf16[1024,256]{1,0:T(8,128)(2,1)} %get-tuple-element.31), channel_id=1, source_target_pairs={{0,3},{1,0},{2,1},{3,2},{4,7},{5,4},{6,5},{7,6},{8,11},{9,8},{10,9... | collective-permute-start | bytes 1572872 | tf_op jit(solution)/shard_map/ppermute | solution.py:383
  10.1 50.7 %all-to-all-start = ((bf16[32,128,256]{2,1,0:T(8,128)(2,1)}), bf16[32,128,256]{2,1,0:T(8,128)(2,1)}, u32[]{:S(2)}, u32[]{:S(2)}) async-start(bf16[32,128,256]{2,1,0:T(8,128)(2,1)} %get-tuple-element.51), calls=%async_computation | async-start | bytes 4194304 | tf_op jit(solution)/shard_map/all_to_all | solution.py:386
  19.7 5.8 %collective-permute-start.5 = (bf16[1024,256]{1,0:T(8,128)(2,1)S(1)}, bf16[1024,256]{1,0:T(8,128)(2,1)S(1)}, u32[]{:S(2)}, u32[]{:S(2)}) collective-permute-start(bf16[1024,256]{1,0:T(8,128)(2,1)S(1)} %collective-permute-done.1.left_ref.refs_0_.refs_3_), channel_id=1, source_target_pairs={{0,4},{4,0},{8,12},{12,8},{16,20},{20,16},{24,28},{28,24},{32,36},... | collective-permute-start | bytes 1572872 | tf_op jit(solution)/shard_map/ppermute | solution.py:391
  20.1 7.8 %collective-permute-start.4 = (bf16[1024,256]{1,0:T(8,128)(2,1)S(1)}, bf16[1024,256]{1,0:T(8,128)(2,1)S(1)}, u32[]{:S(2)}, u32[]{:S(2)}) collective-permute-start(bf16[1024,256]{1,0:T(8,128)(2,1)S(1)} %collective-permute-done.right_ref.refs_0_.refs_1_), channel_id=1, source_target_pairs={{0,4},{4,0},{8,12},{12,8},{16,20},{20,16},{24,28},{28,24},{32,36},... | collective-permute-start | bytes 1572872 | tf_op jit(solution)/shard_map/ppermute | solution.py:390
  20.3 10.0 %collective-permute-start.2 = (bf16[512,256]{1,0:T(8,128)(2,1)S(1)}, bf16[512,256]{1,0:T(8,128)(2,1)S(1)}, u32[]{:S(2)}, u32[]{:S(2)}) collective-permute-start(bf16[512,256]{1,0:T(8,128)(2,1)S(1)} %get-tuple-element.37), channel_id=1, source_target_pairs={{0,1},{1,2},{2,3},{3,0},{4,5},{5,6},{6,7},{7,4},{8,9},{9,10},{10,1... | collective-permute-start | bytes 786440 | tf_op jit(solution)/shard_map/ppermute | solution.py:389
  21.2 9.1 %collective-permute-start.3 = (bf16[512,256]{1,0:T(8,128)(2,1)S(1)}, bf16[512,256]{1,0:T(8,128)(2,1)}, u32[]{:S(2)}, u32[]{:S(2)}) collective-permute-start(bf16[512,256]{1,0:T(8,128)(2,1)S(1)} %get-tuple-element.38), channel_id=1, source_target_pairs={{0,3},{1,0},{2,1},{3,2},{4,7},{5,4},{6,5},{7,6},{8,11},{9,8},{10,9... | collective-permute-start | bytes 786440 | tf_op jit(solution)/shard_map/ppermute | solution.py:389
  36.6 4.7 %collective-permute-start.10 = (f32[64,128]{1,0:T(8,128)S(1)}, f32[64,128]{1,0:T(8,128)S(1)}, u32[]{:S(2)}, u32[]{:S(2)}) collective-permute-start(f32[64,128]{1,0:T(8,128)S(1)} %last_sweep.1), channel_id=1, source_target_pairs={{0,2},{1,3},{2,0},{3,1},{4,6},{5,7},{6,4},{7,5},{8,10},{9,11},{10,... | collective-permute-start | bytes 98312 | tf_op jit(solution)/shard_map/ppermute | solution.py:361
  38.0 4.6 %collective-permute-start.8 = (f32[64,128]{1,0:T(8,128)S(1)}, f32[64,128]{1,0:T(8,128)S(1)}, u32[]{:S(2)}, u32[]{:S(2)}) collective-permute-start(f32[64,128]{1,0:T(8,128)S(1)} %last_sweep.1), channel_id=1, source_target_pairs={{0,1},{1,2},{2,3},{3,0},{4,5},{5,6},{6,7},{7,4},{8,9},{9,10},{10,1... | collective-permute-start | bytes 98312 | tf_op jit(solution)/shard_map/ppermute | solution.py:361
  39.1 3.4 %collective-permute-start.9 = (f32[64,128]{1,0:T(8,128)S(1)}, f32[64,128]{1,0:T(8,128)}, u32[]{:S(2)}, u32[]{:S(2)}) collective-permute-start(f32[64,128]{1,0:T(8,128)S(1)} %last_sweep.1), channel_id=1, source_target_pairs={{0,3},{1,0},{2,1},{3,2},{4,7},{5,4},{6,5},{7,6},{8,11},{9,8},{10,9... | collective-permute-start | bytes 98312 | tf_op jit(solution)/shard_map/ppermute | solution.py:361
  45.8 4.4 %collective-permute-start.12 = (f32[64,128]{1,0:T(8,128)S(1)}, f32[64,128]{1,0:T(8,128)S(1)}, u32[]{:S(2)}, u32[]{:S(2)}) collective-permute-start(f32[64,128]{1,0:T(8,128)S(1)} %add.176), channel_id=1, source_target_pairs={{0,8},{4,12},{8,16},{12,20},{16,24},{20,28},{24,0},{28,4},{32,40},... | collective-permute-start | bytes 98312 | tf_op jit(solution)/shard_map/ppermute | solution.py:361
  48.5 4.3 %collective-permute-start.14 = (f32[64,128]{1,0:T(8,128)S(1)}, f32[64,128]{1,0:T(8,128)S(1)}, u32[]{:S(2)}, u32[]{:S(2)}) collective-permute-start(f32[64,128]{1,0:T(8,128)S(1)} %add.176), channel_id=1, source_target_pairs={{0,16},{4,20},{8,24},{12,28},{16,0},{20,4},{24,8},{28,12},{32,48},... | collective-permute-start | bytes 98312 | tf_op jit(solution)/shard_map/ppermute | solution.py:361
  52.8 5.1 %collective-permute-start.15 = (f32[64,128]{1,0:T(8,128)S(1)}, f32[64,128]{1,0:T(8,128)S(1)}, u32[]{:S(2)}, u32[]{:S(2)}) collective-permute-start(f32[64,128]{1,0:T(8,128)S(1)} %add_add_fusion.2), channel_id=1, source_target_pairs={{0,32},{4,36},{8,40},{12,44},{16,48},{20,52},{24,56},{28,60},{32,6... | collective-permute-start | bytes 98312 | tf_op jit(solution)/shard_map/ppermute | solution.py:361
  54.4 3.4 %collective-permute-start.16 = (f32[64,128]{1,0:T(8,128)S(1)}, f32[64,128]{1,0:T(8,128)S(1)}, u32[]{:S(2)}, u32[]{:S(2)}) collective-permute-start(f32[64,128]{1,0:T(8,128)S(1)} %add_add_fusion.2), channel_id=1, source_target_pairs={{0,96},{4,100},{8,104},{12,108},{16,112},{20,116},{24,120},{28,124... | collective-permute-start | bytes 98312 | tf_op jit(solution)/shard_map/ppermute | solution.py:361
  56.6 4.3 %collective-permute-start.17 = (f32[64,128]{1,0:T(8,128)S(1)}, f32[64,128]{1,0:T(8,128)S(1)}, u32[]{:S(2)}, u32[]{:S(2)}) collective-permute-start(f32[64,128]{1,0:T(8,128)S(1)} %add_add_fusion.2), channel_id=1, source_target_pairs={{0,64},{4,68},{8,72},{12,76},{16,80},{20,84},{24,88},{28,92},{32,9... | collective-permute-start | bytes 98312 | tf_op jit(solution)/shard_map/ppermute | solution.py:361
  83.4 4.5 %collective-permute-start.18 = (f32[64,128]{1,0:T(8,128)S(1)}, f32[64,128]{1,0:T(8,128)S(1)}, u32[]{:S(2)}, u32[]{:S(2)}) collective-permute-start(f32[64,128]{1,0:T(8,128)S(1)} %get-tuple-element.55), channel_id=1, source_target_pairs={{0,1},{1,2},{2,3},{3,0},{4,5},{5,6},{6,7},{7,4},{8,9},{9,10},{10,1... | collective-permute-start | bytes 98312 | tf_op jit(solution)/shard_map/ppermute | solution.py:426
  83.7 4.3 %collective-permute-start.19 = (f32[64,128]{1,0:T(8,128)S(1)}, f32[64,128]{1,0:T(8,128)S(1)}, u32[]{:S(2)}, u32[]{:S(2)}) collective-permute-start(f32[64,128]{1,0:T(8,128)S(1)} %get-tuple-element.55), channel_id=1, source_target_pairs={{0,3},{1,0},{2,1},{3,2},{4,7},{5,4},{6,5},{7,6},{8,11},{9,8},{10,9... | collective-permute-start | bytes 98312 | tf_op jit(solution)/shard_map/ppermute | solution.py:426
  86.6 4.3 %collective-permute-start.20 = (f32[64,128]{1,0:T(8,128)S(1)}, f32[64,128]{1,0:T(8,128)S(1)}, u32[]{:S(2)}, u32[]{:S(2)}) collective-permute-start(f32[64,128]{1,0:T(8,128)S(1)} %get-tuple-element.55), channel_id=1, source_target_pairs={{0,2},{1,3},{2,0},{3,1},{4,6},{5,7},{6,4},{7,5},{8,10},{9,11},{10,... | collective-permute-start | bytes 98312 | tf_op jit(solution)/shard_map/ppermute | solution.py:426
  90.9 4.3 %collective-permute-start.21 = (f32[72,128]{1,0:T(8,128)S(1)}, f32[72,128]{1,0:T(8,128)S(1)}, u32[]{:S(2)}, u32[]{:S(2)}) collective-permute-start(f32[72,128]{1,0:T(8,128)S(1)} %get-tuple-element.64), channel_id=1, source_target_pairs={{0,32},{4,36},{8,40},{12,44},{16,48},{20,52},{24,56},{28,60},{32,6... | collective-permute-start | bytes 110600 | tf_op jit(solution)/shard_map/ppermute | solution.py:429
  91.0 7.0 %collective-permute-start.22 = (f32[72,128]{1,0:T(8,128)S(1)}, f32[72,128]{1,0:T(8,128)S(1)}, u32[]{:S(2)}, u32[]{:S(2)}) collective-permute-start(f32[72,128]{1,0:T(8,128)S(1)} %get-tuple-element.62), channel_id=1, source_target_pairs={{0,96},{4,100},{8,104},{12,108},{16,112},{20,116},{24,120},{28,124... | collective-permute-start | bytes 110600 | tf_op jit(solution)/shard_map/ppermute | solution.py:429
  93.7 4.3 %collective-permute-start.23 = (f32[72,128]{1,0:T(8,128)S(1)}, f32[72,128]{1,0:T(8,128)S(1)}, u32[]{:S(2)}, u32[]{:S(2)}) collective-permute-start(f32[72,128]{1,0:T(8,128)S(1)} %get-tuple-element.63), channel_id=1, source_target_pairs={{0,64},{4,68},{8,72},{12,76},{16,80},{20,84},{24,88},{28,92},{32,9... | collective-permute-start | bytes 110600 | tf_op jit(solution)/shard_map/ppermute | solution.py:429
  98.1 4.1 %collective-permute-start.24 = (f32[72,128]{1,0:T(8,128)S(1)}, f32[72,128]{1,0:T(8,128)S(1)}, u32[]{:S(2)}, u32[]{:S(2)}) collective-permute-start(f32[72,128]{1,0:T(8,128)S(1)} %get-tuple-element.59), channel_id=1, source_target_pairs={{0,8},{4,12},{8,16},{12,20},{16,24},{20,28},{24,0},{28,4},{32,40},... | collective-permute-start | bytes 110600 | tf_op jit(solution)/shard_map/ppermute | solution.py:436
  98.4 4.3 %collective-permute-start.26 = (f32[72,128]{1,0:T(8,128)S(1)}, f32[72,128]{1,0:T(8,128)S(1)}, u32[]{:S(2)}, u32[]{:S(2)}) collective-permute-start(f32[72,128]{1,0:T(8,128)S(1)} %get-tuple-element.61), channel_id=1, source_target_pairs={{0,16},{4,20},{8,24},{12,28},{16,0},{20,4},{24,8},{28,12},{32,48},... | collective-permute-start | bytes 110600 | tf_op jit(solution)/shard_map/ppermute | solution.py:436
  103.9 9.0 %collective-permute-start.27 = (f32[80,128]{1,0:T(8,128)S(1)}, f32[80,128]{1,0:T(8,128)S(1)}, u32[]{:S(2)}, u32[]{:S(2)}) collective-permute-start(f32[80,128]{1,0:T(8,128)S(1)} %pad_maximum_fusion), channel_id=1, source_target_pairs={{0,4},{4,0},{8,12},{12,8},{16,20},{20,16},{24,28},{28,24},{32,36},... | collective-permute-start | bytes 122888 | tf_op jit(solution)/shard_map/ppermute | solution.py:449
  (9 other events, 33.2 us)

commit v3 on v2

--- a/solution.py
+++ b/solution.py
@@ -87,6 +87,22 @@
     )(place, in_hbm(centroids))
 
 
+def sum_kernel(in_ref, out_ref):
+    total = in_ref[0]
+    for i in range(1, in_ref.shape[0]):
+        total = total + in_ref[i]
+    out_ref[...] = total
+
+
+def sum_blocks(blocks):
+    return pl.pallas_call(
+        sum_kernel,
+        out_shape=pltpu.VMEM(blocks.shape[1:], F32),
+        compiler_params=params(4),
+        name="sum_blocks",
+    )(in_vmem(blocks))
+
+
 def forward_kernel(right_ref, left_ref, first_ref, second_ref):
     n = first_ref.shape[0]
     first_ref[...] = right_ref[:n, :]
@@ -179,23 +195,28 @@
 
 
 def last_kernel(off_ref, r_ref, *refs, n_new):
-    pieces, ready, o_ref = refs[:n_new], refs[n_new:-1], refs[-1]
+    pieces, ready, (keep_ref, give_ref, buf) = refs[:n_new], refs[n_new:-3], refs[-3:]
     parts = [ref[:, j : j + TILE] for ref in ready for j in range(0, ref.shape[1], TILE)]
     for c_ref in pieces:
         parts += column_sums(r_ref, c_ref, 256)
     for tile, part in enumerate(parts):
         for j in range(TILE // 128):
-            o_ref[pl.ds(off_ref[tile] + j, 1), :] = part[:, j * 128 : (j + 1) * 128]
+            buf[pl.ds(off_ref[tile] + j, 1), :] = part[:, j * 128 : (j + 1) * 128]
+    half = keep_ref.shape[0]
+    keep_ref[...] = buf[:half, :]
+    give_ref[...] = buf[half:, :]
 
 
 def last_sweep(offsets, scaled, pieces, ready):
     total = sum(p.shape[0] for p in pieces) + sum(p.shape[1] for p in ready)
     vmem = pl.BlockSpec(memory_space=pltpu.VMEM)
+    half = total // 128 // NK
     return pl.pallas_call(
         functools.partial(last_kernel, n_new=len(pieces)),
         in_specs=[pl.BlockSpec(memory_space=pltpu.SMEM)] + [vmem] * (1 + len(pieces) + len(ready)),
-        out_specs=vmem,
-        out_shape=jax.ShapeDtypeStruct((total // 128, 128), F32),
+        out_specs=[vmem, vmem],
+        out_shape=[pltpu.VMEM((half, 128), F32)] * 2,
+        scratch_shapes=[pltpu.VMEM((NK * half, 128), F32)],
         compiler_params=params(8),
         cost_estimate=cost(scaled.shape[0], sum(p.shape[0] for p in pieces), 1),
         name="last_sweep",
@@ -209,10 +230,12 @@
     return parts[0]
 
 
-def second_kernel(off_ref, r_ref, first_ref, in_ref, *refs, n_pieces, tr, rg, ratio):
+def second_kernel(
+    off_ref, to_ref, live_ref, r_ref, mine_ref, other_ref, in_ref, *refs, n_pieces, tr, rg, ratio
+):
     pieces = refs[:n_pieces]
-    out_ref, score_ref, moved_ref, *scratch = refs[n_pieces:]
-    b_scr, col_scr, e_scr, s_scr, u_scr, i_scr, c_scr, m_scr, sem, sems = scratch
+    keep_ref, sent_ref, give_ref, moved_ref, *scratch = refs[n_pieces:]
+    line_scr, score_scr, b_scr, col_scr, e_scr, s_scr, u_scr, i_scr, c_scr, m_scr, sem, sems = scratch
     rows = r_ref.shape[0]
     copies = []
     at = 0
@@ -227,11 +250,13 @@
     tiles = range(0, c_scr.shape[0], TILE)
     n_own = pieces[0].shape[0] // TILE
     lanes = TILE // 128
+    half = mine_ref.shape[0]
+    line_scr[:half, :] = jnp.log2(ratio / mine_ref[...])
+    line_scr[half:, :] = jnp.log2(ratio / other_ref[...])
     for i in range(len(tiles)):
         for j in range(lanes):
             at = (i * lanes + j) * 128
-            b_scr[:, at : at + 128] = first_ref[pl.ds(off_ref[i] + j, 1), :]
-    b_scr[...] = jnp.log2(ratio / b_scr[...])
+            b_scr[:, at : at + 128] = line_scr[pl.ds(off_ref[i] + j, 1), :]
     copies[0].wait()
     col_scr[...] = jnp.zeros_like(col_scr)
     width = 256
@@ -266,7 +291,7 @@
             inverse = 1.0 / jnp.sum(s_scr[g : g + width].T, axis=0, keepdims=True)
             weighted = jnp.sum(u_scr[g : g + width].T, axis=0, keepdims=True)
             place = t * (tr // width) + g // width
-            score_ref[pl.ds(place, 1), :] = weighted * inverse * (1.0 / LOG2E)
+            score_scr[pl.ds(place, 1), :] = weighted * inverse * (1.0 / LOG2E)
             high = inverse.astype(BF16)
             low = (inverse - high.astype(F32)).astype(BF16)
             i_scr[:, g : g + width] = jnp.concatenate(
@@ -283,27 +308,47 @@
         for j in range(lanes):
             at = (i * lanes + j) * 128
             line = jnp.sum(col_scr[:, at : at + 128], axis=0, keepdims=True)
-            out_ref[pl.ds(off_ref[i] + j, 1), :] = line
+            line_scr[pl.ds(off_ref[i] + j, 1), :] = line
+    keep_ref[...] = line_scr[:half, :]
+    give_ref[:half, :] = line_scr[half:, :]
+    blocks = rows // BLOCK_ROWS
+    peers = NZ * NY
+    line_scr[: NK * peers, :] = jnp.zeros((NK * peers, BLOCK_ROWS), F32)
+    for b in range(blocks):
+        at = b % 2 * BLOCK_ROWS
+
+        @pl.when(b < live_ref[0])
+        def _():
+            score = score_scr[b // 2 : b // 2 + 1, at : at + BLOCK_ROWS]
+            line_scr[pl.ds(to_ref[b], 1), :] = score.astype(BF16).astype(F32)
+
+    sent_ref[...] = line_scr[:peers, :]
+    give_ref[half:, :] = line_scr[peers : NK * peers, :]
     store.wait()
 
 
-def second_sweep(offsets, scaled, first, arrived, pieces, ratio):
+def second_sweep(offsets, targets, live, scaled, mine, other, arrived, pieces, ratio):
     rows = scaled.shape[0]
     total = sum(p.shape[0] for p in pieces)
     tr = ROW_TILE
+    half = mine.shape[0]
+    peers = NZ * NY
     vmem = pl.BlockSpec(memory_space=pltpu.VMEM)
+    smem = pl.BlockSpec(memory_space=pltpu.SMEM)
     any_space = pl.BlockSpec(memory_space=pl.ANY)
     return pl.pallas_call(
         functools.partial(second_kernel, n_pieces=len(pieces), tr=tr, rg=16, ratio=ratio),
-        in_specs=[pl.BlockSpec(memory_space=pltpu.SMEM), vmem, vmem, any_space]
-        + [any_space] * len(pieces),
-        out_specs=[vmem, vmem, any_space],
+        in_specs=[smem, smem, smem, vmem, vmem, vmem, any_space] + [any_space] * len(pieces),
+        out_specs=[vmem, vmem, vmem, any_space],
         out_shape=[
-            jax.ShapeDtypeStruct((total // 128, 128), F32),
-            jax.ShapeDtypeStruct((rows // 256, 256), F32),
+            pltpu.VMEM((half, 128), F32),
+            pltpu.VMEM((peers, BLOCK_ROWS), F32),
+            pltpu.VMEM((half + peers, 128), F32),
             pltpu.HBM(arrived.shape, BF16),
         ],
         scratch_shapes=[
+            pltpu.VMEM((total // 128, 128), F32),
+            pltpu.VMEM((rows // 256, 256), F32),
             pltpu.VMEM((1, total), F32),
             pltpu.VMEM((8, total), F32),
             pltpu.VMEM((tr, total), BF16),
@@ -318,51 +363,70 @@
         compiler_params=params(26),
         cost_estimate=cost(rows, total, 3),
         name="second_sweep",
-    )(offsets, in_vmem(scaled), first, in_hbm(arrived), *pieces)
-
-
-def finish_kernel(place_ref, col_ref, last_ref, kept_ref, bal_ref, out_ref, buf, *, scale):
-    lines = col_ref.shape[0]
-    bal_ref[...] = (col_ref[...] + last_ref[:lines, :]) * scale
-    z, y, k = place_ref[0], place_ref[1], place_ref[2]
-    for dz in range(NZ):
-        for dy in range(NY):
-            at = dz * NY + dy
-            to = (((z - dz) & (NZ - 1)) * NY + ((y - dy) & (NY - 1))) * NK
-            buf[pl.ds(to + k, 1), :] = kept_ref[at : at + 1, :]
-            buf[pl.ds(to + 1 - k, 1), :] = last_ref[lines + at : lines + at + 1, :]
-    out_ref[...] = buf[...].astype(BF16)
-
-
-def finish(place, column, last, kept, scale):
-    peers = NZ * NY * NK
+    )(offsets, targets, live, in_vmem(scaled), mine, other, in_hbm(arrived), *pieces)
+
+
+def pack_kernel(k_ref, col_ref, a_ref, b_ref, c_ref, sent_ref, got_ref, out_ref):
+    half = col_ref.shape[0]
+    peers = sent_ref.shape[0]
+    out_ref[:, :half, :] = jnp.broadcast_to(
+        (col_ref[...] + a_ref[...] + (b_ref[...] + c_ref[...]))[None], (peers, half, 128)
+    )
+    out_ref[:, half:, :] = jnp.zeros((peers, out_ref.shape[1] - half, 128), F32)
+    k = k_ref[0]
+    for i in range(peers):
+        out_ref[i, pl.ds(half + k, 1), :] = sent_ref[i : i + 1, :]
+        out_ref[i, pl.ds(half + 1 - k, 1), :] = got_ref[half + i : half + i + 1, :]
+
+
+def pack(k, column, arrived, sent, got):
+    half, peers = column.shape[0], sent.shape[0]
+    vmem = pl.BlockSpec(memory_space=pltpu.VMEM)
+    return pl.pallas_call(
+        pack_kernel,
+        in_specs=[pl.BlockSpec(memory_space=pltpu.SMEM)] + [vmem] * 6,
+        out_specs=vmem,
+        out_shape=jax.ShapeDtypeStruct((peers, half + 8, 128), F32),
+        compiler_params=params(4),
+        name="pack",
+    )(k, column, *arrived, sent, got)
+
+
+def finish_kernel(k_ref, mine_ref, other_ref, all_ref, bal_ref, out_ref, *, scale):
+    half = mine_ref.shape[0]
+    k = k_ref[0]
+    bal_ref[pl.ds(pl.multiple_of(k * half, half), half), :] = mine_ref[...] * scale
+    bal_ref[pl.ds(pl.multiple_of((1 - k) * half, half), half), :] = other_ref[...] * scale
+    peers = all_ref.shape[0]
+    scores = jnp.concatenate([all_ref[i, half : half + NK, :] for i in range(peers)], axis=0)
+    out_ref[...] = scores.astype(BF16)
+
+
+def finish(k, mine, other, everything, scale):
+    half, peers = mine.shape[0], everything.shape[0]
     vmem = pl.BlockSpec(memory_space=pltpu.VMEM)
     return pl.pallas_call(
         functools.partial(finish_kernel, scale=scale),
         in_specs=[pl.BlockSpec(memory_space=pltpu.SMEM), vmem, vmem, vmem],
         out_specs=[vmem, vmem],
         out_shape=[
-            jax.ShapeDtypeStruct(column.shape, F32),
-            jax.ShapeDtypeStruct((peers, 128), BF16),
+            jax.ShapeDtypeStruct((NK * half, 128), F32),
+            jax.ShapeDtypeStruct((NK * peers, BLOCK_ROWS), BF16),
         ],
-        scratch_shapes=[pltpu.VMEM((peers, 128), F32)],
-        compiler_params=params(8),
+        compiler_params=params(4),
         name="finish",
-    )(place, column, last, kept)
-
-
-def all_sum(values, other):
-    for name, perms in (
-        ("cent", [x_perm(s) for s in (1, 3, 2)]),
-        ("rows", [rows_perm(0, 0, 1)]),
-        ("rows", [rows_perm(0, s, 0) for s in (1, 3, 2)]),
-        ("rows", [rows_perm(s, 0, 0) for s in (1, 3, 2)]),
-    ):
-        arrived = [lax.ppermute(values, name, perm) for perm in perms]
-        for part in arrived:
-            values = values + part
-    values, other = lax.optimization_barrier((values, other))
-    return values, other
+    )(k, mine, other, everything)
+
+
+def x_parts(values):
+    return [lax.ppermute(values, "cent", x_perm(s)) for s in (1, 3, 2)]
+
+
+def plane_exchange(blocks):
+    groups = [[(z * NY + y) * NK + k for z in range(NZ) for y in range(NY)] for k in range(NK)]
+    return lax.all_to_all(
+        blocks, "rows", split_axis=0, concat_axis=0, tiled=True, axis_index_groups=groups
+    )
 
 
 def local(embeddings, centroids, owners, live_blocks):
@@ -377,8 +441,8 @@
     peers = NZ * NY * NK
     total = n_cent * NX
 
-    place = jnp.stack([z, y, k]).astype(jnp.int32)
-    own, mine = unit_cents(k.reshape(1).astype(jnp.int32), centroids)
+    core = k.reshape(1).astype(jnp.int32)
+    own, mine = unit_cents(core, centroids)
     right = lax.ppermute(mine, "cent", x_perm(1))
     left = lax.ppermute(mine, "cent", x_perm(-1))
     embeddings, mine = lax.optimization_barrier((embeddings, mine))
@@ -396,6 +460,7 @@
         (far, sums_own, sums_right, sums_left)
     )
     far += [lax.ppermute(t, "rows", swap) for t in far]
+    sums_far = first_sweep(scaled, far[:2])
 
     def line(dx, kk, quarter):
         return (((x + dx) & (NX - 1)) * n_cent + kk * half + quarter * TILE) // 128
@@ -403,51 +468,30 @@
     starts = [line(0, q // 2, q % 2) for q in range(4)]
     for dx in (-1, 1, 2):
         starts += [line(dx, k, 0), line(dx, k, 1), line(dx, 1 - k, 0), line(dx, 1 - k, 1)]
-    offsets = jnp.stack(starts).astype(jnp.int32)
-
-    column = last_sweep(offsets, scaled, far, [*sums_own, *sums_right, *sums_left])
-    column, arrived = all_sum(column, arrived)
+    lines = total // 128
+    offsets = jnp.stack(starts).astype(jnp.int32) ^ (k * (lines // NK)).astype(jnp.int32)
+
+    ready = [*sums_own, *sums_right, *sums_left, *sums_far]
+    keep, give = last_sweep(offsets, scaled, far[2:], ready)
+    keep = keep + lax.ppermute(give, "rows", swap)
+    for part in x_parts(keep):
+        keep = keep + part
+    keep, arrived = lax.optimization_barrier((keep, arrived))
+    keep = sum_blocks(plane_exchange(jnp.broadcast_to(keep[None], (NZ * NY, *keep.shape))))
+    other = lax.ppermute(keep, "rows", swap)
+
     ratio = float(rows * NX * peers) / total
     pieces = [own, right[0], in_hbm(right[1]), left[0], in_hbm(left[1]), *far]
-    column, score, moved = second_sweep(offsets, scaled, column, arrived, pieces, ratio)
-
-    blocks = owners.shape[0]
-    score = score.astype(BF16).astype(F32).reshape(blocks, BLOCK_ROWS)
-    owner_z = (owners // (NK * NY) - z) & (NZ - 1)
-    owner_y = (owners // NK - y) & (NY - 1)
-    owner_k = (owners - k) & (NK - 1)
-    relative = (owner_z * NY + owner_y) * NK + owner_k
-    live = jnp.arange(blocks, dtype=jnp.int32) < live_blocks[0]
-    hit = (relative[None, :] == jnp.arange(peers, dtype=jnp.int32)[:, None]) & live[None, :]
-    sent = jnp.sum(jnp.where(hit[:, :, None], score[None], 0.0), axis=1)
-    sent = sent.reshape(NZ, NY * NK, BLOCK_ROWS)
-    lines = total // 128
-
-    for part in [lax.ppermute(column, "cent", x_perm(s)) for s in (1, 3, 2)]:
-        column = column + part
-    both = [
-        lax.ppermute(jnp.concatenate([column, sent[s]]), "rows", rows_perm(s, 0, 0))
-        for s in (1, 3, 2)
-    ]
-    column = column + both[0][:lines] + both[1][:lines] + both[2][:lines]
-    both = [both[0], both[2], both[1]]
-    sent = jnp.stack([sent[0]] + [b[lines:] for b in both]).reshape(NZ, NY, NK, BLOCK_ROWS)
-    both = [
-        lax.ppermute(
-            jnp.concatenate([column, sent[:, s].reshape(NZ * NK, BLOCK_ROWS)]),
-            "rows",
-            rows_perm(0, s, 0),
-        )
-        for s in (1, 3, 2)
-    ]
-    column = column + both[0][:lines] + both[1][:lines] + both[2][:lines]
-    both = [both[0], both[2], both[1]]
-    got = [b[lines:].reshape(NZ, NK, BLOCK_ROWS) for b in both]
-    sent = jnp.stack([sent[:, 0], *got], axis=1)
-    kept = sent[:, :, 0].reshape(NZ * NY, BLOCK_ROWS)
-    given = sent[:, :, 1].reshape(NZ * NY, BLOCK_ROWS)
-    last = lax.ppermute(jnp.concatenate([column, given]), "rows", swap)
-    balance, moved_score = finish(place, column, last, kept, 1.0 / ratio)
+    targets = ((owners ^ k) & (NK - 1)) * (NZ * NY) + owners // NK
+    column, sent, give, moved = second_sweep(
+        offsets, targets, live_blocks, scaled, keep, other, arrived, pieces, ratio
+    )
+    got = lax.ppermute(give, "rows", swap)
+    column = column + got[: column.shape[0]]
+    everything = plane_exchange(pack(core, column, x_parts(column), sent, got))
+    column = everything[:, : column.shape[0]].sum(0)
+    other = lax.ppermute(column, "rows", swap)
+    balance, moved_score = finish(core, column, other, everything, 1.0 / ratio)
     return moved.reshape(peers * BLOCK_ROWS, d), moved_score.reshape(-1), balance.reshape(-1)
 
 

time: 114 us -> 110 us (0.965)
  blocking collectives: 0 us -> 23.7 us
  starting transfers between devices: 51.6 us -> 31.1 us
  waiting for transfers between devices: 19.8 us -> 12.6 us
    all_to_all x0 -> x2, blocking collectives: none -> 23.7 us  [plane_exchange(): lax.all_to_all(blocks, 'rows', split_axis=0, concat_axis=0, tiled=True, a...]
    ppermute x20 -> x10, starting transfers between devices: 34.1 us -> 12.6 us  [the longest x6 4.93 us: x_parts(): return [lax.ppermute(values, 'cent', x_perm(s)) for s in (1, 3, 2)]]
    ppermute x20 -> x10, waiting for transfers between devices: 18.2 us -> 9.38 us  [the longest x6 5.92 us: x_parts(): return [lax.ppermute(values, 'cent', x_perm(s)) for s in (1, 3, 2)]]
    pallas_call x3 -> x4, Pallas kernels: 7.15 us -> 9.39 us  [first_sweep(): pl.pallas_call(first_kernel, out_shape=[pltpu.VMEM((1, p.shape[0]), F32)...]
    ppermute x1, starting transfers between devices: 2.11 us -> 0.01 us  [local(): right = lax.ppermute(mine, 'cent', x_perm(1))]
    ppermute x1, starting transfers between devices: 1.35 us -> 3.38 us  [local(): left = lax.ppermute(mine, 'cent', x_perm(-1))]
    all_to_all x1, waiting for transfers between devices: 0.01 us -> 1.92 us  [local(): lax.all_to_all(outgoing, 'rows', split_axis=0, concat_axis=0, tiled=True)]
    ppermute x1, starting transfers between devices: 0.2 us -> 1.87 us  [local(): right = [right, lax.ppermute(right, 'rows', swap)]]
  transfers between devices with their start and end apart: 29 -> 19, of which waited for: 14 -> 11; matrix products, arithmetic and copies ran while one was open for 1% -> 0% of each run, Pallas kernels for 12% -> 13%
where the time goes in v3:
time: 110 us
  Pallas kernels  40.5 us (37%)
  starting transfers between devices  31.1 us (28%)
  blocking collectives  23.7 us (22%)
  waiting for transfers between devices  12.6 us (11%)
  between operations  1.52 us (1%)
    all_to_all x2, blocking collectives, plane_exchange(): lax.all_to_all(blocks, 'rows', split_axis=0, concat_axis=0, tiled=True, a...  23.7 us
    pallas_call x1, Pallas kernels, second_sweep(): pl.pallas_call(functools.partial(second_kernel, n_pieces=len(pieces), tr=...  22.7 us
    pallas_call x4, Pallas kernels, first_sweep(): pl.pallas_call(first_kernel, out_shape=[pltpu.VMEM((1, p.shape[0]), F32)...  9.39 us
    all_to_all x1, starting transfers between devices, local(): lax.all_to_all(outgoing, 'rows', split_axis=0, concat_axis=0, tiled=True)  9.1 us
    ppermute x6, waiting for transfers between devices, x_parts(): return [lax.ppermute(values, 'cent', x_perm(s)) for s in (1, 3, 2)]  5.92 us
    ppermute x6, starting transfers between devices, x_parts(): return [lax.ppermute(values, 'cent', x_perm(s)) for s in (1, 3, 2)]  4.93 us
    ppermute x1, starting transfers between devices, local(): other = lax.ppermute(column, 'rows', swap)  3.56 us
    ppermute x1, starting transfers between devices, local(): left = lax.ppermute(mine, 'cent', x_perm(-1))  3.38 us
  transfers between devices with their start and end apart: 19, of which 11 were waited for; matrix products, arithmetic and copies ran while one was open for 0% of the time, Pallas kernels for 13%

profile of v3, /device:TPU:1, one launch (start us, length us, event | category | flops | bytes accessed | tf_op | source)
XLA Modules:
  0.0 109.6 jit_solution(6247935180704258915)
XLA Ops:
  0.7 2.5 %unit_cents.1 = (bf16[2048,256]{1,0:T(8,128)(2,1)S(1)}, bf16[1024,256]{1,0:T(8,128)(2,1)}) custom-call(s32[1]{0:T(128)} %bitcast.16.place_ref.k_ref, f32[2048,256]{1,0:T(8,128)} %c_ref.1), custom_call_target="tpu_custom_call" | custom-call | tf_op jit(solution)/shard_map/unit_cents/pallas_call | solution.py:79
  3.2 3.4 %collective-permute-start.1 = (bf16[1024,256]{1,0:T(8,128)(2,1)}, bf16[1024,256]{1,0:T(8,128)(2,1)S(1)}, u32[]{:S(2)}, u32[]{:S(2)}) collective-permute-start(bf16[1024,256]{1,0:T(8,128)(2,1)} %get-tuple-element.36), channel_id=1, source_target_pairs={{0,3},{1,0},{2,1},{3,2},{4,7},{5,4},{6,5},{7,6},{8,11},{9,8},{10,9... | collective-permute-start | bytes 1572872 | tf_op jit(solution)/shard_map/ppermute | solution.py:447
  7.2 2.8 %unit_rows.1 = (bf16[32,128,256]{2,1,0:T(8,128)(2,1)}, bf16[2048,256]{1,0:T(8,128)(2,1)S(1)}) custom-call(s32[16]{0:T(128)S(1)} %copy-done.3, s32[1]{0:T(128)S(6)} %copy.7.live_ref, f32[2048,256]{1,0:T(8,128)S(1)} %copy-done), custom_call_target="tpu_custom_call" | custom-call | tf_op jit(solution)/shard_map/unit_rows/pallas_call | solution.py:148
  10.1 9.1 %all-to-all-start = ((bf16[32,128,256]{2,1,0:T(8,128)(2,1)}), bf16[32,128,256]{2,1,0:T(8,128)(2,1)}, u32[]{:S(2)}, u32[]{:S(2)}) async-start(bf16[32,128,256]{2,1,0:T(8,128)(2,1)} %get-tuple-element.60), calls=%async_computation | async-start | bytes 4194304 | tf_op jit(solution)/shard_map/all_to_all | solution.py:450
  19.2 1.3 %collective-permute-done.right_ref.refs_0_.refs_1_ = bf16[1024,256]{1,0:T(8,128)(2,1)S(1)} collective-permute-done((bf16[1024,256]{1,0:T(8,128)(2,1)}, bf16[1024,256]{1,0:T(8,128)(2,1)S(1)}, u32[]{:S(2)}, u32[]{:S(2)}) %collective-permute-start) | collective-permute-done | bytes 524320 | tf_op jit(solution)/shard_map/ppermute | solution.py:446
  20.5 1.9 %collective-permute-start.4 = (bf16[1024,256]{1,0:T(8,128)(2,1)S(1)}, bf16[1024,256]{1,0:T(8,128)(2,1)S(1)}, u32[]{:S(2)}, u32[]{:S(2)}) collective-permute-start(bf16[1024,256]{1,0:T(8,128)(2,1)S(1)} %collective-permute-done.right_ref.refs_0_.refs_1_), channel_id=1, source_target_pairs={{0,4},{4,0},{8,12},{12,8},{16,20},{20,16},{24,28},{28,24},{32,36},... | collective-permute-start | bytes 1572872 | tf_op jit(solution)/shard_map/ppermute | solution.py:454
  22.4 2.7 %collective-permute-start.3 = (bf16[512,256]{1,0:T(8,128)(2,1)S(1)}, bf16[512,256]{1,0:T(8,128)(2,1)}, u32[]{:S(2)}, u32[]{:S(2)}) collective-permute-start(bf16[512,256]{1,0:T(8,128)(2,1)S(1)} %get-tuple-element.43), channel_id=1, source_target_pairs={{0,3},{1,0},{2,1},{3,2},{4,7},{5,4},{6,5},{7,6},{8,11},{9,8},{10,9... | collective-permute-start | bytes 786440 | tf_op jit(solution)/shard_map/ppermute | solution.py:453
  25.1 2.4 %first_sweep.4.refs_2_ = f32[1,2048]{1,0:T(1,128)S(1)} custom-call(bf16[2048,256]{1,0:T(8,128)(2,1)S(1)} %get-tuple-element.39.r_ref, bf16[2048,256]{1,0:T(8,128)(2,1)S(1)} %get-tuple-element.44.refs_0_), custom_call_target="tpu_custom_call" | custom-call | flops 2048 | bytes 2048 | tf_op jit(solution)/shard_map/first_sweep/pallas_call | solution.py:188
  27.5 2.4 %first_sweep.5 = (f32[1,1024]{1,0:T(1,128)S(1)}, f32[1,1024]{1,0:T(1,128)S(1)}) custom-call(bf16[2048,256]{1,0:T(8,128)(2,1)S(1)} %get-tuple-element.39.r_ref, bf16[1024,256]{1,0:T(8,128)(2,1)S(1)} %collective-permute-done.right_ref.refs_0_.refs_1_, bf16[1024,256]{1,0:T(8,128)(2,1)S(1)} %collective-permute-done.4.refs_1_.refs_2_), custom_call_target="tpu_custom_call" | custom-call | flops 2048 | bytes 2048 | tf_op jit(solution)/shard_map/first_sweep/pallas_call | solution.py:188
  29.9 2.4 %first_sweep.6 = (f32[1,1024]{1,0:T(1,128)S(1)}, f32[1,1024]{1,0:T(1,128)S(1)}) custom-call(bf16[2048,256]{1,0:T(8,128)(2,1)S(1)} %get-tuple-element.39.r_ref, bf16[1024,256]{1,0:T(8,128)(2,1)S(1)} %collective-permute-done.1.left_ref.refs_0_.refs_3_, bf16[1024,256]{1,0:T(8,128)(2,1)S(1)} %collective-permute-done.5.refs_1_.refs_4_), custom_call_target="tpu_custom_call" | custom-call | flops 2048 | bytes 2048 | tf_op jit(solution)/shard_map/first_sweep/pallas_call | solution.py:188
  32.4 1.2 %collective-permute-start.6 = (bf16[512,256]{1,0:T(8,128)(2,1)S(1)}, bf16[512,256]{1,0:T(8,128)(2,1)}, u32[]{:S(2)}, u32[]{:S(2)}) collective-permute-start(bf16[512,256]{1,0:T(8,128)(2,1)S(1)} %collective-permute-done.2.refs_0_.refs_5_), channel_id=1, source_target_pairs={{0,4},{4,0},{8,12},{12,8},{16,20},{20,16},{24,28},{28,24},{32,36},... | collective-permute-start | bytes 786440 | tf_op jit(solution)/shard_map/ppermute | solution.py:462
  33.9 2.2 %first_sweep.7 = (f32[1,512]{1,0:T(1,128)S(1)}, f32[1,512]{1,0:T(1,128)S(1)}) custom-call(bf16[2048,256]{1,0:T(8,128)(2,1)S(1)} %get-tuple-element.39.r_ref, bf16[512,256]{1,0:T(8,128)(2,1)S(1)} %collective-permute-done.2.refs_0_.refs_5_, bf16[512,256]{1,0:T(8,128)(2,1)} %collective-permute-done.3.refs_1_.refs_6_), custom_call_target="tpu_custom_call" | custom-call | flops 2048 | bytes 1024 | tf_op jit(solution)/shard_map/first_sweep/pallas_call | solution.py:188
  36.2 2.3 %last_sweep.1 = (f32[32,128]{1,0:T(8,128)S(1)}, f32[32,128]{1,0:T(8,128)S(1)}) custom-call(s32[16]{0:T(128)S(1)} %broadcast_xor_fusion.off_ref, bf16[2048,256]{1,0:T(8,128)(2,1)S(1)} %get-tuple-element.39.r_ref, bf16[512,256]{1,0:T(8,128)(2,1)} %collective-permute-done.6.refs_0_.refs_7_, bf16[512,256]{1,0:T(8,128)(2,1)} %collective-permute-done.7.refs_1_.refs_8_, ...), custom_call_target="tpu_custom_call" | custom-call | flops 2048 | bytes 1024 | tf_op jit(solution)/shard_map/last_sweep/pallas_call | solution.py:214
  39.8 1.5 %collective-permute-start.10 = (f32[32,128]{1,0:T(8,128)S(1)}, f32[32,128]{1,0:T(8,128)S(1)}, u32[]{:S(2)}, u32[]{:S(2)}) collective-permute-start(f32[32,128]{1,0:T(8,128)S(1)} %add.126), channel_id=1, source_target_pairs={{0,3},{1,0},{2,1},{3,2},{4,7},{5,4},{6,5},{7,6},{8,11},{9,8},{10,9... | collective-permute-start | bytes 49160 | tf_op jit(solution)/shard_map/ppermute | solution.py:422
  41.9 2.4 %collective-permute-done.11 = f32[32,128]{1,0:T(8,128)S(1)} collective-permute-done((f32[32,128]{1,0:T(8,128)S(1)}, f32[32,128]{1,0:T(8,128)S(1)}, u32[]{:S(2)}, u32[]{:S(2)}) %collective-permute-start.11) | collective-permute-done | bytes 16416 | tf_op jit(solution)/shard_map/ppermute | solution.py:422
  45.1 1.9 %all-to-all-done.in_ref = bf16[32,128,256]{2,1,0:T(8,128)(2,1)} async-done(((bf16[32,128,256]{2,1,0:T(8,128)(2,1)}), bf16[32,128,256]{2,1,0:T(8,128)(2,1)}, u32[]{:S(2)}, u32[]{:S(2)}) %all-to-all-start) | async-done | bytes 2097184 | tf_op jit(solution)/shard_map/all_to_all | solution.py:450
  47.1 13.2 %all_to_all.15.in_ref = f32[16,32,128]{2,1,0:T(8,128)S(1)} all-to-all(f32[16,32,128]{2,1,0:T(8,128)S(1)} %broadcast_in_dim.2), channel_id=1, replica_groups={{0,8,16,24,32,40,48,56,64,72,80,88,96,104,112,120},{4,12,20,28,36,44,52..., dimensions={0} | all-to-all | bytes 524288 | tf_op jit(solution)/shard_map/all_to_all | solution.py:427
  60.3 3.3 %collective-permute-start.12 = (f32[32,128]{1,0:T(8,128)S(1)}, f32[32,128]{1,0:T(8,128)S(1)}, u32[]{:S(2)}, u32[]{:S(2)}) collective-permute-start(f32[32,128]{1,0:T(8,128)S(1)} %sum_blocks.1.mine_ref), channel_id=1, source_target_pairs={{0,4},{4,0},{8,12},{12,8},{16,20},{20,16},{24,28},{28,24},{32,36},... | collective-permute-start | bytes 49160 | tf_op jit(solution)/shard_map/ppermute | solution.py:481
  64.5 22.7 %second_sweep.1 = (f32[32,128]{1,0:T(8,128)S(1)}, f32[16,128]{1,0:T(8,128)S(1)}, f32[48,128]{1,0:T(8,128)S(1)}, bf16[32,128,256]{2,1,0:T(8,128)(2,1)}) custom-call(s32[16]{0:T(128)S(1)} %broadcast_xor_fusion.off_ref, s32[16]{0:T(128)S(1)} %fusion.to_ref, s32[1]{0:T(128)S(6)} %copy.7.live_ref, bf16[2048,256]{1,0:T(8,128)(2,1)S(1)} %get-tuple-element.39.r_ref, ...), custom_call_target="tpu_custom_call" | custom-call | flops 6144 | bytes 8192 | tf_op jit(solution)/shard_map/second_sweep/pallas_call | solution.py:339
  88.5 1.4 %collective-permute-start.16 = (f32[32,128]{1,0:T(8,128)S(1)}, f32[32,128]{1,0:T(8,128)S(1)}, u32[]{:S(2)}, u32[]{:S(2)}) collective-permute-start(f32[32,128]{1,0:T(8,128)S(1)} %slice_add_fusion.col_ref), channel_id=1, source_target_pairs={{0,2},{1,3},{2,0},{3,1},{4,6},{5,7},{6,4},{7,5},{8,10},{9,11},{10,... | collective-permute-start | bytes 49160 | tf_op jit(solution)/shard_map/ppermute | solution.py:422
  91.3 1.3 %collective-permute-done.16.c_ref = f32[32,128]{1,0:T(8,128)S(1)} collective-permute-done((f32[32,128]{1,0:T(8,128)S(1)}, f32[32,128]{1,0:T(8,128)S(1)}, u32[]{:S(2)}, u32[]{:S(2)}) %collective-permute-start.16) | collective-permute-done | bytes 16416 | tf_op jit(solution)/shard_map/ppermute | solution.py:422
  92.7 1.3 %collective-permute-done.14.a_ref = f32[32,128]{1,0:T(8,128)S(1)} collective-permute-done((f32[32,128]{1,0:T(8,128)S(1)}, f32[32,128]{1,0:T(8,128)S(1)}, u32[]{:S(2)}, u32[]{:S(2)}) %collective-permute-start.14) | collective-permute-done | bytes 16416 | tf_op jit(solution)/shard_map/ppermute | solution.py:422
  94.0 10.5 %all_to_all.16.all_ref = f32[16,40,128]{2,1,0:T(8,128)S(1)} all-to-all(f32[16,40,128]{2,1,0:T(8,128)S(1)} %pack.1), channel_id=1, replica_groups={{0,8,16,24,32,40,48,56,64,72,80,88,96,104,112,120},{4,12,20,28,36,44,52..., dimensions={0} | all-to-all | bytes 655360 | tf_op jit(solution)/shard_map/all_to_all | solution.py:427
  104.6 3.6 %collective-permute-start.17 = (f32[32,128]{1,0:T(8,128)S(1)}, f32[32,128]{1,0:T(8,128)S(1)}, u32[]{:S(2)}, u32[]{:S(2)}) collective-permute-start(f32[32,128]{1,0:T(8,128)S(1)} %slice_reduce_fusion.mine_ref), channel_id=1, source_target_pairs={{0,4},{4,0},{8,12},{12,8},{16,20},{20,16},{24,28},{28,24},{32,36},... | collective-permute-start | bytes 49160 | tf_op jit(solution)/shard_map/ppermute | solution.py:493
  (44 shorter events, 8.5 us)
Async XLA Ops:
  0.6 6.6 %copy-start.3 = (s32[16]{0:T(128)S(1)}, s32[16]{0:T(128)}, u32[]{:S(2)}) copy-start(s32[16]{0:T(128)} %owner_ref.1) | copy-start | bytes 196
  0.6 6.6 %copy-start = (f32[2048,256]{1,0:T(8,128)S(1)}, f32[2048,256]{1,0:T(8,128)}, u32[]{:S(2)}) copy-start(f32[2048,256]{1,0:T(8,128)} %e_ref) | copy-start | bytes 6291460
  3.2 16.0 %collective-permute-start.1 = (bf16[1024,256]{1,0:T(8,128)(2,1)}, bf16[1024,256]{1,0:T(8,128)(2,1)S(1)}, u32[]{:S(2)}, u32[]{:S(2)}) collective-permute-start(bf16[1024,256]{1,0:T(8,128)(2,1)} %get-tuple-element.36), channel_id=1, source_target_pairs={{0,3},{1,0},{2,1},{3,2},{4,7},{5,4},{6,5},{7,6},{8,11},{9,8},{10,9... | collective-permute-start | bytes 1572872 | tf_op jit(solution)/shard_map/ppermute | solution.py:447
  6.6 13.9 %collective-permute-start = (bf16[1024,256]{1,0:T(8,128)(2,1)}, bf16[1024,256]{1,0:T(8,128)(2,1)S(1)}, u32[]{:S(2)}, u32[]{:S(2)}) collective-permute-start(bf16[1024,256]{1,0:T(8,128)(2,1)} %get-tuple-element.36), channel_id=1, source_target_pairs={{0,1},{1,2},{2,3},{3,0},{4,5},{5,6},{6,7},{7,4},{8,9},{9,10},{10,1... | collective-permute-start | bytes 1572872 | tf_op jit(solution)/shard_map/ppermute | solution.py:446
  10.1 37.0 %all-to-all-start = ((bf16[32,128,256]{2,1,0:T(8,128)(2,1)}), bf16[32,128,256]{2,1,0:T(8,128)(2,1)}, u32[]{:S(2)}, u32[]{:S(2)}) async-start(bf16[32,128,256]{2,1,0:T(8,128)(2,1)} %get-tuple-element.60), calls=%async_computation | async-start | bytes 4194304 | tf_op jit(solution)/shard_map/all_to_all | solution.py:450
  20.5 7.0 %collective-permute-start.4 = (bf16[1024,256]{1,0:T(8,128)(2,1)S(1)}, bf16[1024,256]{1,0:T(8,128)(2,1)S(1)}, u32[]{:S(2)}, u32[]{:S(2)}) collective-permute-start(bf16[1024,256]{1,0:T(8,128)(2,1)S(1)} %collective-permute-done.right_ref.refs_0_.refs_1_), channel_id=1, source_target_pairs={{0,4},{4,0},{8,12},{12,8},{16,20},{20,16},{24,28},{28,24},{32,36},... | collective-permute-start | bytes 1572872 | tf_op jit(solution)/shard_map/ppermute | solution.py:454
  22.3 7.6 %collective-permute-start.5 = (bf16[1024,256]{1,0:T(8,128)(2,1)S(1)}, bf16[1024,256]{1,0:T(8,128)(2,1)S(1)}, u32[]{:S(2)}, u32[]{:S(2)}) collective-permute-start(bf16[1024,256]{1,0:T(8,128)(2,1)S(1)} %collective-permute-done.1.left_ref.refs_0_.refs_3_), channel_id=1, source_target_pairs={{0,4},{4,0},{8,12},{12,8},{16,20},{20,16},{24,28},{28,24},{32,36},... | collective-permute-start | bytes 1572872 | tf_op jit(solution)/shard_map/ppermute | solution.py:455
  22.4 10.0 %collective-permute-start.2 = (bf16[512,256]{1,0:T(8,128)(2,1)S(1)}, bf16[512,256]{1,0:T(8,128)(2,1)S(1)}, u32[]{:S(2)}, u32[]{:S(2)}) collective-permute-start(bf16[512,256]{1,0:T(8,128)(2,1)S(1)} %get-tuple-element.42), channel_id=1, source_target_pairs={{0,1},{1,2},{2,3},{3,0},{4,5},{5,6},{6,7},{7,4},{8,9},{9,10},{10,1... | collective-permute-start | bytes 786440 | tf_op jit(solution)/shard_map/ppermute | solution.py:453
  22.4 9.9 %collective-permute-start.3 = (bf16[512,256]{1,0:T(8,128)(2,1)S(1)}, bf16[512,256]{1,0:T(8,128)(2,1)}, u32[]{:S(2)}, u32[]{:S(2)}) collective-permute-start(bf16[512,256]{1,0:T(8,128)(2,1)S(1)} %get-tuple-element.43), channel_id=1, source_target_pairs={{0,3},{1,0},{2,1},{3,2},{4,7},{5,4},{6,5},{7,6},{8,11},{9,8},{10,9... | collective-permute-start | bytes 786440 | tf_op jit(solution)/shard_map/ppermute | solution.py:453
  27.5 4.8 %copy-start.1 = (bf16[1024,256]{1,0:T(8,128)(2,1)}, bf16[1024,256]{1,0:T(8,128)(2,1)S(1)}, u32[]{:S(2)}) copy-start(bf16[1024,256]{1,0:T(8,128)(2,1)S(1)} %collective-permute-done.4.refs_1_.refs_2_) | copy-start | bytes 1572868
  29.9 2.4 %copy-start.2 = (bf16[1024,256]{1,0:T(8,128)(2,1)}, bf16[1024,256]{1,0:T(8,128)(2,1)S(1)}, u32[]{:S(2)}) copy-start(bf16[1024,256]{1,0:T(8,128)(2,1)S(1)} %collective-permute-done.5.refs_1_.refs_4_) | copy-start | bytes 1572868
  32.4 3.8 %collective-permute-start.6 = (bf16[512,256]{1,0:T(8,128)(2,1)S(1)}, bf16[512,256]{1,0:T(8,128)(2,1)}, u32[]{:S(2)}, u32[]{:S(2)}) collective-permute-start(bf16[512,256]{1,0:T(8,128)(2,1)S(1)} %collective-permute-done.2.refs_0_.refs_5_), channel_id=1, source_target_pairs={{0,4},{4,0},{8,12},{12,8},{16,20},{20,16},{24,28},{28,24},{32,36},... | collective-permute-start | bytes 786440 | tf_op jit(solution)/shard_map/ppermute | solution.py:462
  33.5 2.6 %collective-permute-start.7 = (bf16[512,256]{1,0:T(8,128)(2,1)}, bf16[512,256]{1,0:T(8,128)(2,1)}, u32[]{:S(2)}, u32[]{:S(2)}) collective-permute-start(bf16[512,256]{1,0:T(8,128)(2,1)} %collective-permute-done.3.refs_1_.refs_6_), channel_id=1, source_target_pairs={{0,4},{4,0},{8,12},{12,8},{16,20},{20,16},{24,28},{28,24},{32,36},... | collective-permute-start | bytes 786440 | tf_op jit(solution)/shard_map/ppermute | solution.py:462
  38.5 1.3 %collective-permute-start.8 = (f32[32,128]{1,0:T(8,128)S(1)}, f32[32,128]{1,0:T(8,128)S(1)}, u32[]{:S(2)}, u32[]{:S(2)}) collective-permute-start(f32[32,128]{1,0:T(8,128)S(1)} %get-tuple-element.59), channel_id=1, source_target_pairs={{0,4},{4,0},{8,12},{12,8},{16,20},{20,16},{24,28},{28,24},{32,36},... | collective-permute-start | bytes 49160 | tf_op jit(solution)/shard_map/ppermute | solution.py:476
  39.8 4.5 %collective-permute-start.11 = (f32[32,128]{1,0:T(8,128)S(1)}, f32[32,128]{1,0:T(8,128)S(1)}, u32[]{:S(2)}, u32[]{:S(2)}) collective-permute-start(f32[32,128]{1,0:T(8,128)S(1)} %add.126), channel_id=1, source_target_pairs={{0,2},{1,3},{2,0},{3,1},{4,6},{5,7},{6,4},{7,5},{8,10},{9,11},{10,... | collective-permute-start | bytes 49160 | tf_op jit(solution)/shard_map/ppermute | solution.py:422
  39.8 4.5 %collective-permute-start.10 = (f32[32,128]{1,0:T(8,128)S(1)}, f32[32,128]{1,0:T(8,128)S(1)}, u32[]{:S(2)}, u32[]{:S(2)}) collective-permute-start(f32[32,128]{1,0:T(8,128)S(1)} %add.126), channel_id=1, source_target_pairs={{0,3},{1,0},{2,1},{3,2},{4,7},{5,4},{6,5},{7,6},{8,11},{9,8},{10,9... | collective-permute-start | bytes 49160 | tf_op jit(solution)/shard_map/ppermute | solution.py:422
  41.3 3.8 %collective-permute-start.9 = (f32[32,128]{1,0:T(8,128)S(1)}, f32[32,128]{1,0:T(8,128)S(1)}, u32[]{:S(2)}, u32[]{:S(2)}) collective-permute-start(f32[32,128]{1,0:T(8,128)S(1)} %add.126), channel_id=1, source_target_pairs={{0,1},{1,2},{2,3},{3,0},{4,5},{5,6},{6,7},{7,4},{8,9},{9,10},{10,1... | collective-permute-start | bytes 49160 | tf_op jit(solution)/shard_map/ppermute | solution.py:422
  60.3 4.2 %collective-permute-start.12 = (f32[32,128]{1,0:T(8,128)S(1)}, f32[32,128]{1,0:T(8,128)S(1)}, u32[]{:S(2)}, u32[]{:S(2)}) collective-permute-start(f32[32,128]{1,0:T(8,128)S(1)} %sum_blocks.1.mine_ref), channel_id=1, source_target_pairs={{0,4},{4,0},{8,12},{12,8},{16,20},{20,16},{24,28},{28,24},{32,36},... | collective-permute-start | bytes 49160 | tf_op jit(solution)/shard_map/ppermute | solution.py:481
  87.2 1.3 %collective-permute-start.13 = (f32[48,128]{1,0:T(8,128)S(1)}, f32[48,128]{1,0:T(8,128)S(1)}, u32[]{:S(2)}, u32[]{:S(2)}) collective-permute-start(f32[48,128]{1,0:T(8,128)S(1)} %get-tuple-element.65), channel_id=1, source_target_pairs={{0,4},{4,0},{8,12},{12,8},{16,20},{20,16},{24,28},{28,24},{32,36},... | collective-permute-start | bytes 73736 | tf_op jit(solution)/shard_map/ppermute | solution.py:489
  88.5 4.1 %collective-permute-start.16 = (f32[32,128]{1,0:T(8,128)S(1)}, f32[32,128]{1,0:T(8,128)S(1)}, u32[]{:S(2)}, u32[]{:S(2)}) collective-permute-start(f32[32,128]{1,0:T(8,128)S(1)} %slice_add_fusion.col_ref), channel_id=1, source_target_pairs={{0,2},{1,3},{2,0},{3,1},{4,6},{5,7},{6,4},{7,5},{8,10},{9,11},{10,... | collective-permute-start | bytes 49160 | tf_op jit(solution)/shard_map/ppermute | solution.py:422
  89.8 2.9 %collective-permute-start.15 = (f32[32,128]{1,0:T(8,128)S(1)}, f32[32,128]{1,0:T(8,128)S(1)}, u32[]{:S(2)}, u32[]{:S(2)}) collective-permute-start(f32[32,128]{1,0:T(8,128)S(1)} %slice_add_fusion.col_ref), channel_id=1, source_target_pairs={{0,3},{1,0},{2,1},{3,2},{4,7},{5,4},{6,5},{7,6},{8,11},{9,8},{10,9... | collective-permute-start | bytes 49160 | tf_op jit(solution)/shard_map/ppermute | solution.py:422
  90.2 3.8 %collective-permute-start.14 = (f32[32,128]{1,0:T(8,128)S(1)}, f32[32,128]{1,0:T(8,128)S(1)}, u32[]{:S(2)}, u32[]{:S(2)}) collective-permute-start(f32[32,128]{1,0:T(8,128)S(1)} %slice_add_fusion.col_ref), channel_id=1, source_target_pairs={{0,1},{1,2},{2,3},{3,0},{4,5},{5,6},{6,7},{7,4},{8,9},{9,10},{10,1... | collective-permute-start | bytes 49160 | tf_op jit(solution)/shard_map/ppermute | solution.py:422
  104.6 4.4 %collective-permute-start.17 = (f32[32,128]{1,0:T(8,128)S(1)}, f32[32,128]{1,0:T(8,128)S(1)}, u32[]{:S(2)}, u32[]{:S(2)}) collective-permute-start(f32[32,128]{1,0:T(8,128)S(1)} %slice_reduce_fusion.mine_ref), channel_id=1, source_target_pairs={{0,4},{4,0},{8,12},{12,8},{16,20},{20,16},{24,28},{28,24},{32,36},... | collective-permute-start | bytes 49160 | tf_op jit(solution)/shard_map/ppermute | solution.py:493

commit v4 on v3

v4 whole, which is shorter than its diff:
```python
import functools
import math

import jax
import jax.numpy as jnp
from jax import lax
from jax.experimental import pallas as pl
from jax.experimental.pallas import tpu as pltpu
from jax.sharding import PartitionSpec as P

BLOCK_ROWS = 128
SCALE = 50.0
EPSILON = 1e-06
LOG2E = math.log2(math.e)
NT = (((1,), (1,)), ((), ()))
NN = (((1,), (0,)), ((), ()))
F32, BF16 = jnp.float32, jnp.bfloat16
NX, NY, NZ, NK = 4, 4, 4, 2
TILE = 512
ROW_TILE = 512
MIB = 2**20


def params(mib):
    return pltpu.CompilerParams(vmem_limit_bytes=mib * MIB)


def in_hbm(x):
    return pltpu.with_memory_space_constraint(x, pltpu.HBM)


def in_vmem(x):
    return pltpu.with_memory_space_constraint(x, pltpu.VMEM)


def cost(rows, cents, passes):
    return pl.CostEstimate(flops=passes * rows, transcendentals=0, bytes_accessed=cents)


def x_perm(shift):
    return [(i, (i + shift) % NX) for i in range(NX)]


def rows_perm(dz, dy, dk):
    out = []
    for z in range(NZ):
        for y in range(NY):
            for k in range(NK):
                target = ((z + dz) % NZ * NY + (y + dy) % NY) * NK + (k + dk) % NK
                out.append(((z * NY + y) * NK + k, target))
    return out


def unit_f32(values):
    squares = jnp.sum(values * values, axis=-1, keepdims=True)
    return values * lax.rsqrt(squares + EPSILON)


def cents_kernel(place_ref, c_ref, all_ref, half_ref, buf, sems):
    half = buf.shape[1]
    copies = []
    for i in range(NK):
        start = pl.multiple_of((place_ref[1] ^ i) * half, half)
        copies.append(pltpu.make_async_copy(c_ref.at[pl.ds(start, half), :], buf.at[i], sems.at[i]))
    for copy in copies:
        copy.start()
    for i, copy in enumerate(copies):
        copy.wait()
        unit = unit_f32(buf[i]).astype(BF16)
        all_ref[pl.ds(pl.multiple_of((place_ref[1] ^ i) * half, half), half), :] = unit
        if i == 0:
            half_ref[...] = unit


def unit_cents(place, centroids):
    n, d = centroids.shape
    half = n // NK
    vmem = pl.BlockSpec(memory_space=pltpu.VMEM)
    return pl.pallas_call(
        cents_kernel,
        in_specs=[pl.BlockSpec(memory_space=pltpu.SMEM), pl.BlockSpec(memory_space=pltpu.HBM)],
        out_specs=[vmem, vmem],
        out_shape=[pltpu.VMEM((n, d), BF16), pltpu.VMEM((half, d), BF16)],
        scratch_shapes=[pltpu.VMEM((NK, half, d), F32), pltpu.SemaphoreType.DMA((NK,))],
        compiler_params=params(8),
        name="unit_cents",
    )(place, in_hbm(centroids))


def forward_kernel(right_ref, left_ref, first_ref, second_ref):
    n = first_ref.shape[0]
    first_ref[...] = right_ref[:n, :]
    second_ref[...] = left_ref[n:, :]


def forward_parts(right, left):
    n, d = right.shape
    vmem = pl.BlockSpec(memory_space=pltpu.VMEM)
    return pl.pallas_call(
        forward_kernel,
        in_specs=[vmem, vmem],
        out_specs=[vmem, vmem],
        out_shape=[jax.ShapeDtypeStruct((n // 2, d), BF16)] * 2,
        compiler_params=params(8),
        cost_estimate=cost(2**26, 0, 2**11),
        name="forward_parts",
    )(right, left)


def rows_kernel(owner_ref, live_ref, e_ref, out_ref, scaled_ref):
    step = pl.program_id(0)

    @pl.when(step == 0)
    def _():
        out_ref[...] = jnp.zeros_like(out_ref)

    unit = unit_f32(e_ref[...])
    scaled_ref[...] = (unit * (SCALE * LOG2E)).astype(BF16)
    low = unit.astype(BF16)
    count = e_ref.shape[0] // BLOCK_ROWS
    for b in range(count):
        block = step * count + b

        @pl.when(block < live_ref[0])
        def _():
            out_ref[owner_ref[block]] = low[b * BLOCK_ROWS : (b + 1) * BLOCK_ROWS]


def unit_rows(owners, live, embeddings, peers):
    n, d = embeddings.shape
    steps = 4
    return pl.pallas_call(
        rows_kernel,
        grid_spec=pltpu.PrefetchScalarGridSpec(
            num_scalar_prefetch=2,
            grid=(steps,),
            in_specs=[pl.BlockSpec((n // steps, d), lambda i, o, l: (i, 0))],
            out_specs=[
                pl.BlockSpec((peers, BLOCK_ROWS, d), lambda i, o, l: (0, 0, 0)),
                pl.BlockSpec((n // steps, d), lambda i, o, l: (i, 0)),
            ],
        ),
        out_shape=[pltpu.HBM((peers, BLOCK_ROWS, d), BF16), pltpu.VMEM((n, d), BF16)],
        compiler_params=params(8),
        name="unit_rows",
    )(owners, live, embeddings)


def column_sums(r_ref, c_ref, w_ref, at, tr):
    n = c_ref.shape[0]
    tc = min(TILE, n)
    out = []
    for c in range(0, n, tc):
        cents = c_ref[c : c + tc, :]
        total = jnp.zeros((8, tc), F32)
        for i in range(0, r_ref.shape[0], tr):
            p = lax.dot_general(r_ref[i : i + tr, :], cents, NT, preferred_element_type=F32)
            weights = jnp.exp2(p)
            w_ref[i : i + tr, at + c : at + c + tc] = weights.astype(BF16)
            total = total + weights.reshape(tr // 8, 8, tc).sum(0)
        out.append(jnp.sum(total, axis=0, keepdims=True))
    return out


def first_kernel(r_ref, *refs):
    pieces, (o_ref, w_ref) = refs[:-2], refs[-2:]
    at = 0
    for c_ref in pieces:
        for part in column_sums(r_ref, c_ref, w_ref, at, 256):
            o_ref[:, at : at + part.shape[1]] = part
            at += part.shape[1]


def first_sweep(scaled, pieces):
    total = sum(p.shape[0] for p in pieces)
    return pl.pallas_call(
        first_kernel,
        out_shape=[pltpu.VMEM((1, total), F32), pltpu.VMEM((scaled.shape[0], total), BF16)],
        compiler_params=params(8),
        cost_estimate=cost(scaled.shape[0], total, 1),
        name="first_sweep",
    )(in_vmem(scaled), *[in_vmem(p) for p in pieces])


def tile_lines(place_ref, lines):
    x, k = place_ref[0], place_ref[1]
    shard = lines // NX
    half = shard // NK
    out = []
    for dx in (0, -1, 1, 2):
        start = ((x + dx) & (NX - 1)) * shard
        for kk in (0, 1) if dx == 0 else (k, 1 - k):
            for quarter in range(0, half, TILE // 128):
                out.append((start + kk * half + quarter) ^ (k * (lines // NK)))
    return out


def last_kernel(place_ref, r_ref, *refs, n_new):
    pieces, ready, (keep_ref, give_ref, w_ref, buf) = refs[:n_new], refs[n_new:-4], refs[-4:]
    parts = [ref[:, j : j + TILE] for ref in ready for j in range(0, ref.shape[1], TILE)]
    at = 0
    for c_ref in pieces:
        parts += column_sums(r_ref, c_ref, w_ref, at, 256)
        at += c_ref.shape[0]
    for at, part in zip(tile_lines(place_ref, buf.shape[0]), parts):
        for j in range(TILE // 128):
            buf[pl.ds(at + j, 1), :] = part[:, j * 128 : (j + 1) * 128]
    half = keep_ref.shape[0]
    keep_ref[...] = buf[:half, :]
    give_ref[...] = buf[half:, :]


def last_sweep(place, scaled, pieces, ready):
    new = sum(p.shape[0] for p in pieces)
    total = new + sum(p.shape[1] for p in ready)
    vmem = pl.BlockSpec(memory_space=pltpu.VMEM)
    half = total // 128 // NK
    return pl.pallas_call(
        functools.partial(last_kernel, n_new=len(pieces)),
        in_specs=[pl.BlockSpec(memory_space=pltpu.SMEM)] + [vmem] * (1 + len(pieces) + len(ready)),
        out_specs=[vmem] * 3,
        out_shape=[pltpu.VMEM((half, 128), F32)] * 2
        + [pltpu.VMEM((scaled.shape[0], new), BF16)],
        scratch_shapes=[pltpu.VMEM((NK * half, 128), F32)],
        compiler_params=params(8),
        cost_estimate=cost(scaled.shape[0], new, 1),
        name="last_sweep",
    )(place, *[in_vmem(p) for p in (scaled, *pieces, *ready)])


def lane_sum(x):
    parts = [x[:, j : j + 128] for j in range(0, x.shape[1], 128)]
    while len(parts) > 1:
        parts = [parts[i] + parts[i + 1] for i in range(0, len(parts), 2)]
    return parts[0]


def second_kernel(
    place_ref, owner_ref, live_ref, r_ref, mine_ref, other_ref, *refs, n_pieces, n_weights, tr, ratio
):
    pieces, stored = refs[:n_pieces], refs[n_pieces : n_pieces + n_weights]
    keep_ref, sent_ref, give_ref, *scratch = refs[n_pieces + n_weights :]
    line_scr, score_scr, b_scr, low_scr, s_scr, i_scr = scratch
    rows = r_ref.shape[0]
    cents = [ref.at[j : j + TILE] for ref in pieces for j in range(0, ref.shape[0], TILE)]
    tiles = [(ref, j) for ref in stored for j in range(0, ref.shape[1], TILE)]
    starts = tile_lines(place_ref, line_scr.shape[0])
    lanes = TILE // 128
    half = mine_ref.shape[0]
    line_scr[:half, :] = ratio / mine_ref[...]
    line_scr[half:, :] = ratio / other_ref[...]
    for i in range(len(tiles)):
        for j in range(lanes):
            at = (i * lanes + j) * 128
            b_scr[:, at : at + 128] = line_scr[pl.ds(starts[i] + j, 1), :]
    low_scr[...] = jnp.broadcast_to(b_scr[...], low_scr.shape).astype(BF16)
    width = 256
    rg = 16

    def body(t, carry):
        row = pl.multiple_of(t * tr, tr)
        mixed = jnp.zeros((tr, r_ref.shape[1]), F32)
        for i, (ref, j) in enumerate(tiles):
            here = slice(i * TILE, (i + 1) * TILE)
            e = ref[pl.ds(row, tr), j : j + TILE] * low_scr[0:1, here]
            for g in range(0, tr, rg):
                part = lane_sum(e[g : g + rg].astype(F32))
                if i == 0:
                    s_scr[g : g + rg] = part
                else:
                    s_scr[g : g + rg] += part
            mixed = mixed + lax.dot_general(e, cents[i][...], NN, preferred_element_type=F32)
        weighted = lane_sum(mixed * r_ref[pl.ds(row, tr), :].astype(F32))
        for g in range(0, tr, width):
            inverse = 1.0 / jnp.sum(s_scr[g : g + width].T, axis=0, keepdims=True)
            score = jnp.sum(weighted[g : g + width].T, axis=0, keepdims=True) * inverse
            score_scr[pl.ds(t * (tr // width) + g // width, 1), :] = score * (1.0 / LOG2E)
            high = inverse.astype(BF16)
            low = (inverse - high.astype(F32)).astype(BF16)
            i_scr[:, pl.ds(pl.multiple_of(row + g, width), width)] = jnp.concatenate(
                [high, low, jnp.zeros((14, width), BF16)], axis=0
            )
        return carry

    lax.fori_loop(0, rows // tr, body, 0)
    for i, (ref, j) in enumerate(tiles):
        part = lax.dot_general(i_scr[...], ref[:, j : j + TILE], NN, preferred_element_type=F32)
        line = (part[0:1] + part[1:2]) * b_scr[:, i * TILE : (i + 1) * TILE]
        for j in range(lanes):
            line_scr[pl.ds(starts[i] + j, 1), :] = line[:, j * 128 : (j + 1) * 128]
    keep_ref[...] = line_scr[:half, :]
    give_ref[:half, :] = line_scr[half:, :]
    blocks = rows // BLOCK_ROWS
    peers = NZ * NY
    line_scr[: NK * peers, :] = jnp.zeros((NK * peers, BLOCK_ROWS), F32)
    for b in range(blocks):
        at = b % 2 * BLOCK_ROWS

        @pl.when(b < live_ref[0])
        def _():
            score = score_scr[b // 2 : b // 2 + 1, at : at + BLOCK_ROWS]
            owner = owner_ref[b]
            to = ((owner ^ place_ref[1]) & (NK - 1)) * peers + (owner >> 1)
            line_scr[pl.ds(to, 1), :] = score.astype(BF16).astype(F32)

    sent_ref[...] = line_scr[:peers, :]
    give_ref[half:, :] = line_scr[peers : NK * peers, :]


def second_sweep(place, owners, live, scaled, mine, other, pieces, weights, ratio):
    rows = scaled.shape[0]
    total = sum(p.shape[0] for p in pieces)
    tr = ROW_TILE
    half = mine.shape[0]
    peers = NZ * NY
    vmem = pl.BlockSpec(memory_space=pltpu.VMEM)
    smem = pl.BlockSpec(memory_space=pltpu.SMEM)
    kernel = functools.partial(
        second_kernel, n_pieces=len(pieces), n_weights=len(weights), tr=tr, ratio=ratio
    )
    return pl.pallas_call(
        kernel,
        in_specs=[smem] * 3 + [vmem] * (3 + len(pieces) + len(weights)),
        out_specs=[vmem, vmem, vmem],
        out_shape=[
            pltpu.VMEM((half, 128), F32),
            pltpu.VMEM((peers, BLOCK_ROWS), F32),
            pltpu.VMEM((half + peers, 128), F32),
        ],
        scratch_shapes=[
            pltpu.VMEM((total // 128, 128), F32),
            pltpu.VMEM((rows // 256, 256), F32),
            pltpu.VMEM((1, total), F32),
            pltpu.VMEM((16, total), BF16),
            pltpu.VMEM((tr, 128), F32),
            pltpu.VMEM((16, rows), BF16),
        ],
        compiler_params=params(10),
        cost_estimate=cost(rows, total, 3),
        name="second_sweep",
    )(
        place,
        owners,
        live,
        in_vmem(scaled),
        mine,
        other,
        *[in_vmem(p) for p in pieces],
        *[in_vmem(w) for w in weights],
    )


def place_kernel(in_ref, out_ref, buf, sems):
    steps = sems.shape[1]
    size = in_ref.shape[0] // steps
    loads, stores = [], []
    for i in range(steps):
        part = pl.ds(i * size, size)
        loads.append(pltpu.make_async_copy(in_ref.at[part], buf.at[part], sems.at[0, i]))
        stores.append(pltpu.make_async_copy(buf.at[part], out_ref.at[part], sems.at[1, i]))
        loads[-1].start()
    for load, store in zip(loads, stores):
        load.wait()
        store.start()
    for store in stores:
        store.wait()


def place_rows(arrived):
    return pl.pallas_call(
        place_kernel,
        in_specs=[pl.BlockSpec(memory_space=pl.ANY)],
        out_specs=pl.BlockSpec(memory_space=pl.ANY),
        out_shape=pltpu.HBM(arrived.shape, BF16),
        scratch_shapes=[pltpu.VMEM(arrived.shape, BF16), pltpu.SemaphoreType.DMA((2, 4))],
        compiler_params=params(8),
        cost_estimate=pl.CostEstimate(flops=0, transcendentals=0, bytes_accessed=2**23),
        name="place_rows",
    )(in_hbm(arrived))


def pack_kernel(k_ref, col_ref, a_ref, b_ref, c_ref, sent_ref, got_ref, out_ref):
    half = col_ref.shape[0]
    peers = sent_ref.shape[0]
    out_ref[:, :half, :] = jnp.broadcast_to(
        (col_ref[...] + a_ref[...] + (b_ref[...] + c_ref[...]))[None], (peers, half, 128)
    )
    out_ref[:, half:, :] = jnp.zeros((peers, out_ref.shape[1] - half, 128), F32)
    k = k_ref[1]
    for i in range(peers):
        out_ref[i, pl.ds(half + k, 1), :] = sent_ref[i : i + 1, :]
        out_ref[i, pl.ds(half + 1 - k, 1), :] = got_ref[half + i : half + i + 1, :]


def pack(k, column, arrived, sent, got):
    half, peers = column.shape[0], sent.shape[0]
    vmem = pl.BlockSpec(memory_space=pltpu.VMEM)
    return pl.pallas_call(
        pack_kernel,
        in_specs=[pl.BlockSpec(memory_space=pltpu.SMEM)] + [vmem] * 6,
        out_specs=vmem,
        out_shape=jax.ShapeDtypeStruct((peers, half + 8, 128), F32),
        compiler_params=params(4),
        name="pack",
    )(k, column, *arrived, sent, got)


def finish_kernel(k_ref, mine_ref, other_ref, all_ref, bal_ref, out_ref, *, scale):
    half = mine_ref.shape[0]
    k = k_ref[1]
    bal_ref[pl.ds(pl.multiple_of(k * half, half), half), :] = mine_ref[...] * scale
    bal_ref[pl.ds(pl.multiple_of((1 - k) * half, half), half), :] = other_ref[...] * scale
    peers = all_ref.shape[0]
    scores = jnp.concatenate([all_ref[i, half : half + NK, :] for i in range(peers)], axis=0)
    out_ref[...] = scores.astype(BF16)


def finish(k, mine, other, everything, scale):
    half, peers = mine.shape[0], everything.shape[0]
    vmem = pl.BlockSpec(memory_space=pltpu.VMEM)
    return pl.pallas_call(
        functools.partial(finish_kernel, scale=scale),
        in_specs=[pl.BlockSpec(memory_space=pltpu.SMEM), vmem, vmem, vmem],
        out_specs=[vmem, vmem],
        out_shape=[
            jax.ShapeDtypeStruct((NK * half, 128), F32),
            jax.ShapeDtypeStruct((NK * peers, BLOCK_ROWS), BF16),
        ],
        compiler_params=params(4),
        name="finish",
    )(k, mine, other, everything)


def x_parts(values):
    return [lax.ppermute(values, "cent", x_perm(s)) for s in (1, 3, 2)]


def plane_exchange(blocks):
    groups = [[(z * NY + y) * NK + k for z in range(NZ) for y in range(NY)] for k in range(NK)]
    return lax.all_to_all(
        blocks, "rows", split_axis=0, concat_axis=0, tiled=True, axis_index_groups=groups
    )


def local(embeddings, centroids, owners, live_blocks):
    x = lax.axis_index("cent")
    row_place = lax.axis_index("rows")
    k = row_place & (NK - 1)
    n_cent, d = centroids.shape
    half = n_cent // NK
    rows = embeddings.shape[0]
    peers = NZ * NY * NK
    total = n_cent * NX

    place = jnp.stack([x, k]).astype(jnp.int32)
    own, mine = unit_cents(place, centroids)
    right = lax.ppermute(mine, "cent", x_perm(1))
    left = lax.ppermute(mine, "cent", x_perm(-1))
    embeddings, mine = lax.optimization_barrier((embeddings, mine))
    outgoing, scaled = unit_rows(owners, live_blocks, embeddings, peers)
    arrived = lax.all_to_all(outgoing, "rows", split_axis=0, concat_axis=0, tiled=True)
    right, left, scaled = lax.optimization_barrier((right, left, scaled))
    swap = rows_perm(0, 0, 1)
    far = [lax.ppermute(t, "cent", x_perm(s)) for t, s in zip(forward_parts(right, left), (1, -1))]
    right = [right, lax.ppermute(right, "rows", swap)]
    left = [left, lax.ppermute(left, "rows", swap)]
    sums_own, w_own = first_sweep(scaled, [own])
    sums_right, w_right = first_sweep(scaled, right)
    sums_left, w_left = first_sweep(scaled, left)
    far, sums_own, sums_right, sums_left = lax.optimization_barrier(
        (far, sums_own, sums_right, sums_left)
    )
    far += [lax.ppermute(t, "rows", swap) for t in far]
    sums_far, w_far = first_sweep(scaled, far[:2])

    ready = [sums_own, sums_right, sums_left, sums_far]
    keep, give, w_last = last_sweep(place, scaled, far[2:], ready)
    keep = keep + lax.ppermute(give, "rows", swap)
    for part in x_parts(keep):
        keep = keep + part
    for dz, dy in ((0, 1), (1, 0)):
        for part in [lax.ppermute(keep, "rows", rows_perm(dz * s, dy * s, 0)) for s in (1, 3, 2)]:
            keep = keep + part
    other = lax.ppermute(keep, "rows", swap)

    ratio = float(rows * NX * peers) / total
    pieces = [own, *right, *left, *far]
    weights = [w_own, w_right, w_left, w_far, w_last]
    column, sent, give = second_sweep(
        place, owners, live_blocks, scaled, keep, other, pieces, weights, ratio
    )
    sent, arrived = lax.optimization_barrier((sent, arrived))
    moved = place_rows(arrived)
    sent, moved = lax.optimization_barrier((sent, moved))
    got = lax.ppermute(give, "rows", swap)
    column = column + got[: column.shape[0]]
    everything = plane_exchange(pack(place, column, x_parts(column), sent, got))
    column = everything[:, : column.shape[0]].sum(0)
    other = lax.ppermute(column, "rows", swap)
    balance, moved_score = finish(place, column, other, everything, 1.0 / ratio)
    return moved.reshape(peers * BLOCK_ROWS, d), moved_score.reshape(-1), balance.reshape(-1)


def solution(mesh):
    placed = (P(("rows", "cent"), None), P("cent", None), P(("rows", "cent")), P(("rows", "cent")))
    return jax.shard_map(
        local,
        mesh=mesh,
        in_specs=placed,
        out_specs=(P(("rows", "cent"), None), P(("rows", "cent")), P()),
        check_vma=False,
    )
```

time: 110 us -> 107 us (0.973)
  blocking collectives: 23.7 us -> 10.6 us
  starting transfers between devices: 31.1 us -> 40.7 us
  Pallas kernels: 40.5 us -> 37.5 us
  local copies, waits for them, and re-layouts: 0.12 us -> 2.25 us
  waiting for transfers between devices: 12.6 us -> 13.9 us
    all_to_all x2 -> x1, blocking collectives: 23.7 us -> 10.6 us  [plane_exchange(): lax.all_to_all(blocks, 'rows', split_axis=0, concat_axis=0, tiled=True, a...]
    ppermute x0 -> x6, starting transfers between devices: none -> 8.68 us  [local(): lax.ppermute(keep, 'rows', rows_perm(dz * s, dy * s, 0))]
    ppermute x0 -> x6, waiting for transfers between devices: none -> 6.12 us  [local(): lax.ppermute(keep, 'rows', rows_perm(dz * s, dy * s, 0))]
    pallas_call x6, Pallas kernels: 32.1 us -> 28.1 us  [the longest x1 17.2 us: second_sweep(): pl.pallas_call(kernel, in_specs=[smem] * 3 + [vmem] * (3 + len(pieces) +...]
    unnamed x8 -> x6, local copies, waits for them, and re-layouts: 0.02 us -> 2.25 us
    all_to_all x1, waiting for transfers between devices: 1.92 us -> 0.01 us  [local(): lax.all_to_all(outgoing, 'rows', split_axis=0, concat_axis=0, tiled=True)]
    ppermute x1, starting transfers between devices: 3.33 us -> 5.23 us  [local(): other = lax.ppermute(keep, 'rows', swap)]
    ppermute x6, waiting for transfers between devices: 5.92 us -> 4.32 us  [x_parts(): return [lax.ppermute(values, 'cent', x_perm(s)) for s in (1, 3, 2)]]
  transfers between devices with their start and end apart: 19 -> 25, of which waited for: 11 -> 11; matrix products, arithmetic and copies ran while one was open for 0% -> 0% of each run, Pallas kernels for 13% -> 31%
where the time goes in v4:
time: 107 us
  starting transfers between devices  40.7 us (38%)
  Pallas kernels  37.5 us (35%)
  waiting for transfers between devices  13.9 us (13%)
  blocking collectives  10.6 us (10%)
  local copies, waits for them, and re-layouts  2.25 us (2%)
  between operations  1.48 us (1%)
    pallas_call x1, Pallas kernels, second_sweep(): pl.pallas_call(kernel, in_specs=[smem] * 3 + [vmem] * (3 + len(pieces) +...  17.2 us
    all_to_all x1, blocking collectives, plane_exchange(): lax.all_to_all(blocks, 'rows', split_axis=0, concat_axis=0, tiled=True, a...  10.6 us
    all_to_all x1, starting transfers between devices, local(): lax.all_to_all(outgoing, 'rows', split_axis=0, concat_axis=0, tiled=True)  9.11 us
    ppermute x6, starting transfers between devices, local(): lax.ppermute(keep, 'rows', rows_perm(dz * s, dy * s, 0))  8.68 us
    pallas_call x4, Pallas kernels, first_sweep(): pl.pallas_call(first_kernel, out_shape=[pltpu.VMEM((1, total), F32), pltp...  8.55 us
    ppermute x6, waiting for transfers between devices, local(): lax.ppermute(keep, 'rows', rows_perm(dz * s, dy * s, 0))  6.12 us
    ppermute x6, starting transfers between devices, x_parts(): return [lax.ppermute(values, 'cent', x_perm(s)) for s in (1, 3, 2)]  5.26 us
    ppermute x1, starting transfers between devices, local(): other = lax.ppermute(keep, 'rows', swap)  5.23 us
  transfers between devices with their start and end apart: 25, of which 11 were waited for; matrix products, arithmetic and copies ran while one was open for 0% of the time, Pallas kernels for 31%

profile of v4, /device:TPU:1, one launch (start us, length us, event | category | flops | bytes accessed | tf_op | source)
XLA Modules:
  0.0 106.5 jit_solution(2634184506264599283)
XLA Ops:
  0.7 2.9 %unit_cents.1 = (bf16[2048,256]{1,0:T(8,128)(2,1)S(1)}, bf16[1024,256]{1,0:T(8,128)(2,1)}) custom-call(s32[2]{0:T(128)S(1)} %pad_add_fusion.place_ref.k_ref, f32[2048,256]{1,0:T(8,128)} %c_ref.1), custom_call_target="tpu_custom_call" | custom-call | tf_op jit(solution)/shard_map/unit_cents/pallas_call | solution.py:79
  3.6 3.4 %collective-permute-start.1 = (bf16[1024,256]{1,0:T(8,128)(2,1)}, bf16[1024,256]{1,0:T(8,128)(2,1)S(1)}, u32[]{:S(2)}, u32[]{:S(2)}) collective-permute-start(bf16[1024,256]{1,0:T(8,128)(2,1)} %get-tuple-element.38), channel_id=1, source_target_pairs={{0,3},{1,0},{2,1},{3,2},{4,7},{5,4},{6,5},{7,6},{8,11},{9,8},{10,9... | collective-permute-start | bytes 1572872 | tf_op jit(solution)/shard_map/ppermute | solution.py:458
  7.7 1.6 %copy-done = f32[2048,256]{1,0:T(8,128)S(1)} copy-done((f32[2048,256]{1,0:T(8,128)S(1)}, f32[2048,256]{1,0:T(8,128)}, u32[]{:S(2)}) %copy-start) | copy-done | bytes 2097176
  9.9 2.8 %unit_rows.1 = (bf16[32,128,256]{2,1,0:T(8,128)(2,1)}, bf16[2048,256]{1,0:T(8,128)(2,1)S(1)}) custom-call(s32[16]{0:T(128)S(1)} %copy-done.1, s32[1]{0:T(128)S(6)} %copy.7.live_ref, f32[2048,256]{1,0:T(8,128)S(1)} %copy-done), custom_call_target="tpu_custom_call" | custom-call | tf_op jit(solution)/shard_map/unit_rows/pallas_call | solution.py:132
  12.7 9.1 %all-to-all-start = ((bf16[32,128,256]{2,1,0:T(8,128)(2,1)}), bf16[32,128,256]{2,1,0:T(8,128)(2,1)}, u32[]{:S(2)}, u32[]{:S(2)}) async-start(bf16[32,128,256]{2,1,0:T(8,128)(2,1)} %get-tuple-element.64), calls=%async_computation | async-start | bytes 4194304 | tf_op jit(solution)/shard_map/all_to_all | solution.py:461
  23.0 2.6 %collective-permute-start.3 = (bf16[512,256]{1,0:T(8,128)(2,1)S(1)}, bf16[512,256]{1,0:T(8,128)(2,1)S(1)}, u32[]{:S(2)}, u32[]{:S(2)}) collective-permute-start(bf16[512,256]{1,0:T(8,128)(2,1)S(1)} %get-tuple-element.45), channel_id=1, source_target_pairs={{0,3},{1,0},{2,1},{3,2},{4,7},{5,4},{6,5},{7,6},{8,11},{9,8},{10,9... | collective-permute-start | bytes 786440 | tf_op jit(solution)/shard_map/ppermute | solution.py:464
  25.6 2.4 %first_sweep.4 = (f32[1,2048]{1,0:T(1,128)S(1)}, bf16[2048,2048]{1,0:T(8,128)(2,1)S(1)}) custom-call(bf16[2048,256]{1,0:T(8,128)(2,1)S(1)} %get-tuple-element.41.r_ref, bf16[2048,256]{1,0:T(8,128)(2,1)S(1)} %get-tuple-element.46.refs_0_), custom_call_target="tpu_custom_call" | custom-call | flops 2048 | bytes 2048 | tf_op jit(solution)/shard_map/first_sweep/pallas_call | solution.py:176
  28.0 2.4 %first_sweep.6 = (f32[1,2048]{1,0:T(1,128)S(1)}, bf16[2048,2048]{1,0:T(8,128)(2,1)S(1)}) custom-call(bf16[2048,256]{1,0:T(8,128)(2,1)S(1)} %get-tuple-element.41.r_ref, bf16[1024,256]{1,0:T(8,128)(2,1)S(1)} %collective-permute-done.1.left_ref.refs_0_.refs_3_, bf16[1024,256]{1,0:T(8,128)(2,1)S(1)} %collective-permute-done.5.refs_1_.refs_4_), custom_call_target="tpu_custom_call" | custom-call | flops 2048 | bytes 2048 | tf_op jit(solution)/shard_map/first_sweep/pallas_call | solution.py:176
  30.5 2.4 %first_sweep.5 = (f32[1,2048]{1,0:T(1,128)S(1)}, bf16[2048,2048]{1,0:T(8,128)(2,1)S(1)}) custom-call(bf16[2048,256]{1,0:T(8,128)(2,1)S(1)} %get-tuple-element.41.r_ref, bf16[1024,256]{1,0:T(8,128)(2,1)S(1)} %collective-permute-done.right_ref.refs_0_.refs_1_, bf16[1024,256]{1,0:T(8,128)(2,1)S(1)} %collective-permute-done.4.refs_1_.refs_2_), custom_call_target="tpu_custom_call" | custom-call | flops 2048 | bytes 2048 | tf_op jit(solution)/shard_map/first_sweep/pallas_call | solution.py:176
  34.3 1.3 %first_sweep.7 = (f32[1,1024]{1,0:T(1,128)S(1)}, bf16[2048,1024]{1,0:T(8,128)(2,1)S(1)}) custom-call(bf16[2048,256]{1,0:T(8,128)(2,1)S(1)} %get-tuple-element.41.r_ref, bf16[512,256]{1,0:T(8,128)(2,1)S(1)} %collective-permute-done.2.refs_0_.refs_5_, bf16[512,256]{1,0:T(8,128)(2,1)S(1)} %collective-permute-done.3.refs_1_.refs_6_), custom_call_target="tpu_custom_call" | custom-call | flops 2048 | bytes 1024 | tf_op jit(solution)/shard_map/first_sweep/pallas_call | solution.py:176
  35.6 1.9 %last_sweep.1 = (f32[32,128]{1,0:T(8,128)S(1)}, f32[32,128]{1,0:T(8,128)S(1)}, bf16[2048,1024]{1,0:T(8,128)(2,1)S(1)}) custom-call(s32[2]{0:T(128)S(1)} %pad_add_fusion.place_ref.k_ref, bf16[2048,256]{1,0:T(8,128)(2,1)S(1)} %get-tuple-element.41.r_ref, bf16[512,256]{1,0:T(8,128)(2,1)S(1)} %collective-permute-done.6.refs_0_.refs_7_, ...), custom_call_target="tpu_custom_call" | custom-call | flops 2048 | bytes 1024 | tf_op jit(solution)/shard_map/last_sweep/pallas_call | solution.py:218
  38.8 1.4 %collective-permute-start.11 = (f32[32,128]{1,0:T(8,128)S(1)}, f32[32,128]{1,0:T(8,128)S(1)}, u32[]{:S(2)}, u32[]{:S(2)}) collective-permute-start(f32[32,128]{1,0:T(8,128)S(1)} %add.33), channel_id=1, source_target_pairs={{0,2},{1,3},{2,0},{3,1},{4,6},{5,7},{6,4},{7,5},{8,10},{9,11},{10,... | collective-permute-start | bytes 49160 | tf_op jit(solution)/shard_map/ppermute | solution.py:435
  41.6 1.7 %collective-permute-done.11 = f32[32,128]{1,0:T(8,128)S(1)} collective-permute-done((f32[32,128]{1,0:T(8,128)S(1)}, f32[32,128]{1,0:T(8,128)S(1)}, u32[]{:S(2)}, u32[]{:S(2)}) %collective-permute-start.11) | collective-permute-done | bytes 16416 | tf_op jit(solution)/shard_map/ppermute | solution.py:435
  43.3 1.7 %collective-permute-done.9 = f32[32,128]{1,0:T(8,128)S(1)} collective-permute-done((f32[32,128]{1,0:T(8,128)S(1)}, f32[32,128]{1,0:T(8,128)S(1)}, u32[]{:S(2)}, u32[]{:S(2)}) %collective-permute-start.9) | collective-permute-done | bytes 16416 | tf_op jit(solution)/shard_map/ppermute | solution.py:435
  45.0 2.9 %collective-permute-start.14 = (f32[32,128]{1,0:T(8,128)S(1)}, f32[32,128]{1,0:T(8,128)S(1)}, u32[]{:S(2)}, u32[]{:S(2)}) collective-permute-start(f32[32,128]{1,0:T(8,128)S(1)} %add_add_fusion.2), channel_id=1, source_target_pairs={{0,16},{4,20},{8,24},{12,28},{16,0},{20,4},{24,8},{28,12},{32,48},... | collective-permute-start | bytes 49160 | tf_op jit(solution)/shard_map/ppermute | solution.py:482
  49.3 1.5 %collective-permute-done.13 = f32[32,128]{1,0:T(8,128)S(1)} collective-permute-done((f32[32,128]{1,0:T(8,128)S(1)}, f32[32,128]{1,0:T(8,128)S(1)}, u32[]{:S(2)}, u32[]{:S(2)}) %collective-permute-start.13) | collective-permute-done | bytes 16416 | tf_op jit(solution)/shard_map/ppermute | solution.py:482
  50.8 1.7 %collective-permute-done.12 = f32[32,128]{1,0:T(8,128)S(1)} collective-permute-done((f32[32,128]{1,0:T(8,128)S(1)}, f32[32,128]{1,0:T(8,128)S(1)}, u32[]{:S(2)}, u32[]{:S(2)}) %collective-permute-start.12) | collective-permute-done | bytes 16416 | tf_op jit(solution)/shard_map/ppermute | solution.py:482
  52.5 2.9 %collective-permute-start.17 = (f32[32,128]{1,0:T(8,128)S(1)}, f32[32,128]{1,0:T(8,128)S(1)}, u32[]{:S(2)}, u32[]{:S(2)}) collective-permute-start(f32[32,128]{1,0:T(8,128)S(1)} %add_add_fusion.1), channel_id=1, source_target_pairs={{0,64},{4,68},{8,72},{12,76},{16,80},{20,84},{24,88},{28,92},{32,9... | collective-permute-start | bytes 49160 | tf_op jit(solution)/shard_map/ppermute | solution.py:482
  58.0 1.8 %collective-permute-done.15 = f32[32,128]{1,0:T(8,128)S(1)} collective-permute-done((f32[32,128]{1,0:T(8,128)S(1)}, f32[32,128]{1,0:T(8,128)S(1)}, u32[]{:S(2)}, u32[]{:S(2)}) %collective-permute-start.15) | collective-permute-done | bytes 16416 | tf_op jit(solution)/shard_map/ppermute | solution.py:482
  59.8 5.2 %collective-permute-start.18 = (f32[32,128]{1,0:T(8,128)S(1)}, f32[32,128]{1,0:T(8,128)S(1)}, u32[]{:S(2)}, u32[]{:S(2)}) collective-permute-start(f32[32,128]{1,0:T(8,128)S(1)} %add_add_fusion.mine_ref), channel_id=1, source_target_pairs={{0,4},{4,0},{8,12},{12,8},{16,20},{20,16},{24,28},{28,24},{32,36},... | collective-permute-start | bytes 49160 | tf_op jit(solution)/shard_map/ppermute | solution.py:484
  65.8 17.2 %second_sweep.1 = (f32[32,128]{1,0:T(8,128)S(1)}, f32[16,128]{1,0:T(8,128)S(1)}, f32[48,128]{1,0:T(8,128)S(1)}) custom-call(s32[2]{0:T(128)S(1)} %pad_add_fusion.place_ref.k_ref, s32[16]{0:T(128)S(1)} %copy-done.2, s32[1]{0:T(128)S(6)} %copy.7.live_ref, bf16[2048,256]{1,0:T(8,128)(2,1)S(1)} %get-tuple-element.41.r_ref, f32[32,128]{1,0:T(8,128)S(1)} %add_add_fusion.mine_ref, ...), custom_call_target="tpu_custom_call" | custom-call | flops 6144 | bytes 8192 | tf_op jit(solution)/shard_map/second_sweep/pallas_call | solution.py:321
  86.7 2.4 %place_rows.1 = bf16[32,128,256]{2,1,0:T(8,128)(2,1)} custom-call(bf16[32,128,256]{2,1,0:T(8,128)(2,1)} %all-to-all-done.in_ref), custom_call_target="tpu_custom_call" | custom-call | bytes 8388608 | tf_op jit(solution)/shard_map/place_rows/pallas_call | solution.py:370
  90.7 10.6 %all_to_all.10.all_ref = f32[16,40,128]{2,1,0:T(8,128)S(1)} all-to-all(f32[16,40,128]{2,1,0:T(8,128)S(1)} %pack.1), channel_id=1, replica_groups={{0,8,16,24,32,40,48,56,64,72,80,88,96,104,112,120},{4,12,20,28,36,44,52..., dimensions={0} | all-to-all | bytes 655360 | tf_op jit(solution)/shard_map/all_to_all | solution.py:440
  101.4 3.2 %collective-permute-start.23 = (f32[32,128]{1,0:T(8,128)S(1)}, f32[32,128]{1,0:T(8,128)S(1)}, u32[]{:S(2)}, u32[]{:S(2)}) collective-permute-start(f32[32,128]{1,0:T(8,128)S(1)} %slice_reduce_fusion.mine_ref), channel_id=1, source_target_pairs={{0,4},{4,0},{8,12},{12,8},{16,20},{20,16},{24,28},{28,24},{32,36},... | collective-permute-start | bytes 49160 | tf_op jit(solution)/shard_map/ppermute | solution.py:499
  (52 shorter events, 18.2 us)
Async XLA Ops:
  3.6 18.2 %collective-permute-start.1 = (bf16[1024,256]{1,0:T(8,128)(2,1)}, bf16[1024,256]{1,0:T(8,128)(2,1)S(1)}, u32[]{:S(2)}, u32[]{:S(2)}) collective-permute-start(bf16[1024,256]{1,0:T(8,128)(2,1)} %get-tuple-element.38), channel_id=1, source_target_pairs={{0,3},{1,0},{2,1},{3,2},{4,7},{5,4},{6,5},{7,6},{8,11},{9,8},{10,9... | collective-permute-start | bytes 1572872 | tf_op jit(solution)/shard_map/ppermute | solution.py:458
  7.0 14.8 %collective-permute-start = (bf16[1024,256]{1,0:T(8,128)(2,1)}, bf16[1024,256]{1,0:T(8,128)(2,1)S(1)}, u32[]{:S(2)}, u32[]{:S(2)}) collective-permute-start(bf16[1024,256]{1,0:T(8,128)(2,1)} %get-tuple-element.38), channel_id=1, source_target_pairs={{0,1},{1,2},{2,3},{3,0},{4,5},{5,6},{6,7},{7,4},{8,9},{9,10},{10,1... | collective-permute-start | bytes 1572872 | tf_op jit(solution)/shard_map/ppermute | solution.py:457
  12.7 74.0 %all-to-all-start = ((bf16[32,128,256]{2,1,0:T(8,128)(2,1)}), bf16[32,128,256]{2,1,0:T(8,128)(2,1)}, u32[]{:S(2)}, u32[]{:S(2)}) async-start(bf16[32,128,256]{2,1,0:T(8,128)(2,1)} %get-tuple-element.64), calls=%async_computation | async-start | bytes 4194304 | tf_op jit(solution)/shard_map/all_to_all | solution.py:461
  21.9 8.6 %collective-permute-start.4 = (bf16[1024,256]{1,0:T(8,128)(2,1)S(1)}, bf16[1024,256]{1,0:T(8,128)(2,1)S(1)}, u32[]{:S(2)}, u32[]{:S(2)}) collective-permute-start(bf16[1024,256]{1,0:T(8,128)(2,1)S(1)} %collective-permute-done.right_ref.refs_0_.refs_1_), channel_id=1, source_target_pairs={{0,4},{4,0},{8,12},{12,8},{16,20},{20,16},{24,28},{28,24},{32,36},... | collective-permute-start | bytes 1572872 | tf_op jit(solution)/shard_map/ppermute | solution.py:465
  22.8 5.3 %collective-permute-start.5 = (bf16[1024,256]{1,0:T(8,128)(2,1)S(1)}, bf16[1024,256]{1,0:T(8,128)(2,1)S(1)}, u32[]{:S(2)}, u32[]{:S(2)}) collective-permute-start(bf16[1024,256]{1,0:T(8,128)(2,1)S(1)} %collective-permute-done.1.left_ref.refs_0_.refs_3_), channel_id=1, source_target_pairs={{0,4},{4,0},{8,12},{12,8},{16,20},{20,16},{24,28},{28,24},{32,36},... | collective-permute-start | bytes 1572872 | tf_op jit(solution)/shard_map/ppermute | solution.py:466
  22.8 10.1 %collective-permute-start.2 = (bf16[512,256]{1,0:T(8,128)(2,1)S(1)}, bf16[512,256]{1,0:T(8,128)(2,1)S(1)}, u32[]{:S(2)}, u32[]{:S(2)}) collective-permute-start(bf16[512,256]{1,0:T(8,128)(2,1)S(1)} %get-tuple-element.44), channel_id=1, source_target_pairs={{0,1},{1,2},{2,3},{3,0},{4,5},{5,6},{6,7},{7,4},{8,9},{9,10},{10,1... | collective-permute-start | bytes 786440 | tf_op jit(solution)/shard_map/ppermute | solution.py:464
  23.0 9.9 %collective-permute-start.3 = (bf16[512,256]{1,0:T(8,128)(2,1)S(1)}, bf16[512,256]{1,0:T(8,128)(2,1)S(1)}, u32[]{:S(2)}, u32[]{:S(2)}) collective-permute-start(bf16[512,256]{1,0:T(8,128)(2,1)S(1)} %get-tuple-element.45), channel_id=1, source_target_pairs={{0,3},{1,0},{2,1},{3,2},{4,7},{5,4},{6,5},{7,6},{8,11},{9,8},{10,9... | collective-permute-start | bytes 786440 | tf_op jit(solution)/shard_map/ppermute | solution.py:464
  32.9 2.7 %collective-permute-start.6 = (bf16[512,256]{1,0:T(8,128)(2,1)S(1)}, bf16[512,256]{1,0:T(8,128)(2,1)S(1)}, u32[]{:S(2)}, u32[]{:S(2)}) collective-permute-start(bf16[512,256]{1,0:T(8,128)(2,1)S(1)} %collective-permute-done.2.refs_0_.refs_5_), channel_id=1, source_target_pairs={{0,4},{4,0},{8,12},{12,8},{16,20},{20,16},{24,28},{28,24},{32,36},... | collective-permute-start | bytes 786440 | tf_op jit(solution)/shard_map/ppermute | solution.py:473
  34.0 1.6 %collective-permute-start.7 = (bf16[512,256]{1,0:T(8,128)(2,1)S(1)}, bf16[512,256]{1,0:T(8,128)(2,1)S(1)}, u32[]{:S(2)}, u32[]{:S(2)}) collective-permute-start(bf16[512,256]{1,0:T(8,128)(2,1)S(1)} %collective-permute-done.3.refs_1_.refs_6_), channel_id=1, source_target_pairs={{0,4},{4,0},{8,12},{12,8},{16,20},{20,16},{24,28},{28,24},{32,36},... | collective-permute-start | bytes 786440 | tf_op jit(solution)/shard_map/ppermute | solution.py:473
  38.8 4.5 %collective-permute-start.11 = (f32[32,128]{1,0:T(8,128)S(1)}, f32[32,128]{1,0:T(8,128)S(1)}, u32[]{:S(2)}, u32[]{:S(2)}) collective-permute-start(f32[32,128]{1,0:T(8,128)S(1)} %add.33), channel_id=1, source_target_pairs={{0,2},{1,3},{2,0},{3,1},{4,6},{5,7},{6,4},{7,5},{8,10},{9,11},{10,... | collective-permute-start | bytes 49160 | tf_op jit(solution)/shard_map/ppermute | solution.py:435
  40.1 3.1 %collective-permute-start.10 = (f32[32,128]{1,0:T(8,128)S(1)}, f32[32,128]{1,0:T(8,128)S(1)}, u32[]{:S(2)}, u32[]{:S(2)}) collective-permute-start(f32[32,128]{1,0:T(8,128)S(1)} %add.33), channel_id=1, source_target_pairs={{0,3},{1,0},{2,1},{3,2},{4,7},{5,4},{6,5},{7,6},{8,11},{9,8},{10,9... | collective-permute-start | bytes 49160 | tf_op jit(solution)/shard_map/ppermute | solution.py:435
  40.7 4.2 %collective-permute-start.9 = (f32[32,128]{1,0:T(8,128)S(1)}, f32[32,128]{1,0:T(8,128)S(1)}, u32[]{:S(2)}, u32[]{:S(2)}) collective-permute-start(f32[32,128]{1,0:T(8,128)S(1)} %add.33), channel_id=1, source_target_pairs={{0,1},{1,2},{2,3},{3,0},{4,5},{5,6},{6,7},{7,4},{8,9},{9,10},{10,1... | collective-permute-start | bytes 49160 | tf_op jit(solution)/shard_map/ppermute | solution.py:435
  45.0 4.4 %collective-permute-start.14 = (f32[32,128]{1,0:T(8,128)S(1)}, f32[32,128]{1,0:T(8,128)S(1)}, u32[]{:S(2)}, u32[]{:S(2)}) collective-permute-start(f32[32,128]{1,0:T(8,128)S(1)} %add_add_fusion.2), channel_id=1, source_target_pairs={{0,16},{4,20},{8,24},{12,28},{16,0},{20,4},{24,8},{28,12},{32,48},... | collective-permute-start | bytes 49160 | tf_op jit(solution)/shard_map/ppermute | solution.py:482
  47.8 3.0 %collective-permute-start.13 = (f32[32,128]{1,0:T(8,128)S(1)}, f32[32,128]{1,0:T(8,128)S(1)}, u32[]{:S(2)}, u32[]{:S(2)}) collective-permute-start(f32[32,128]{1,0:T(8,128)S(1)} %add_add_fusion.2), channel_id=1, source_target_pairs={{0,24},{4,28},{8,0},{12,4},{16,8},{20,12},{24,16},{28,20},{32,56},... | collective-permute-start | bytes 49160 | tf_op jit(solution)/shard_map/ppermute | solution.py:482
  48.7 3.8 %collective-permute-start.12 = (f32[32,128]{1,0:T(8,128)S(1)}, f32[32,128]{1,0:T(8,128)S(1)}, u32[]{:S(2)}, u32[]{:S(2)}) collective-permute-start(f32[32,128]{1,0:T(8,128)S(1)} %add_add_fusion.2), channel_id=1, source_target_pairs={{0,8},{4,12},{8,16},{12,20},{16,24},{20,28},{24,0},{28,4},{32,40},... | collective-permute-start | bytes 49160 | tf_op jit(solution)/shard_map/ppermute | solution.py:482
  52.5 4.3 %collective-permute-start.17 = (f32[32,128]{1,0:T(8,128)S(1)}, f32[32,128]{1,0:T(8,128)S(1)}, u32[]{:S(2)}, u32[]{:S(2)}) collective-permute-start(f32[32,128]{1,0:T(8,128)S(1)} %add_add_fusion.1), channel_id=1, source_target_pairs={{0,64},{4,68},{8,72},{12,76},{16,80},{20,84},{24,88},{28,92},{32,9... | collective-permute-start | bytes 49160 | tf_op jit(solution)/shard_map/ppermute | solution.py:482
  55.4 2.6 %collective-permute-start.16 = (f32[32,128]{1,0:T(8,128)S(1)}, f32[32,128]{1,0:T(8,128)S(1)}, u32[]{:S(2)}, u32[]{:S(2)}) collective-permute-start(f32[32,128]{1,0:T(8,128)S(1)} %add_add_fusion.1), channel_id=1, source_target_pairs={{0,96},{4,100},{8,104},{12,108},{16,112},{20,116},{24,120},{28,124... | collective-permute-start | bytes 49160 | tf_op jit(solution)/shard_map/ppermute | solution.py:482
  56.0 3.8 %collective-permute-start.15 = (f32[32,128]{1,0:T(8,128)S(1)}, f32[32,128]{1,0:T(8,128)S(1)}, u32[]{:S(2)}, u32[]{:S(2)}) collective-permute-start(f32[32,128]{1,0:T(8,128)S(1)} %add_add_fusion.1), channel_id=1, source_target_pairs={{0,32},{4,36},{8,40},{12,44},{16,48},{20,52},{24,56},{28,60},{32,6... | collective-permute-start | bytes 49160 | tf_op jit(solution)/shard_map/ppermute | solution.py:482
  59.8 6.1 %collective-permute-start.18 = (f32[32,128]{1,0:T(8,128)S(1)}, f32[32,128]{1,0:T(8,128)S(1)}, u32[]{:S(2)}, u32[]{:S(2)}) collective-permute-start(f32[32,128]{1,0:T(8,128)S(1)} %add_add_fusion.mine_ref), channel_id=1, source_target_pairs={{0,4},{4,0},{8,12},{12,8},{16,20},{20,16},{24,28},{28,24},{32,36},... | collective-permute-start | bytes 49160 | tf_op jit(solution)/shard_map/ppermute | solution.py:484
  83.0 1.3 %collective-permute-start.19 = (f32[48,128]{1,0:T(8,128)S(1)}, f32[48,128]{1,0:T(8,128)S(1)}, u32[]{:S(2)}, u32[]{:S(2)}) collective-permute-start(f32[48,128]{1,0:T(8,128)S(1)} %get-tuple-element.69), channel_id=1, source_target_pairs={{0,4},{4,0},{8,12},{12,8},{16,20},{20,16},{24,28},{28,24},{32,36},... | collective-permute-start | bytes 73736 | tf_op jit(solution)/shard_map/ppermute | solution.py:495
  84.3 4.9 %collective-permute-start.22 = (f32[32,128]{1,0:T(8,128)S(1)}, f32[32,128]{1,0:T(8,128)S(1)}, u32[]{:S(2)}, u32[]{:S(2)}) collective-permute-start(f32[32,128]{1,0:T(8,128)S(1)} %slice_add_fusion.col_ref), channel_id=1, source_target_pairs={{0,2},{1,3},{2,0},{3,1},{4,6},{5,7},{6,4},{7,5},{8,10},{9,11},{10,... | collective-permute-start | bytes 49160 | tf_op jit(solution)/shard_map/ppermute | solution.py:435
  85.3 3.9 %collective-permute-start.21 = (f32[32,128]{1,0:T(8,128)S(1)}, f32[32,128]{1,0:T(8,128)S(1)}, u32[]{:S(2)}, u32[]{:S(2)}) collective-permute-start(f32[32,128]{1,0:T(8,128)S(1)} %slice_add_fusion.col_ref), channel_id=1, source_target_pairs={{0,3},{1,0},{2,1},{3,2},{4,7},{5,4},{6,5},{7,6},{8,11},{9,8},{10,9... | collective-permute-start | bytes 49160 | tf_op jit(solution)/shard_map/ppermute | solution.py:435
  86.3 3.8 %collective-permute-start.20 = (f32[32,128]{1,0:T(8,128)S(1)}, f32[32,128]{1,0:T(8,128)S(1)}, u32[]{:S(2)}, u32[]{:S(2)}) collective-permute-start(f32[32,128]{1,0:T(8,128)S(1)} %slice_add_fusion.col_ref), channel_id=1, source_target_pairs={{0,1},{1,2},{2,3},{3,0},{4,5},{5,6},{6,7},{7,4},{8,9},{9,10},{10,1... | collective-permute-start | bytes 49160 | tf_op jit(solution)/shard_map/ppermute | solution.py:435
  101.4 4.0 %collective-permute-start.23 = (f32[32,128]{1,0:T(8,128)S(1)}, f32[32,128]{1,0:T(8,128)S(1)}, u32[]{:S(2)}, u32[]{:S(2)}) collective-permute-start(f32[32,128]{1,0:T(8,128)S(1)} %slice_reduce_fusion.mine_ref), channel_id=1, source_target_pairs={{0,4},{4,0},{8,12},{12,8},{16,20},{20,16},{24,28},{28,24},{32,36},... | collective-permute-start | bytes 49160 | tf_op jit(solution)/shard_map/ppermute | solution.py:499
  (4 other events, 41.4 us)

commit v5 on v4

--- a/solution.py
+++ b/solution.py
@@ -60,14 +60,14 @@
     half = buf.shape[1]
     copies = []
     for i in range(NK):
-        start = pl.multiple_of((place_ref[1] ^ i) * half, half)
+        start = pl.multiple_of(((place_ref[0] & 1) ^ i) * half, half)
         copies.append(pltpu.make_async_copy(c_ref.at[pl.ds(start, half), :], buf.at[i], sems.at[i]))
     for copy in copies:
         copy.start()
     for i, copy in enumerate(copies):
         copy.wait()
         unit = unit_f32(buf[i]).astype(BF16)
-        all_ref[pl.ds(pl.multiple_of((place_ref[1] ^ i) * half, half), half), :] = unit
+        all_ref[pl.ds(pl.multiple_of(((place_ref[0] & 1) ^ i) * half, half), half), :] = unit
         if i == 0:
             half_ref[...] = unit
 
@@ -107,43 +107,42 @@
     )(right, left)
 
 
-def rows_kernel(owner_ref, live_ref, e_ref, out_ref, scaled_ref):
-    step = pl.program_id(0)
-
-    @pl.when(step == 0)
-    def _():
-        out_ref[...] = jnp.zeros_like(out_ref)
-
-    unit = unit_f32(e_ref[...])
-    scaled_ref[...] = (unit * (SCALE * LOG2E)).astype(BF16)
-    low = unit.astype(BF16)
-    count = e_ref.shape[0] // BLOCK_ROWS
-    for b in range(count):
-        block = step * count + b
-
-        @pl.when(block < live_ref[0])
-        def _():
-            out_ref[owner_ref[block]] = low[b * BLOCK_ROWS : (b + 1) * BLOCK_ROWS]
+def rows_kernel(owner_ref, live_ref, e_ref, out_ref, scaled_ref, buf, sems):
+    steps = sems.shape[0]
+    size = buf.shape[0] // steps
+    copies = []
+    for i in range(steps):
+        part = pl.ds(i * size, size)
+        copies.append(pltpu.make_async_copy(e_ref.at[part, :], buf.at[part, :], sems.at[i]))
+        copies[-1].start()
+    out_ref[...] = jnp.zeros_like(out_ref)
+    for i, copy in enumerate(copies):
+        copy.wait()
+        unit = unit_f32(buf[i * size : (i + 1) * size, :])
+        scaled_ref[i * size : (i + 1) * size, :] = (unit * (SCALE * LOG2E)).astype(BF16)
+        low = unit.astype(BF16)
+        for b in range(size // BLOCK_ROWS):
+            block = i * (size // BLOCK_ROWS) + b
+
+            @pl.when(block < live_ref[0])
+            def _():
+                out_ref[owner_ref[block]] = low[b * BLOCK_ROWS : (b + 1) * BLOCK_ROWS]
 
 
 def unit_rows(owners, live, embeddings, peers):
     n, d = embeddings.shape
-    steps = 4
+    vmem = pl.BlockSpec(memory_space=pltpu.VMEM)
+    smem = pl.BlockSpec(memory_space=pltpu.SMEM)
+    whole = pl.BlockSpec((peers, BLOCK_ROWS, d), lambda: (0, 0, 0))
     return pl.pallas_call(
         rows_kernel,
-        grid_spec=pltpu.PrefetchScalarGridSpec(
-            num_scalar_prefetch=2,
-            grid=(steps,),
-            in_specs=[pl.BlockSpec((n // steps, d), lambda i, o, l: (i, 0))],
-            out_specs=[
-                pl.BlockSpec((peers, BLOCK_ROWS, d), lambda i, o, l: (0, 0, 0)),
-                pl.BlockSpec((n // steps, d), lambda i, o, l: (i, 0)),
-            ],
-        ),
+        in_specs=[smem, smem, pl.BlockSpec(memory_space=pl.ANY)],
+        out_specs=[whole, vmem],
         out_shape=[pltpu.HBM((peers, BLOCK_ROWS, d), BF16), pltpu.VMEM((n, d), BF16)],
-        compiler_params=params(8),
+        scratch_shapes=[pltpu.VMEM((n, d), F32), pltpu.SemaphoreType.DMA((4,))],
+        compiler_params=params(10),
         name="unit_rows",
-    )(owners, live, embeddings)
+    )(owners, live, in_hbm(embeddings))
 
 
 def column_sums(r_ref, c_ref, w_ref, at, tr):
@@ -183,7 +182,7 @@
 
 
 def tile_lines(place_ref, lines):
-    x, k = place_ref[0], place_ref[1]
+    x, k = place_ref[0] >> 1, place_ref[0] & 1
     shard = lines // NX
     half = shard // NK
     out = []
@@ -300,7 +299,7 @@
         def _():
             score = score_scr[b // 2 : b // 2 + 1, at : at + BLOCK_ROWS]
             owner = owner_ref[b]
-            to = ((owner ^ place_ref[1]) & (NK - 1)) * peers + (owner >> 1)
+            to = ((owner ^ place_ref[0]) & (NK - 1)) * peers + (owner >> 1)
             line_scr[pl.ds(to, 1), :] = score.astype(BF16).astype(F32)
 
     sent_ref[...] = line_scr[:peers, :]
@@ -386,7 +385,7 @@
         (col_ref[...] + a_ref[...] + (b_ref[...] + c_ref[...]))[None], (peers, half, 128)
     )
     out_ref[:, half:, :] = jnp.zeros((peers, out_ref.shape[1] - half, 128), F32)
-    k = k_ref[1]
+    k = k_ref[0] & 1
     for i in range(peers):
         out_ref[i, pl.ds(half + k, 1), :] = sent_ref[i : i + 1, :]
         out_ref[i, pl.ds(half + 1 - k, 1), :] = got_ref[half + i : half + i + 1, :]
@@ -407,7 +406,7 @@
 
 def finish_kernel(k_ref, mine_ref, other_ref, all_ref, bal_ref, out_ref, *, scale):
     half = mine_ref.shape[0]
-    k = k_ref[1]
+    k = k_ref[0] & 1
     bal_ref[pl.ds(pl.multiple_of(k * half, half), half), :] = mine_ref[...] * scale
     bal_ref[pl.ds(pl.multiple_of((1 - k) * half, half), half), :] = other_ref[...] * scale
     peers = all_ref.shape[0]
@@ -452,7 +451,7 @@
     peers = NZ * NY * NK
     total = n_cent * NX
 
-    place = jnp.stack([x, k]).astype(jnp.int32)
+    place = (x * NK + k).reshape(1).astype(jnp.int32)
     own, mine = unit_cents(place, centroids)
     right = lax.ppermute(mine, "cent", x_perm(1))
     left = lax.ppermute(mine, "cent", x_perm(-1))

time: 107 us -> 104 us (0.972)
  local copies, waits for them, and re-layouts: 2.25 us -> 0.66 us
  Pallas kernels: 37.5 us -> 36.2 us
    unnamed x6 -> x4, local copies, waits for them, and re-layouts: 2.25 us -> 0.66 us
  transfers between devices with their start and end apart: 25 -> 25, of which waited for: 11 -> 11; matrix products, arithmetic and copies ran while one was open for 0% -> 0% of each run, Pallas kernels for 31% -> 32%
where the time goes in v5:
time: 104 us
  starting transfers between devices  41.1 us (40%)
  Pallas kernels  36.2 us (35%)
  waiting for transfers between devices  13.5 us (13%)
  blocking collectives  10.6 us (10%)
  between operations  1.49 us (1%)
    pallas_call x1, Pallas kernels, second_sweep(): pl.pallas_call(kernel, in_specs=[smem] * 3 + [vmem] * (3 + len(pieces) +...  17.2 us
    all_to_all x1, blocking collectives, plane_exchange(): lax.all_to_all(blocks, 'rows', split_axis=0, concat_axis=0, tiled=True, a...  10.6 us
    ppermute x6, starting transfers between devices, local(): lax.ppermute(keep, 'rows', rows_perm(dz * s, dy * s, 0))  9.29 us
    all_to_all x1, starting transfers between devices, local(): lax.all_to_all(outgoing, 'rows', split_axis=0, concat_axis=0, tiled=True)  9.13 us
    pallas_call x4, Pallas kernels, first_sweep(): pl.pallas_call(first_kernel, out_shape=[pltpu.VMEM((1, total), F32), pltp...  8.55 us
    ppermute x6, waiting for transfers between devices, local(): lax.ppermute(keep, 'rows', rows_perm(dz * s, dy * s, 0))  6.17 us
    ppermute x6, starting transfers between devices, x_parts(): return [lax.ppermute(values, 'cent', x_perm(s)) for s in (1, 3, 2)]  4.95 us
    ppermute x1, starting transfers between devices, local(): other = lax.ppermute(keep, 'rows', swap)  4.67 us
  transfers between devices with their start and end apart: 25, of which 11 were waited for; matrix products, arithmetic and copies ran while one was open for 0% of the time, Pallas kernels for 32%

profile of v5, /device:TPU:1, one launch (start us, length us, event | category | flops | bytes accessed | tf_op | source)
XLA Modules:
  0.0 103.7 jit_solution(2763296309273548373)
XLA Ops:
  0.6 2.4 %unit_cents.1 = (bf16[2048,256]{1,0:T(8,128)(2,1)S(1)}, bf16[1024,256]{1,0:T(8,128)(2,1)}) custom-call(s32[1]{0:T(128)} %bitcast.place_ref.k_ref, f32[2048,256]{1,0:T(8,128)} %c_ref.1), custom_call_target="tpu_custom_call" | custom-call | tf_op jit(solution)/shard_map/unit_cents/pallas_call | solution.py:79
  3.0 3.4 %collective-permute-start.1 = (bf16[1024,256]{1,0:T(8,128)(2,1)}, bf16[1024,256]{1,0:T(8,128)(2,1)S(1)}, u32[]{:S(2)}, u32[]{:S(2)}) collective-permute-start(bf16[1024,256]{1,0:T(8,128)(2,1)} %get-tuple-element.38), channel_id=1, source_target_pairs={{0,3},{1,0},{2,1},{3,2},{4,7},{5,4},{6,5},{7,6},{8,11},{9,8},{10,9... | collective-permute-start | bytes 1572872 | tf_op jit(solution)/shard_map/ppermute | solution.py:457
  7.7 3.7 %unit_rows.1 = (bf16[32,128,256]{2,1,0:T(8,128)(2,1)}, bf16[2048,256]{1,0:T(8,128)(2,1)S(1)}) custom-call(s32[16]{0:T(128)S(1)} %copy-done, s32[1]{0:T(128)S(6)} %copy.7.live_ref, f32[2048,256]{1,0:T(8,128)} %e_ref), custom_call_target="tpu_custom_call" | custom-call | tf_op jit(solution)/shard_map/unit_rows/pallas_call | solution.py:137
  11.4 9.1 %all-to-all-start = ((bf16[32,128,256]{2,1,0:T(8,128)(2,1)}), bf16[32,128,256]{2,1,0:T(8,128)(2,1)}, u32[]{:S(2)}, u32[]{:S(2)}) async-start(bf16[32,128,256]{2,1,0:T(8,128)(2,1)} %get-tuple-element.64), calls=%async_computation | async-start | bytes 4194304 | tf_op jit(solution)/shard_map/all_to_all | solution.py:460
  20.6 1.6 %collective-permute-start.4 = (bf16[1024,256]{1,0:T(8,128)(2,1)S(1)}, bf16[1024,256]{1,0:T(8,128)(2,1)S(1)}, u32[]{:S(2)}, u32[]{:S(2)}) collective-permute-start(bf16[1024,256]{1,0:T(8,128)(2,1)S(1)} %collective-permute-done.right_ref.refs_0_.refs_1_), channel_id=1, source_target_pairs={{0,4},{4,0},{8,12},{12,8},{16,20},{20,16},{24,28},{28,24},{32,36},... | collective-permute-start | bytes 1572872 | tf_op jit(solution)/shard_map/ppermute | solution.py:464
  22.3 2.7 %collective-permute-start.3 = (bf16[512,256]{1,0:T(8,128)(2,1)S(1)}, bf16[512,256]{1,0:T(8,128)(2,1)S(1)}, u32[]{:S(2)}, u32[]{:S(2)}) collective-permute-start(bf16[512,256]{1,0:T(8,128)(2,1)S(1)} %get-tuple-element.45), channel_id=1, source_target_pairs={{0,3},{1,0},{2,1},{3,2},{4,7},{5,4},{6,5},{7,6},{8,11},{9,8},{10,9... | collective-permute-start | bytes 786440 | tf_op jit(solution)/shard_map/ppermute | solution.py:463
  24.9 2.4 %first_sweep.4 = (f32[1,2048]{1,0:T(1,128)S(1)}, bf16[2048,2048]{1,0:T(8,128)(2,1)S(1)}) custom-call(bf16[2048,256]{1,0:T(8,128)(2,1)S(1)} %get-tuple-element.41.r_ref, bf16[2048,256]{1,0:T(8,128)(2,1)S(1)} %get-tuple-element.46.refs_0_), custom_call_target="tpu_custom_call" | custom-call | flops 2048 | bytes 2048 | tf_op jit(solution)/shard_map/first_sweep/pallas_call | solution.py:175
  27.4 2.4 %first_sweep.6 = (f32[1,2048]{1,0:T(1,128)S(1)}, bf16[2048,2048]{1,0:T(8,128)(2,1)S(1)}) custom-call(bf16[2048,256]{1,0:T(8,128)(2,1)S(1)} %get-tuple-element.41.r_ref, bf16[1024,256]{1,0:T(8,128)(2,1)S(1)} %collective-permute-done.1.left_ref.refs_0_.refs_3_, bf16[1024,256]{1,0:T(8,128)(2,1)S(1)} %collective-permute-done.5.refs_1_.refs_4_), custom_call_target="tpu_custom_call" | custom-call | flops 2048 | bytes 2048 | tf_op jit(solution)/shard_map/first_sweep/pallas_call | solution.py:175
  29.8 2.4 %first_sweep.5 = (f32[1,2048]{1,0:T(1,128)S(1)}, bf16[2048,2048]{1,0:T(8,128)(2,1)S(1)}) custom-call(bf16[2048,256]{1,0:T(8,128)(2,1)S(1)} %get-tuple-element.41.r_ref, bf16[1024,256]{1,0:T(8,128)(2,1)S(1)} %collective-permute-done.right_ref.refs_0_.refs_1_, bf16[1024,256]{1,0:T(8,128)(2,1)S(1)} %collective-permute-done.4.refs_1_.refs_2_), custom_call_target="tpu_custom_call" | custom-call | flops 2048 | bytes 2048 | tf_op jit(solution)/shard_map/first_sweep/pallas_call | solution.py:175
  33.7 1.3 %first_sweep.7 = (f32[1,1024]{1,0:T(1,128)S(1)}, bf16[2048,1024]{1,0:T(8,128)(2,1)S(1)}) custom-call(bf16[2048,256]{1,0:T(8,128)(2,1)S(1)} %get-tuple-element.41.r_ref, bf16[512,256]{1,0:T(8,128)(2,1)S(1)} %collective-permute-done.2.refs_0_.refs_5_, bf16[512,256]{1,0:T(8,128)(2,1)S(1)} %collective-permute-done.3.refs_1_.refs_6_), custom_call_target="tpu_custom_call" | custom-call | flops 2048 | bytes 1024 | tf_op jit(solution)/shard_map/first_sweep/pallas_call | solution.py:175
  35.0 1.3 %last_sweep.1 = (f32[32,128]{1,0:T(8,128)S(1)}, f32[32,128]{1,0:T(8,128)S(1)}, bf16[2048,1024]{1,0:T(8,128)(2,1)S(1)}) custom-call(s32[1]{0:T(128)} %bitcast.place_ref.k_ref, bf16[2048,256]{1,0:T(8,128)(2,1)S(1)} %get-tuple-element.41.r_ref, bf16[512,256]{1,0:T(8,128)(2,1)S(1)} %collective-permute-done.6.refs_0_.refs_7_, ...), custom_call_target="tpu_custom_call" | custom-call | flops 2048 | bytes 1024 | tf_op jit(solution)/shard_map/last_sweep/pallas_call | solution.py:217
  39.8 2.4 %collective-permute-done.11 = f32[32,128]{1,0:T(8,128)S(1)} collective-permute-done((f32[32,128]{1,0:T(8,128)S(1)}, f32[32,128]{1,0:T(8,128)S(1)}, u32[]{:S(2)}, u32[]{:S(2)}) %collective-permute-start.11) | collective-permute-done | bytes 16416 | tf_op jit(solution)/shard_map/ppermute | solution.py:434
  42.1 1.2 %collective-permute-done.9 = f32[32,128]{1,0:T(8,128)S(1)} collective-permute-done((f32[32,128]{1,0:T(8,128)S(1)}, f32[32,128]{1,0:T(8,128)S(1)}, u32[]{:S(2)}, u32[]{:S(2)}) %collective-permute-start.9) | collective-permute-done | bytes 16416 | tf_op jit(solution)/shard_map/ppermute | solution.py:434
  43.3 2.9 %collective-permute-start.14 = (f32[32,128]{1,0:T(8,128)S(1)}, f32[32,128]{1,0:T(8,128)S(1)}, u32[]{:S(2)}, u32[]{:S(2)}) collective-permute-start(f32[32,128]{1,0:T(8,128)S(1)} %add_add_fusion.2), channel_id=1, source_target_pairs={{0,16},{4,20},{8,24},{12,28},{16,0},{20,4},{24,8},{28,12},{32,48},... | collective-permute-start | bytes 49160 | tf_op jit(solution)/shard_map/ppermute | solution.py:481
  47.7 1.5 %collective-permute-done.13 = f32[32,128]{1,0:T(8,128)S(1)} collective-permute-done((f32[32,128]{1,0:T(8,128)S(1)}, f32[32,128]{1,0:T(8,128)S(1)}, u32[]{:S(2)}, u32[]{:S(2)}) %collective-permute-start.13) | collective-permute-done | bytes 16416 | tf_op jit(solution)/shard_map/ppermute | solution.py:481
  49.2 1.6 %collective-permute-done.12 = f32[32,128]{1,0:T(8,128)S(1)} collective-permute-done((f32[32,128]{1,0:T(8,128)S(1)}, f32[32,128]{1,0:T(8,128)S(1)}, u32[]{:S(2)}, u32[]{:S(2)}) %collective-permute-start.12) | collective-permute-done | bytes 16416 | tf_op jit(solution)/shard_map/ppermute | solution.py:481
  50.8 3.4 %collective-permute-start.17 = (f32[32,128]{1,0:T(8,128)S(1)}, f32[32,128]{1,0:T(8,128)S(1)}, u32[]{:S(2)}, u32[]{:S(2)}) collective-permute-start(f32[32,128]{1,0:T(8,128)S(1)} %add_add_fusion.1), channel_id=1, source_target_pairs={{0,64},{4,68},{8,72},{12,76},{16,80},{20,84},{24,88},{28,92},{32,9... | collective-permute-start | bytes 49160 | tf_op jit(solution)/shard_map/ppermute | solution.py:481
  56.9 1.9 %collective-permute-done.15 = f32[32,128]{1,0:T(8,128)S(1)} collective-permute-done((f32[32,128]{1,0:T(8,128)S(1)}, f32[32,128]{1,0:T(8,128)S(1)}, u32[]{:S(2)}, u32[]{:S(2)}) %collective-permute-start.15) | collective-permute-done | bytes 16416 | tf_op jit(solution)/shard_map/ppermute | solution.py:481
  58.8 4.7 %collective-permute-start.18 = (f32[32,128]{1,0:T(8,128)S(1)}, f32[32,128]{1,0:T(8,128)S(1)}, u32[]{:S(2)}, u32[]{:S(2)}) collective-permute-start(f32[32,128]{1,0:T(8,128)S(1)} %add_add_fusion.mine_ref), channel_id=1, source_target_pairs={{0,4},{4,0},{8,12},{12,8},{16,20},{20,16},{24,28},{28,24},{32,36},... | collective-permute-start | bytes 49160 | tf_op jit(solution)/shard_map/ppermute | solution.py:483
  64.3 17.2 %second_sweep.1 = (f32[32,128]{1,0:T(8,128)S(1)}, f32[16,128]{1,0:T(8,128)S(1)}, f32[48,128]{1,0:T(8,128)S(1)}) custom-call(s32[1]{0:T(128)} %bitcast.place_ref.k_ref, s32[16]{0:T(128)S(1)} %copy-done.1, s32[1]{0:T(128)S(6)} %copy.7.live_ref, bf16[2048,256]{1,0:T(8,128)(2,1)S(1)} %get-tuple-element.41.r_ref, f32[32,128]{1,0:T(8,128)S(1)} %add_add_fusion.mine_ref, ...), custom_call_target="tpu_custom_call" | custom-call | flops 6144 | bytes 8192 | tf_op jit(solution)/shard_map/second_sweep/pallas_call | solution.py:320
  82.8 1.4 %collective-permute-start.22 = (f32[32,128]{1,0:T(8,128)S(1)}, f32[32,128]{1,0:T(8,128)S(1)}, u32[]{:S(2)}, u32[]{:S(2)}) collective-permute-start(f32[32,128]{1,0:T(8,128)S(1)} %slice_add_fusion.col_ref), channel_id=1, source_target_pairs={{0,2},{1,3},{2,0},{3,1},{4,6},{5,7},{6,4},{7,5},{8,10},{9,11},{10,... | collective-permute-start | bytes 49160 | tf_op jit(solution)/shard_map/ppermute | solution.py:434
  85.6 2.4 %place_rows.1 = bf16[32,128,256]{2,1,0:T(8,128)(2,1)} custom-call(bf16[32,128,256]{2,1,0:T(8,128)(2,1)} %all-to-all-done.in_ref), custom_call_target="tpu_custom_call" | custom-call | bytes 8388608 | tf_op jit(solution)/shard_map/place_rows/pallas_call | solution.py:369
  88.4 10.6 %all_to_all.10.all_ref = f32[16,40,128]{2,1,0:T(8,128)S(1)} all-to-all(f32[16,40,128]{2,1,0:T(8,128)S(1)} %pack.1), channel_id=1, replica_groups={{0,8,16,24,32,40,48,56,64,72,80,88,96,104,112,120},{4,12,20,28,36,44,52..., dimensions={0} | all-to-all | bytes 655360 | tf_op jit(solution)/shard_map/all_to_all | solution.py:439
  99.0 3.2 %collective-permute-start.23 = (f32[32,128]{1,0:T(8,128)S(1)}, f32[32,128]{1,0:T(8,128)S(1)}, u32[]{:S(2)}, u32[]{:S(2)}) collective-permute-start(f32[32,128]{1,0:T(8,128)S(1)} %slice_reduce_fusion.mine_ref), channel_id=1, source_target_pairs={{0,4},{4,0},{8,12},{12,8},{16,20},{20,16},{24,28},{28,24},{32,36},... | collective-permute-start | bytes 49160 | tf_op jit(solution)/shard_map/ppermute | solution.py:498
  (49 shorter events, 15.1 us)
Async XLA Ops:
  3.0 17.5 %collective-permute-start.1 = (bf16[1024,256]{1,0:T(8,128)(2,1)}, bf16[1024,256]{1,0:T(8,128)(2,1)S(1)}, u32[]{:S(2)}, u32[]{:S(2)}) collective-permute-start(bf16[1024,256]{1,0:T(8,128)(2,1)} %get-tuple-element.38), channel_id=1, source_target_pairs={{0,3},{1,0},{2,1},{3,2},{4,7},{5,4},{6,5},{7,6},{8,11},{9,8},{10,9... | collective-permute-start | bytes 1572872 | tf_op jit(solution)/shard_map/ppermute | solution.py:457
  6.4 14.2 %collective-permute-start = (bf16[1024,256]{1,0:T(8,128)(2,1)}, bf16[1024,256]{1,0:T(8,128)(2,1)S(1)}, u32[]{:S(2)}, u32[]{:S(2)}) collective-permute-start(bf16[1024,256]{1,0:T(8,128)(2,1)} %get-tuple-element.38), channel_id=1, source_target_pairs={{0,1},{1,2},{2,3},{3,0},{4,5},{5,6},{6,7},{7,4},{8,9},{9,10},{10,1... | collective-permute-start | bytes 1572872 | tf_op jit(solution)/shard_map/ppermute | solution.py:456
  11.4 74.2 %all-to-all-start = ((bf16[32,128,256]{2,1,0:T(8,128)(2,1)}), bf16[32,128,256]{2,1,0:T(8,128)(2,1)}, u32[]{:S(2)}, u32[]{:S(2)}) async-start(bf16[32,128,256]{2,1,0:T(8,128)(2,1)} %get-tuple-element.64), calls=%async_computation | async-start | bytes 4194304 | tf_op jit(solution)/shard_map/all_to_all | solution.py:460
  20.6 9.2 %collective-permute-start.4 = (bf16[1024,256]{1,0:T(8,128)(2,1)S(1)}, bf16[1024,256]{1,0:T(8,128)(2,1)S(1)}, u32[]{:S(2)}, u32[]{:S(2)}) collective-permute-start(bf16[1024,256]{1,0:T(8,128)(2,1)S(1)} %collective-permute-done.right_ref.refs_0_.refs_1_), channel_id=1, source_target_pairs={{0,4},{4,0},{8,12},{12,8},{16,20},{20,16},{24,28},{28,24},{32,36},... | collective-permute-start | bytes 1572872 | tf_op jit(solution)/shard_map/ppermute | solution.py:464
  22.2 5.2 %collective-permute-start.5 = (bf16[1024,256]{1,0:T(8,128)(2,1)S(1)}, bf16[1024,256]{1,0:T(8,128)(2,1)S(1)}, u32[]{:S(2)}, u32[]{:S(2)}) collective-permute-start(bf16[1024,256]{1,0:T(8,128)(2,1)S(1)} %collective-permute-done.1.left_ref.refs_0_.refs_3_), channel_id=1, source_target_pairs={{0,4},{4,0},{8,12},{12,8},{16,20},{20,16},{24,28},{28,24},{32,36},... | collective-permute-start | bytes 1572872 | tf_op jit(solution)/shard_map/ppermute | solution.py:465
  22.2 10.0 %collective-permute-start.2 = (bf16[512,256]{1,0:T(8,128)(2,1)S(1)}, bf16[512,256]{1,0:T(8,128)(2,1)S(1)}, u32[]{:S(2)}, u32[]{:S(2)}) collective-permute-start(bf16[512,256]{1,0:T(8,128)(2,1)S(1)} %get-tuple-element.44), channel_id=1, source_target_pairs={{0,1},{1,2},{2,3},{3,0},{4,5},{5,6},{6,7},{7,4},{8,9},{9,10},{10,1... | collective-permute-start | bytes 786440 | tf_op jit(solution)/shard_map/ppermute | solution.py:463
  22.3 10.0 %collective-permute-start.3 = (bf16[512,256]{1,0:T(8,128)(2,1)S(1)}, bf16[512,256]{1,0:T(8,128)(2,1)S(1)}, u32[]{:S(2)}, u32[]{:S(2)}) collective-permute-start(bf16[512,256]{1,0:T(8,128)(2,1)S(1)} %get-tuple-element.45), channel_id=1, source_target_pairs={{0,3},{1,0},{2,1},{3,2},{4,7},{5,4},{6,5},{7,6},{8,11},{9,8},{10,9... | collective-permute-start | bytes 786440 | tf_op jit(solution)/shard_map/ppermute | solution.py:463
  32.3 2.7 %collective-permute-start.6 = (bf16[512,256]{1,0:T(8,128)(2,1)S(1)}, bf16[512,256]{1,0:T(8,128)(2,1)S(1)}, u32[]{:S(2)}, u32[]{:S(2)}) collective-permute-start(bf16[512,256]{1,0:T(8,128)(2,1)S(1)} %collective-permute-done.2.refs_0_.refs_5_), channel_id=1, source_target_pairs={{0,4},{4,0},{8,12},{12,8},{16,20},{20,16},{24,28},{28,24},{32,36},... | collective-permute-start | bytes 786440 | tf_op jit(solution)/shard_map/ppermute | solution.py:472
  33.4 1.6 %collective-permute-start.7 = (bf16[512,256]{1,0:T(8,128)(2,1)S(1)}, bf16[512,256]{1,0:T(8,128)(2,1)S(1)}, u32[]{:S(2)}, u32[]{:S(2)}) collective-permute-start(bf16[512,256]{1,0:T(8,128)(2,1)S(1)} %collective-permute-done.3.refs_1_.refs_6_), channel_id=1, source_target_pairs={{0,4},{4,0},{8,12},{12,8},{16,20},{20,16},{24,28},{28,24},{32,36},... | collective-permute-start | bytes 786440 | tf_op jit(solution)/shard_map/ppermute | solution.py:472
  37.6 4.5 %collective-permute-start.11 = (f32[32,128]{1,0:T(8,128)S(1)}, f32[32,128]{1,0:T(8,128)S(1)}, u32[]{:S(2)}, u32[]{:S(2)}) collective-permute-start(f32[32,128]{1,0:T(8,128)S(1)} %add.37), channel_id=1, source_target_pairs={{0,2},{1,3},{2,0},{3,1},{4,6},{5,7},{6,4},{7,5},{8,10},{9,11},{10,... | collective-permute-start | bytes 49160 | tf_op jit(solution)/shard_map/ppermute | solution.py:434
  38.3 3.8 %collective-permute-start.10 = (f32[32,128]{1,0:T(8,128)S(1)}, f32[32,128]{1,0:T(8,128)S(1)}, u32[]{:S(2)}, u32[]{:S(2)}) collective-permute-start(f32[32,128]{1,0:T(8,128)S(1)} %add.37), channel_id=1, source_target_pairs={{0,3},{1,0},{2,1},{3,2},{4,7},{5,4},{6,5},{7,6},{8,11},{9,8},{10,9... | collective-permute-start | bytes 49160 | tf_op jit(solution)/shard_map/ppermute | solution.py:434
  39.1 4.2 %collective-permute-start.9 = (f32[32,128]{1,0:T(8,128)S(1)}, f32[32,128]{1,0:T(8,128)S(1)}, u32[]{:S(2)}, u32[]{:S(2)}) collective-permute-start(f32[32,128]{1,0:T(8,128)S(1)} %add.37), channel_id=1, source_target_pairs={{0,1},{1,2},{2,3},{3,0},{4,5},{5,6},{6,7},{7,4},{8,9},{9,10},{10,1... | collective-permute-start | bytes 49160 | tf_op jit(solution)/shard_map/ppermute | solution.py:434
  43.3 4.4 %collective-permute-start.14 = (f32[32,128]{1,0:T(8,128)S(1)}, f32[32,128]{1,0:T(8,128)S(1)}, u32[]{:S(2)}, u32[]{:S(2)}) collective-permute-start(f32[32,128]{1,0:T(8,128)S(1)} %add_add_fusion.2), channel_id=1, source_target_pairs={{0,16},{4,20},{8,24},{12,28},{16,0},{20,4},{24,8},{28,12},{32,48},... | collective-permute-start | bytes 49160 | tf_op jit(solution)/shard_map/ppermute | solution.py:481
  46.2 3.0 %collective-permute-start.13 = (f32[32,128]{1,0:T(8,128)S(1)}, f32[32,128]{1,0:T(8,128)S(1)}, u32[]{:S(2)}, u32[]{:S(2)}) collective-permute-start(f32[32,128]{1,0:T(8,128)S(1)} %add_add_fusion.2), channel_id=1, source_target_pairs={{0,24},{4,28},{8,0},{12,4},{16,8},{20,12},{24,16},{28,20},{32,56},... | collective-permute-start | bytes 49160 | tf_op jit(solution)/shard_map/ppermute | solution.py:481
  47.0 3.8 %collective-permute-start.12 = (f32[32,128]{1,0:T(8,128)S(1)}, f32[32,128]{1,0:T(8,128)S(1)}, u32[]{:S(2)}, u32[]{:S(2)}) collective-permute-start(f32[32,128]{1,0:T(8,128)S(1)} %add_add_fusion.2), channel_id=1, source_target_pairs={{0,8},{4,12},{8,16},{12,20},{16,24},{20,28},{24,0},{28,4},{32,40},... | collective-permute-start | bytes 49160 | tf_op jit(solution)/shard_map/ppermute | solution.py:481
  50.8 4.9 %collective-permute-start.17 = (f32[32,128]{1,0:T(8,128)S(1)}, f32[32,128]{1,0:T(8,128)S(1)}, u32[]{:S(2)}, u32[]{:S(2)}) collective-permute-start(f32[32,128]{1,0:T(8,128)S(1)} %add_add_fusion.1), channel_id=1, source_target_pairs={{0,64},{4,68},{8,72},{12,76},{16,80},{20,84},{24,88},{28,92},{32,9... | collective-permute-start | bytes 49160 | tf_op jit(solution)/shard_map/ppermute | solution.py:481
  54.3 2.6 %collective-permute-start.16 = (f32[32,128]{1,0:T(8,128)S(1)}, f32[32,128]{1,0:T(8,128)S(1)}, u32[]{:S(2)}, u32[]{:S(2)}) collective-permute-start(f32[32,128]{1,0:T(8,128)S(1)} %add_add_fusion.1), channel_id=1, source_target_pairs={{0,96},{4,100},{8,104},{12,108},{16,112},{20,116},{24,120},{28,124... | collective-permute-start | bytes 49160 | tf_op jit(solution)/shard_map/ppermute | solution.py:481
  54.7 4.1 %collective-permute-start.15 = (f32[32,128]{1,0:T(8,128)S(1)}, f32[32,128]{1,0:T(8,128)S(1)}, u32[]{:S(2)}, u32[]{:S(2)}) collective-permute-start(f32[32,128]{1,0:T(8,128)S(1)} %add_add_fusion.1), channel_id=1, source_target_pairs={{0,32},{4,36},{8,40},{12,44},{16,48},{20,52},{24,56},{28,60},{32,6... | collective-permute-start | bytes 49160 | tf_op jit(solution)/shard_map/ppermute | solution.py:481
  58.8 5.5 %collective-permute-start.18 = (f32[32,128]{1,0:T(8,128)S(1)}, f32[32,128]{1,0:T(8,128)S(1)}, u32[]{:S(2)}, u32[]{:S(2)}) collective-permute-start(f32[32,128]{1,0:T(8,128)S(1)} %add_add_fusion.mine_ref), channel_id=1, source_target_pairs={{0,4},{4,0},{8,12},{12,8},{16,20},{20,16},{24,28},{28,24},{32,36},... | collective-permute-start | bytes 49160 | tf_op jit(solution)/shard_map/ppermute | solution.py:483
  81.5 1.3 %collective-permute-start.19 = (f32[48,128]{1,0:T(8,128)S(1)}, f32[48,128]{1,0:T(8,128)S(1)}, u32[]{:S(2)}, u32[]{:S(2)}) collective-permute-start(f32[48,128]{1,0:T(8,128)S(1)} %get-tuple-element.69), channel_id=1, source_target_pairs={{0,4},{4,0},{8,12},{12,8},{16,20},{20,16},{24,28},{28,24},{32,36},... | collective-permute-start | bytes 73736 | tf_op jit(solution)/shard_map/ppermute | solution.py:494
  82.8 5.3 %collective-permute-start.22 = (f32[32,128]{1,0:T(8,128)S(1)}, f32[32,128]{1,0:T(8,128)S(1)}, u32[]{:S(2)}, u32[]{:S(2)}) collective-permute-start(f32[32,128]{1,0:T(8,128)S(1)} %slice_add_fusion.col_ref), channel_id=1, source_target_pairs={{0,2},{1,3},{2,0},{3,1},{4,6},{5,7},{6,4},{7,5},{8,10},{9,11},{10,... | collective-permute-start | bytes 49160 | tf_op jit(solution)/shard_map/ppermute | solution.py:434
  84.1 3.9 %collective-permute-start.21 = (f32[32,128]{1,0:T(8,128)S(1)}, f32[32,128]{1,0:T(8,128)S(1)}, u32[]{:S(2)}, u32[]{:S(2)}) collective-permute-start(f32[32,128]{1,0:T(8,128)S(1)} %slice_add_fusion.col_ref), channel_id=1, source_target_pairs={{0,3},{1,0},{2,1},{3,2},{4,7},{5,4},{6,5},{7,6},{8,11},{9,8},{10,9... | collective-permute-start | bytes 49160 | tf_op jit(solution)/shard_map/ppermute | solution.py:434
  84.6 3.8 %collective-permute-start.20 = (f32[32,128]{1,0:T(8,128)S(1)}, f32[32,128]{1,0:T(8,128)S(1)}, u32[]{:S(2)}, u32[]{:S(2)}) collective-permute-start(f32[32,128]{1,0:T(8,128)S(1)} %slice_add_fusion.col_ref), channel_id=1, source_target_pairs={{0,1},{1,2},{2,3},{3,0},{4,5},{5,6},{6,7},{7,4},{8,9},{9,10},{10,1... | collective-permute-start | bytes 49160 | tf_op jit(solution)/shard_map/ppermute | solution.py:434
  99.0 4.0 %collective-permute-start.23 = (f32[32,128]{1,0:T(8,128)S(1)}, f32[32,128]{1,0:T(8,128)S(1)}, u32[]{:S(2)}, u32[]{:S(2)}) collective-permute-start(f32[32,128]{1,0:T(8,128)S(1)} %slice_reduce_fusion.mine_ref), channel_id=1, source_target_pairs={{0,4},{4,0},{8,12},{12,8},{16,20},{20,16},{24,28},{28,24},{32,36},... | collective-permute-start | bytes 49160 | tf_op jit(solution)/shard_map/ppermute | solution.py:498
  (3 other events, 38.9 us)

commit v6 on v5

--- a/solution.py
+++ b/solution.py
@@ -87,24 +87,22 @@
     )(place, in_hbm(centroids))
 
 
-def forward_kernel(right_ref, left_ref, first_ref, second_ref):
-    n = first_ref.shape[0]
-    first_ref[...] = right_ref[:n, :]
-    second_ref[...] = left_ref[n:, :]
-
-
-def forward_parts(right, left):
-    n, d = right.shape
-    vmem = pl.BlockSpec(memory_space=pltpu.VMEM)
-    return pl.pallas_call(
-        forward_kernel,
-        in_specs=[vmem, vmem],
-        out_specs=[vmem, vmem],
-        out_shape=[jax.ShapeDtypeStruct((n // 2, d), BF16)] * 2,
+def forward_kernel(in_ref, out_ref, *, start):
+    out_ref[...] = in_ref[start : start + out_ref.shape[0], :]
+
+
+def forward_part(piece, start, weight):
+    n, d = piece.shape
+    vmem = pl.BlockSpec(memory_space=pltpu.VMEM)
+    return pl.pallas_call(
+        functools.partial(forward_kernel, start=start),
+        in_specs=[vmem],
+        out_specs=vmem,
+        out_shape=jax.ShapeDtypeStruct((n // 2, d), BF16),
         compiler_params=params(8),
-        cost_estimate=cost(2**26, 0, 2**11),
-        name="forward_parts",
-    )(right, left)
+        cost_estimate=cost(weight, 0, 2**11),
+        name="forward_part",
+    )(piece)
 
 
 def rows_kernel(owner_ref, live_ref, e_ref, out_ref, scaled_ref, buf, sems):
@@ -458,9 +456,10 @@
     embeddings, mine = lax.optimization_barrier((embeddings, mine))
     outgoing, scaled = unit_rows(owners, live_blocks, embeddings, peers)
     arrived = lax.all_to_all(outgoing, "rows", split_axis=0, concat_axis=0, tiled=True)
+    far_left = lax.ppermute(forward_part(left, half // 2, 1), "cent", x_perm(-1))
     right, left, scaled = lax.optimization_barrier((right, left, scaled))
     swap = rows_perm(0, 0, 1)
-    far = [lax.ppermute(t, "cent", x_perm(s)) for t, s in zip(forward_parts(right, left), (1, -1))]
+    far = [lax.ppermute(forward_part(right, 0, 2**26), "cent", x_perm(1)), far_left]
     right = [right, lax.ppermute(right, "rows", swap)]
     left = [left, lax.ppermute(left, "rows", swap)]
     sums_own, w_own = first_sweep(scaled, [own])

time: 104 us -> 104 us (level)
  waiting for transfers between devices: 13.5 us -> 15.2 us
  starting transfers between devices: 41.1 us -> 39.5 us
    ppermute x1, starting transfers between devices: 0.01 us -> 1.6 us  [local(): left = [left, lax.ppermute(left, 'rows', swap)]]
    ppermute x1, starting transfers between devices: 1.58 us -> 0.01 us  [local(): right = [right, lax.ppermute(right, 'rows', swap)]]
    ppermute x2, waiting for transfers between devices: 0.01 us -> 1.28 us  [the longest x1 1.28 us: local(): lax.ppermute(forward_part(right, 0, 2 ** 26), 'cent', x_perm(1))]
  transfers between devices with their start and end apart: 25 -> 25, of which waited for: 11 -> 13; matrix products, arithmetic and copies ran while one was open for 0% -> 0% of each run, Pallas kernels for 32% -> 32%
where the time goes in v6:
time: 104 us
  starting transfers between devices  39.5 us (38%)
  Pallas kernels  36.2 us (35%)
  waiting for transfers between devices  15.2 us (15%)
  blocking collectives  10.6 us (10%)
  between operations  1.48 us (1%)
    pallas_call x1, Pallas kernels, second_sweep(): pl.pallas_call(kernel, in_specs=[smem] * 3 + [vmem] * (3 + len(pieces) +...  17.2 us
    all_to_all x1, blocking collectives, plane_exchange(): lax.all_to_all(blocks, 'rows', split_axis=0, concat_axis=0, tiled=True, a...  10.6 us
    all_to_all x1, starting transfers between devices, local(): lax.all_to_all(outgoing, 'rows', split_axis=0, concat_axis=0, tiled=True)  9.13 us
    ppermute x6, starting transfers between devices, local(): lax.ppermute(keep, 'rows', rows_perm(dz * s, dy * s, 0))  8.6 us
    pallas_call x4, Pallas kernels, first_sweep(): pl.pallas_call(first_kernel, out_shape=[pltpu.VMEM((1, total), F32), pltp...  8.55 us
    ppermute x6, waiting for transfers between devices, local(): lax.ppermute(keep, 'rows', rows_perm(dz * s, dy * s, 0))  6.18 us
    ppermute x1, starting transfers between devices, local(): other = lax.ppermute(keep, 'rows', swap)  5.14 us
    ppermute x6, starting transfers between devices, x_parts(): return [lax.ppermute(values, 'cent', x_perm(s)) for s in (1, 3, 2)]  4.16 us
  transfers between devices with their start and end apart: 25, of which 13 were waited for; matrix products, arithmetic and copies ran while one was open for 0% of the time, Pallas kernels for 32%

profile of v6, /device:TPU:1, one launch (start us, length us, event | category | flops | bytes accessed | tf_op | source)
XLA Modules:
  0.0 103.6 jit_solution(4905708596998234243)
XLA Ops:
  0.6 2.4 %unit_cents.1 = (bf16[2048,256]{1,0:T(8,128)(2,1)S(1)}, bf16[1024,256]{1,0:T(8,128)(2,1)}) custom-call(s32[1]{0:T(128)} %bitcast.place_ref.k_ref, f32[2048,256]{1,0:T(8,128)} %c_ref.1), custom_call_target="tpu_custom_call" | custom-call | tf_op jit(solution)/shard_map/unit_cents/pallas_call | solution.py:79
  3.0 3.4 %collective-permute-start.1 = (bf16[1024,256]{1,0:T(8,128)(2,1)}, bf16[1024,256]{1,0:T(8,128)(2,1)S(1)}, u32[]{:S(2)}, u32[]{:S(2)}) collective-permute-start(bf16[1024,256]{1,0:T(8,128)(2,1)} %get-tuple-element.36), channel_id=1, source_target_pairs={{0,3},{1,0},{2,1},{3,2},{4,7},{5,4},{6,5},{7,6},{8,11},{9,8},{10,9... | collective-permute-start | bytes 1572872 | tf_op jit(solution)/shard_map/ppermute | solution.py:455
  7.7 3.7 %unit_rows.1 = (bf16[32,128,256]{2,1,0:T(8,128)(2,1)}, bf16[2048,256]{1,0:T(8,128)(2,1)S(1)}) custom-call(s32[16]{0:T(128)S(1)} %copy-done, s32[1]{0:T(128)S(6)} %copy.7.live_ref, f32[2048,256]{1,0:T(8,128)} %e_ref), custom_call_target="tpu_custom_call" | custom-call | tf_op jit(solution)/shard_map/unit_rows/pallas_call | solution.py:135
  11.4 9.1 %all-to-all-start = ((bf16[32,128,256]{2,1,0:T(8,128)(2,1)}), bf16[32,128,256]{2,1,0:T(8,128)(2,1)}, u32[]{:S(2)}, u32[]{:S(2)}) async-start(bf16[32,128,256]{2,1,0:T(8,128)(2,1)} %get-tuple-element.60), calls=%async_computation | async-start | bytes 4194304 | tf_op jit(solution)/shard_map/all_to_all | solution.py:458
  20.5 1.6 %collective-permute-start.5 = (bf16[1024,256]{1,0:T(8,128)(2,1)S(1)}, bf16[1024,256]{1,0:T(8,128)(2,1)S(1)}, u32[]{:S(2)}, u32[]{:S(2)}) collective-permute-start(bf16[1024,256]{1,0:T(8,128)(2,1)S(1)} %collective-permute-done.1.in_ref.refs_0_.refs_3_), channel_id=1, source_target_pairs={{0,4},{4,0},{8,12},{12,8},{16,20},{20,16},{24,28},{28,24},{32,36},... | collective-permute-start | bytes 1572872 | tf_op jit(solution)/shard_map/ppermute | solution.py:464
  22.2 2.0 %collective-permute-start.3 = (bf16[512,256]{1,0:T(8,128)(2,1)S(1)}, bf16[512,256]{1,0:T(8,128)(2,1)S(1)}, u32[]{:S(2)}, u32[]{:S(2)}) collective-permute-start(bf16[512,256]{1,0:T(8,128)(2,1)S(1)} %forward_part.3), channel_id=1, source_target_pairs={{0,3},{1,0},{2,1},{3,2},{4,7},{5,4},{6,5},{7,6},{8,11},{9,8},{10,9... | collective-permute-start | bytes 786440 | tf_op jit(solution)/shard_map/ppermute | solution.py:459
  24.2 2.4 %first_sweep.4 = (f32[1,2048]{1,0:T(1,128)S(1)}, bf16[2048,2048]{1,0:T(8,128)(2,1)S(1)}) custom-call(bf16[2048,256]{1,0:T(8,128)(2,1)S(1)} %get-tuple-element.39.r_ref, bf16[2048,256]{1,0:T(8,128)(2,1)S(1)} %get-tuple-element.41.refs_0_), custom_call_target="tpu_custom_call" | custom-call | flops 2048 | bytes 2048 | tf_op jit(solution)/shard_map/first_sweep/pallas_call | solution.py:173
  26.6 2.4 %first_sweep.5 = (f32[1,2048]{1,0:T(1,128)S(1)}, bf16[2048,2048]{1,0:T(8,128)(2,1)S(1)}) custom-call(bf16[2048,256]{1,0:T(8,128)(2,1)S(1)} %get-tuple-element.39.r_ref, bf16[1024,256]{1,0:T(8,128)(2,1)S(1)} %collective-permute-done.in_ref.refs_0_.refs_1_, bf16[1024,256]{1,0:T(8,128)(2,1)S(1)} %collective-permute-done.4.refs_1_.refs_2_), custom_call_target="tpu_custom_call" | custom-call | flops 2048 | bytes 2048 | tf_op jit(solution)/shard_map/first_sweep/pallas_call | solution.py:173
  29.1 2.4 %first_sweep.6 = (f32[1,2048]{1,0:T(1,128)S(1)}, bf16[2048,2048]{1,0:T(8,128)(2,1)S(1)}) custom-call(bf16[2048,256]{1,0:T(8,128)(2,1)S(1)} %get-tuple-element.39.r_ref, bf16[1024,256]{1,0:T(8,128)(2,1)S(1)} %collective-permute-done.1.in_ref.refs_0_.refs_3_, bf16[1024,256]{1,0:T(8,128)(2,1)S(1)} %collective-permute-done.5.refs_1_.refs_4_), custom_call_target="tpu_custom_call" | custom-call | flops 2048 | bytes 2048 | tf_op jit(solution)/shard_map/first_sweep/pallas_call | solution.py:173
  31.5 1.3 %collective-permute-done.2.refs_0_.refs_5_ = bf16[512,256]{1,0:T(8,128)(2,1)S(1)} collective-permute-done((bf16[512,256]{1,0:T(8,128)(2,1)S(1)}, bf16[512,256]{1,0:T(8,128)(2,1)S(1)}, u32[]{:S(2)}, u32[]{:S(2)}) %collective-permute-start.2) | collective-permute-done | bytes 262176 | tf_op jit(solution)/shard_map/ppermute | solution.py:462
  32.8 1.3 %collective-permute-start.6 = (bf16[512,256]{1,0:T(8,128)(2,1)S(1)}, bf16[512,256]{1,0:T(8,128)(2,1)S(1)}, u32[]{:S(2)}, u32[]{:S(2)}) collective-permute-start(bf16[512,256]{1,0:T(8,128)(2,1)S(1)} %collective-permute-done.2.refs_0_.refs_5_), channel_id=1, source_target_pairs={{0,4},{4,0},{8,12},{12,8},{16,20},{20,16},{24,28},{28,24},{32,36},... | collective-permute-start | bytes 786440 | tf_op jit(solution)/shard_map/ppermute | solution.py:471
  34.1 1.3 %first_sweep.7 = (f32[1,1024]{1,0:T(1,128)S(1)}, bf16[2048,1024]{1,0:T(8,128)(2,1)S(1)}) custom-call(bf16[2048,256]{1,0:T(8,128)(2,1)S(1)} %get-tuple-element.39.r_ref, bf16[512,256]{1,0:T(8,128)(2,1)S(1)} %collective-permute-done.2.refs_0_.refs_5_, bf16[512,256]{1,0:T(8,128)(2,1)S(1)} %collective-permute-done.3.refs_1_.refs_6_), custom_call_target="tpu_custom_call" | custom-call | flops 2048 | bytes 1024 | tf_op jit(solution)/shard_map/first_sweep/pallas_call | solution.py:173
  35.7 1.3 %last_sweep.1 = (f32[32,128]{1,0:T(8,128)S(1)}, f32[32,128]{1,0:T(8,128)S(1)}, bf16[2048,1024]{1,0:T(8,128)(2,1)S(1)}) custom-call(s32[1]{0:T(128)} %bitcast.place_ref.k_ref, bf16[2048,256]{1,0:T(8,128)(2,1)S(1)} %get-tuple-element.39.r_ref, bf16[512,256]{1,0:T(8,128)(2,1)S(1)} %collective-permute-done.6.refs_0_.refs_7_, ...), custom_call_target="tpu_custom_call" | custom-call | flops 2048 | bytes 1024 | tf_op jit(solution)/shard_map/last_sweep/pallas_call | solution.py:215
  40.0 2.9 %collective-permute-done.11 = f32[32,128]{1,0:T(8,128)S(1)} collective-permute-done((f32[32,128]{1,0:T(8,128)S(1)}, f32[32,128]{1,0:T(8,128)S(1)}, u32[]{:S(2)}, u32[]{:S(2)}) %collective-permute-start.11) | collective-permute-done | bytes 16416 | tf_op jit(solution)/shard_map/ppermute | solution.py:432
  43.8 2.9 %collective-permute-start.14 = (f32[32,128]{1,0:T(8,128)S(1)}, f32[32,128]{1,0:T(8,128)S(1)}, u32[]{:S(2)}, u32[]{:S(2)}) collective-permute-start(f32[32,128]{1,0:T(8,128)S(1)} %add_add_fusion.2), channel_id=1, source_target_pairs={{0,16},{4,20},{8,24},{12,28},{16,0},{20,4},{24,8},{28,12},{32,48},... | collective-permute-start | bytes 49160 | tf_op jit(solution)/shard_map/ppermute | solution.py:480
  48.2 1.5 %collective-permute-done.13 = f32[32,128]{1,0:T(8,128)S(1)} collective-permute-done((f32[32,128]{1,0:T(8,128)S(1)}, f32[32,128]{1,0:T(8,128)S(1)}, u32[]{:S(2)}, u32[]{:S(2)}) %collective-permute-start.13) | collective-permute-done | bytes 16416 | tf_op jit(solution)/shard_map/ppermute | solution.py:480
  49.7 1.7 %collective-permute-done.12 = f32[32,128]{1,0:T(8,128)S(1)} collective-permute-done((f32[32,128]{1,0:T(8,128)S(1)}, f32[32,128]{1,0:T(8,128)S(1)}, u32[]{:S(2)}, u32[]{:S(2)}) %collective-permute-start.12) | collective-permute-done | bytes 16416 | tf_op jit(solution)/shard_map/ppermute | solution.py:480
  51.4 2.8 %collective-permute-start.17 = (f32[32,128]{1,0:T(8,128)S(1)}, f32[32,128]{1,0:T(8,128)S(1)}, u32[]{:S(2)}, u32[]{:S(2)}) collective-permute-start(f32[32,128]{1,0:T(8,128)S(1)} %add_add_fusion.1), channel_id=1, source_target_pairs={{0,64},{4,68},{8,72},{12,76},{16,80},{20,84},{24,88},{28,92},{32,9... | collective-permute-start | bytes 49160 | tf_op jit(solution)/shard_map/ppermute | solution.py:480
  56.8 1.9 %collective-permute-done.15 = f32[32,128]{1,0:T(8,128)S(1)} collective-permute-done((f32[32,128]{1,0:T(8,128)S(1)}, f32[32,128]{1,0:T(8,128)S(1)}, u32[]{:S(2)}, u32[]{:S(2)}) %collective-permute-start.15) | collective-permute-done | bytes 16416 | tf_op jit(solution)/shard_map/ppermute | solution.py:480
  58.6 5.1 %collective-permute-start.18 = (f32[32,128]{1,0:T(8,128)S(1)}, f32[32,128]{1,0:T(8,128)S(1)}, u32[]{:S(2)}, u32[]{:S(2)}) collective-permute-start(f32[32,128]{1,0:T(8,128)S(1)} %add_add_fusion.mine_ref), channel_id=1, source_target_pairs={{0,4},{4,0},{8,12},{12,8},{16,20},{20,16},{24,28},{28,24},{32,36},... | collective-permute-start | bytes 49160 | tf_op jit(solution)/shard_map/ppermute | solution.py:482
  64.6 17.2 %second_sweep.1 = (f32[32,128]{1,0:T(8,128)S(1)}, f32[16,128]{1,0:T(8,128)S(1)}, f32[48,128]{1,0:T(8,128)S(1)}) custom-call(s32[1]{0:T(128)} %bitcast.place_ref.k_ref, s32[16]{0:T(128)S(1)} %copy-done.1, s32[1]{0:T(128)S(6)} %copy.7.live_ref, bf16[2048,256]{1,0:T(8,128)(2,1)S(1)} %get-tuple-element.39.r_ref, f32[32,128]{1,0:T(8,128)S(1)} %add_add_fusion.mine_ref, ...), custom_call_target="tpu_custom_call" | custom-call | flops 6144 | bytes 8192 | tf_op jit(solution)/shard_map/second_sweep/pallas_call | solution.py:318
  85.6 2.4 %place_rows.1 = bf16[32,128,256]{2,1,0:T(8,128)(2,1)} custom-call(bf16[32,128,256]{2,1,0:T(8,128)(2,1)} %all-to-all-done.in_ref), custom_call_target="tpu_custom_call" | custom-call | bytes 8388608 | tf_op jit(solution)/shard_map/place_rows/pallas_call | solution.py:367
  88.3 10.6 %all_to_all.10.all_ref = f32[16,40,128]{2,1,0:T(8,128)S(1)} all-to-all(f32[16,40,128]{2,1,0:T(8,128)S(1)} %pack.1), channel_id=1, replica_groups={{0,8,16,24,32,40,48,56,64,72,80,88,96,104,112,120},{4,12,20,28,36,44,52..., dimensions={0} | all-to-all | bytes 655360 | tf_op jit(solution)/shard_map/all_to_all | solution.py:437
  99.0 3.2 %collective-permute-start.23 = (f32[32,128]{1,0:T(8,128)S(1)}, f32[32,128]{1,0:T(8,128)S(1)}, u32[]{:S(2)}, u32[]{:S(2)}) collective-permute-start(f32[32,128]{1,0:T(8,128)S(1)} %slice_reduce_fusion.mine_ref), channel_id=1, source_target_pairs={{0,4},{4,0},{8,12},{12,8},{16,20},{20,16},{24,28},{28,24},{32,36},... | collective-permute-start | bytes 49160 | tf_op jit(solution)/shard_map/ppermute | solution.py:497
  (50 shorter events, 15.4 us)
Async XLA Ops:
  3.0 17.5 %collective-permute-start.1 = (bf16[1024,256]{1,0:T(8,128)(2,1)}, bf16[1024,256]{1,0:T(8,128)(2,1)S(1)}, u32[]{:S(2)}, u32[]{:S(2)}) collective-permute-start(bf16[1024,256]{1,0:T(8,128)(2,1)} %get-tuple-element.36), channel_id=1, source_target_pairs={{0,3},{1,0},{2,1},{3,2},{4,7},{5,4},{6,5},{7,6},{8,11},{9,8},{10,9... | collective-permute-start | bytes 1572872 | tf_op jit(solution)/shard_map/ppermute | solution.py:455
  6.4 14.2 %collective-permute-start = (bf16[1024,256]{1,0:T(8,128)(2,1)}, bf16[1024,256]{1,0:T(8,128)(2,1)S(1)}, u32[]{:S(2)}, u32[]{:S(2)}) collective-permute-start(bf16[1024,256]{1,0:T(8,128)(2,1)} %get-tuple-element.36), channel_id=1, source_target_pairs={{0,1},{1,2},{2,3},{3,0},{4,5},{5,6},{6,7},{7,4},{8,9},{9,10},{10,1... | collective-permute-start | bytes 1572872 | tf_op jit(solution)/shard_map/ppermute | solution.py:454
  11.4 74.2 %all-to-all-start = ((bf16[32,128,256]{2,1,0:T(8,128)(2,1)}), bf16[32,128,256]{2,1,0:T(8,128)(2,1)}, u32[]{:S(2)}, u32[]{:S(2)}) async-start(bf16[32,128,256]{2,1,0:T(8,128)(2,1)} %get-tuple-element.60), calls=%async_computation | async-start | bytes 4194304 | tf_op jit(solution)/shard_map/all_to_all | solution.py:458
  20.5 8.5 %collective-permute-start.5 = (bf16[1024,256]{1,0:T(8,128)(2,1)S(1)}, bf16[1024,256]{1,0:T(8,128)(2,1)S(1)}, u32[]{:S(2)}, u32[]{:S(2)}) collective-permute-start(bf16[1024,256]{1,0:T(8,128)(2,1)S(1)} %collective-permute-done.1.in_ref.refs_0_.refs_3_), channel_id=1, source_target_pairs={{0,4},{4,0},{8,12},{12,8},{16,20},{20,16},{24,28},{28,24},{32,36},... | collective-permute-start | bytes 1572872 | tf_op jit(solution)/shard_map/ppermute | solution.py:464
  22.1 4.5 %collective-permute-start.4 = (bf16[1024,256]{1,0:T(8,128)(2,1)S(1)}, bf16[1024,256]{1,0:T(8,128)(2,1)S(1)}, u32[]{:S(2)}, u32[]{:S(2)}) collective-permute-start(bf16[1024,256]{1,0:T(8,128)(2,1)S(1)} %collective-permute-done.in_ref.refs_0_.refs_1_), channel_id=1, source_target_pairs={{0,4},{4,0},{8,12},{12,8},{16,20},{20,16},{24,28},{28,24},{32,36},... | collective-permute-start | bytes 1572872 | tf_op jit(solution)/shard_map/ppermute | solution.py:463
  22.2 9.3 %collective-permute-start.3 = (bf16[512,256]{1,0:T(8,128)(2,1)S(1)}, bf16[512,256]{1,0:T(8,128)(2,1)S(1)}, u32[]{:S(2)}, u32[]{:S(2)}) collective-permute-start(bf16[512,256]{1,0:T(8,128)(2,1)S(1)} %forward_part.3), channel_id=1, source_target_pairs={{0,3},{1,0},{2,1},{3,2},{4,7},{5,4},{6,5},{7,6},{8,11},{9,8},{10,9... | collective-permute-start | bytes 786440 | tf_op jit(solution)/shard_map/ppermute | solution.py:459
  24.2 8.6 %collective-permute-start.2 = (bf16[512,256]{1,0:T(8,128)(2,1)S(1)}, bf16[512,256]{1,0:T(8,128)(2,1)S(1)}, u32[]{:S(2)}, u32[]{:S(2)}) collective-permute-start(bf16[512,256]{1,0:T(8,128)(2,1)S(1)} %forward_part.2), channel_id=1, source_target_pairs={{0,1},{1,2},{2,3},{3,0},{4,5},{5,6},{6,7},{7,4},{8,9},{9,10},{10,1... | collective-permute-start | bytes 786440 | tf_op jit(solution)/shard_map/ppermute | solution.py:462
  32.8 2.7 %collective-permute-start.6 = (bf16[512,256]{1,0:T(8,128)(2,1)S(1)}, bf16[512,256]{1,0:T(8,128)(2,1)S(1)}, u32[]{:S(2)}, u32[]{:S(2)}) collective-permute-start(bf16[512,256]{1,0:T(8,128)(2,1)S(1)} %collective-permute-done.2.refs_0_.refs_5_), channel_id=1, source_target_pairs={{0,4},{4,0},{8,12},{12,8},{16,20},{20,16},{24,28},{28,24},{32,36},... | collective-permute-start | bytes 786440 | tf_op jit(solution)/shard_map/ppermute | solution.py:471
  34.1 1.5 %collective-permute-start.7 = (bf16[512,256]{1,0:T(8,128)(2,1)S(1)}, bf16[512,256]{1,0:T(8,128)(2,1)S(1)}, u32[]{:S(2)}, u32[]{:S(2)}) collective-permute-start(bf16[512,256]{1,0:T(8,128)(2,1)S(1)} %collective-permute-done.3.refs_1_.refs_6_), channel_id=1, source_target_pairs={{0,4},{4,0},{8,12},{12,8},{16,20},{20,16},{24,28},{28,24},{32,36},... | collective-permute-start | bytes 786440 | tf_op jit(solution)/shard_map/ppermute | solution.py:471
  37.0 1.3 %collective-permute-start.8 = (f32[32,128]{1,0:T(8,128)S(1)}, f32[32,128]{1,0:T(8,128)S(1)}, u32[]{:S(2)}, u32[]{:S(2)}) collective-permute-start(f32[32,128]{1,0:T(8,128)S(1)} %get-tuple-element.53), channel_id=1, source_target_pairs={{0,4},{4,0},{8,12},{12,8},{16,20},{20,16},{24,28},{28,24},{32,36},... | collective-permute-start | bytes 49160 | tf_op jit(solution)/shard_map/ppermute | solution.py:476
  38.3 4.5 %collective-permute-start.11 = (f32[32,128]{1,0:T(8,128)S(1)}, f32[32,128]{1,0:T(8,128)S(1)}, u32[]{:S(2)}, u32[]{:S(2)}) collective-permute-start(f32[32,128]{1,0:T(8,128)S(1)} %add.37), channel_id=1, source_target_pairs={{0,2},{1,3},{2,0},{3,1},{4,6},{5,7},{6,4},{7,5},{8,10},{9,11},{10,... | collective-permute-start | bytes 49160 | tf_op jit(solution)/shard_map/ppermute | solution.py:432
  38.3 4.5 %collective-permute-start.10 = (f32[32,128]{1,0:T(8,128)S(1)}, f32[32,128]{1,0:T(8,128)S(1)}, u32[]{:S(2)}, u32[]{:S(2)}) collective-permute-start(f32[32,128]{1,0:T(8,128)S(1)} %add.37), channel_id=1, source_target_pairs={{0,3},{1,0},{2,1},{3,2},{4,7},{5,4},{6,5},{7,6},{8,11},{9,8},{10,9... | collective-permute-start | bytes 49160 | tf_op jit(solution)/shard_map/ppermute | solution.py:432
  39.5 4.3 %collective-permute-start.9 = (f32[32,128]{1,0:T(8,128)S(1)}, f32[32,128]{1,0:T(8,128)S(1)}, u32[]{:S(2)}, u32[]{:S(2)}) collective-permute-start(f32[32,128]{1,0:T(8,128)S(1)} %add.37), channel_id=1, source_target_pairs={{0,1},{1,2},{2,3},{3,0},{4,5},{5,6},{6,7},{7,4},{8,9},{9,10},{10,1... | collective-permute-start | bytes 49160 | tf_op jit(solution)/shard_map/ppermute | solution.py:432
  43.8 4.4 %collective-permute-start.14 = (f32[32,128]{1,0:T(8,128)S(1)}, f32[32,128]{1,0:T(8,128)S(1)}, u32[]{:S(2)}, u32[]{:S(2)}) collective-permute-start(f32[32,128]{1,0:T(8,128)S(1)} %add_add_fusion.2), channel_id=1, source_target_pairs={{0,16},{4,20},{8,24},{12,28},{16,0},{20,4},{24,8},{28,12},{32,48},... | collective-permute-start | bytes 49160 | tf_op jit(solution)/shard_map/ppermute | solution.py:480
  46.7 3.0 %collective-permute-start.13 = (f32[32,128]{1,0:T(8,128)S(1)}, f32[32,128]{1,0:T(8,128)S(1)}, u32[]{:S(2)}, u32[]{:S(2)}) collective-permute-start(f32[32,128]{1,0:T(8,128)S(1)} %add_add_fusion.2), channel_id=1, source_target_pairs={{0,24},{4,28},{8,0},{12,4},{16,8},{20,12},{24,16},{28,20},{32,56},... | collective-permute-start | bytes 49160 | tf_op jit(solution)/shard_map/ppermute | solution.py:480
  47.6 3.8 %collective-permute-start.12 = (f32[32,128]{1,0:T(8,128)S(1)}, f32[32,128]{1,0:T(8,128)S(1)}, u32[]{:S(2)}, u32[]{:S(2)}) collective-permute-start(f32[32,128]{1,0:T(8,128)S(1)} %add_add_fusion.2), channel_id=1, source_target_pairs={{0,8},{4,12},{8,16},{12,20},{16,24},{20,28},{24,0},{28,4},{32,40},... | collective-permute-start | bytes 49160 | tf_op jit(solution)/shard_map/ppermute | solution.py:480
  51.4 4.3 %collective-permute-start.17 = (f32[32,128]{1,0:T(8,128)S(1)}, f32[32,128]{1,0:T(8,128)S(1)}, u32[]{:S(2)}, u32[]{:S(2)}) collective-permute-start(f32[32,128]{1,0:T(8,128)S(1)} %add_add_fusion.1), channel_id=1, source_target_pairs={{0,64},{4,68},{8,72},{12,76},{16,80},{20,84},{24,88},{28,92},{32,9... | collective-permute-start | bytes 49160 | tf_op jit(solution)/shard_map/ppermute | solution.py:480
  54.2 2.6 %collective-permute-start.16 = (f32[32,128]{1,0:T(8,128)S(1)}, f32[32,128]{1,0:T(8,128)S(1)}, u32[]{:S(2)}, u32[]{:S(2)}) collective-permute-start(f32[32,128]{1,0:T(8,128)S(1)} %add_add_fusion.1), channel_id=1, source_target_pairs={{0,96},{4,100},{8,104},{12,108},{16,112},{20,116},{24,120},{28,124... | collective-permute-start | bytes 49160 | tf_op jit(solution)/shard_map/ppermute | solution.py:480
  54.8 3.8 %collective-permute-start.15 = (f32[32,128]{1,0:T(8,128)S(1)}, f32[32,128]{1,0:T(8,128)S(1)}, u32[]{:S(2)}, u32[]{:S(2)}) collective-permute-start(f32[32,128]{1,0:T(8,128)S(1)} %add_add_fusion.1), channel_id=1, source_target_pairs={{0,32},{4,36},{8,40},{12,44},{16,48},{20,52},{24,56},{28,60},{32,6... | collective-permute-start | bytes 49160 | tf_op jit(solution)/shard_map/ppermute | solution.py:480
  58.6 6.0 %collective-permute-start.18 = (f32[32,128]{1,0:T(8,128)S(1)}, f32[32,128]{1,0:T(8,128)S(1)}, u32[]{:S(2)}, u32[]{:S(2)}) collective-permute-start(f32[32,128]{1,0:T(8,128)S(1)} %add_add_fusion.mine_ref), channel_id=1, source_target_pairs={{0,4},{4,0},{8,12},{12,8},{16,20},{20,16},{24,28},{28,24},{32,36},... | collective-permute-start | bytes 49160 | tf_op jit(solution)/shard_map/ppermute | solution.py:482
  83.0 5.0 %collective-permute-start.22 = (f32[32,128]{1,0:T(8,128)S(1)}, f32[32,128]{1,0:T(8,128)S(1)}, u32[]{:S(2)}, u32[]{:S(2)}) collective-permute-start(f32[32,128]{1,0:T(8,128)S(1)} %slice_add_fusion.col_ref), channel_id=1, source_target_pairs={{0,2},{1,3},{2,0},{3,1},{4,6},{5,7},{6,4},{7,5},{8,10},{9,11},{10,... | collective-permute-start | bytes 49160 | tf_op jit(solution)/shard_map/ppermute | solution.py:432
  84.1 3.9 %collective-permute-start.21 = (f32[32,128]{1,0:T(8,128)S(1)}, f32[32,128]{1,0:T(8,128)S(1)}, u32[]{:S(2)}, u32[]{:S(2)}) collective-permute-start(f32[32,128]{1,0:T(8,128)S(1)} %slice_add_fusion.col_ref), channel_id=1, source_target_pairs={{0,3},{1,0},{2,1},{3,2},{4,7},{5,4},{6,5},{7,6},{8,11},{9,8},{10,9... | collective-permute-start | bytes 49160 | tf_op jit(solution)/shard_map/ppermute | solution.py:432
  84.5 3.8 %collective-permute-start.20 = (f32[32,128]{1,0:T(8,128)S(1)}, f32[32,128]{1,0:T(8,128)S(1)}, u32[]{:S(2)}, u32[]{:S(2)}) collective-permute-start(f32[32,128]{1,0:T(8,128)S(1)} %slice_add_fusion.col_ref), channel_id=1, source_target_pairs={{0,1},{1,2},{2,3},{3,0},{4,5},{5,6},{6,7},{7,4},{8,9},{9,10},{10,1... | collective-permute-start | bytes 49160 | tf_op jit(solution)/shard_map/ppermute | solution.py:432
  99.0 4.0 %collective-permute-start.23 = (f32[32,128]{1,0:T(8,128)S(1)}, f32[32,128]{1,0:T(8,128)S(1)}, u32[]{:S(2)}, u32[]{:S(2)}) collective-permute-start(f32[32,128]{1,0:T(8,128)S(1)} %slice_reduce_fusion.mine_ref), channel_id=1, source_target_pairs={{0,4},{4,0},{8,12},{12,8},{16,20},{20,16},{24,28},{28,24},{32,36},... | collective-permute-start | bytes 49160 | tf_op jit(solution)/shard_map/ppermute | solution.py:497
  (3 other events, 39.9 us)
